TPU v7x, 32 devices: a whole 2x2x4 slice. The times are simulated.
32 devices in a mesh: dp: 8 (over y, x, core), kv: 4 (over z).
Axes of the slice: x: 2, y: 2, z: 4, core: 2. Of those that a mesh axis runs over, the one named last changes fastest.
Arguments:
- tokens_in: bfloat16 [8192, 2048], P('dp'), may hold values from -6 to 6
- attn_gain: float32 [2048], replicated, may hold values from 0.5 to 1.5
- w_query: bfloat16 [2048, 2048], P(None, 'kv'), may hold values from -0.125 to 0.125
- w_key: bfloat16 [2048, 256], P(None, 'kv'), may hold values from -0.125 to 0.125
- w_value: bfloat16 [2048, 256], P(None, 'kv'), may hold values from -0.125 to 0.125
- w_output: bfloat16 [4, 512, 2048], P('kv'), may hold values from -0.5 to 0.5
- mlp_gain: float32 [2048], replicated, may hold values from 0.5 to 1.5
- w_gate: bfloat16 [2048, 5632], P(None, 'kv'), may hold values from -0.125 to 0.125
- w_up: bfloat16 [2048, 5632], P(None, 'kv'), may hold values from -0.125 to 0.125
- w_down: bfloat16 [4, 1408, 2048], P('kv'), may hold values from -0.078125 to 0.078125
- counts: int32 [8], P('dp'), may hold values from 768 to 1024, as said below
- segments: int32 [8192], P('dp'), may hold values from 0 to 8191, as said below
- cotangent: bfloat16 [8192, 2048], P('dp'), may hold values from -6 to 6
Outputs:
- layer_out: bfloat16 [8192, 2048], P(('dp', 'kv'))
- grad_tokens: float32 [8192, 2048], P(('dp', 'kv'))
- grad_attn_gain: float32 [2048], P('dp')
- grad_query_w: float32 [2048, 2048], P('dp', 'kv')
- grad_key_w: float32 [2048, 256], P('dp', 'kv')
- grad_value_w: float32 [2048, 256], P('dp', 'kv')
- grad_output_w: float32 [4, 512, 2048], P('kv', 'dp')
- grad_mlp_gain: float32 [2048], P('dp')
- grad_gate_w: float32 [2048, 5632], P('dp', 'kv')
- grad_up_w: float32 [2048, 5632], P('dp', 'kv')
- grad_down_w: float32 [4, 1408, 2048], P('kv', 'dp')
Inputs may be any that keep to these rules, and one draw needn't show every extreme that they name: `counts`: each pack's real tokens come first and its padding last; at most 256 padded tokens a pack; some packs have none. `segments`: ids never fall; every pack of 1024 rows begins a new segment at its first row, and no segment crosses packs; every padded token is a segment of its own, numbered by its index; a real segment is a chat fragment of at most 256 tokens or a whole pack.
All inputs are finite; a program needn't handle non-finite values.
Results may differ from a plain program's by a relative error of at most 0.024.
Values may be sent and summed in bfloat16 or wider, within the bound.
A program may use at most 256 MiB of HBM per device.

v0:
```python
import jax
import jax.numpy as jnp
from jax import lax
from jax.sharding import PartitionSpec as P

EPS = 1e-05


def norm_rows(values, norm_gain):
    inverse = lax.rsqrt(jnp.mean(values * values, axis=1, keepdims=True) + EPS)
    return values * inverse * norm_gain


def rope_tables(places, head_width):
    half_width = head_width // 2
    frequency = 10000.0 ** (-(jnp.arange(half_width, dtype=jnp.float32) * 2.0 / head_width))
    angles = places.astype(jnp.float32)[:, None] * frequency[None, :]
    cosine = jnp.concatenate([jnp.cos(angles), jnp.cos(angles)], axis=1)
    sinus = jnp.concatenate([jnp.sin(angles), jnp.sin(angles)], axis=1)
    return (cosine, sinus)


def rotate(vectors, cosine, sinus):
    half_width = vectors.shape[-1] // 2
    turned = jnp.concatenate([-vectors[..., half_width:], vectors[..., :half_width]], axis=-1)
    return vectors * cosine[:, None, :] + turned * sinus[:, None, :]


def seg_positions(segment_ids):
    places = jnp.arange(segment_ids.shape[0], dtype=jnp.int32)
    boundary = jnp.concatenate([jnp.ones((1,), jnp.bool_), segment_ids[1:] != segment_ids[:-1]])
    starts_at = lax.cummax(jnp.where(boundary, places, 0), axis=0)
    return places - starts_at


def product_left(first_mat, second_mat):
    return lax.dot_general(
        first_mat, second_mat, (((0,), (0,)), ((), ())), preferred_element_type=jnp.float32
    )


def product_right(first_mat, second_mat):
    return lax.dot_general(
        first_mat, second_mat, (((1,), (1,)), ((), ())), preferred_element_type=jnp.float32
    )


def block_scores(query_mat, key_mat, query_seg, key_seg, query_place, key_place, score_scale):
    raw_scores = (
        jnp.einsum("qhd,kd->hqk", query_mat, key_mat, preferred_element_type=jnp.float32)
        * score_scale
    )
    allowed = (key_place[None, :] <= query_place[:, None]) & (
        key_seg[None, :] == query_seg[:, None]
    )
    return jnp.where(allowed[None], raw_scores, -jnp.inf)


def swiglu(gate_act, up_act):
    return jax.nn.silu(gate_act) * up_act


def per_device(
    tokens_in,
    attn_gain,
    w_query,
    w_key,
    w_value,
    w_output,
    mlp_gain,
    w_gate,
    w_up,
    w_down,
    counts,
    segments,
    cotangent,
):
    row_count = tokens_in.shape[0]
    head_width = w_key.shape[1]
    head_count = w_query.shape[1] // head_width
    row_share = row_count // lax.axis_size("kv")
    own_start = lax.axis_index("kv") * row_share
    score_scale = head_width ** (-0.5)
    block_rows = min(512, row_count)
    places = jnp.arange(row_count, dtype=jnp.int32)
    tokens_f = tokens_in.astype(jnp.float32)
    cosine, sinus = rope_tables(seg_positions(segments), head_width)
    act_one = norm_rows(tokens_f, attn_gain).astype(jnp.bfloat16)
    query_raw = jnp.dot(act_one, w_query, preferred_element_type=jnp.float32).reshape(
        row_count, head_count, head_width
    )
    key_raw = jnp.dot(act_one, w_key, preferred_element_type=jnp.float32).reshape(
        row_count, 1, head_width
    )
    value_b = jnp.dot(act_one, w_value, preferred_element_type=jnp.float32).astype(jnp.bfloat16)
    query_b = rotate(query_raw, cosine, sinus).astype(jnp.bfloat16)
    key_b = rotate(key_raw, cosine, sinus)[:, 0, :].astype(jnp.bfloat16)
    outputs = []
    logsums = []
    for begin_row in range(0, row_count, block_rows):
        end_row = begin_row + block_rows
        scores = block_scores(
            query_b[begin_row:end_row],
            key_b[:end_row],
            segments[begin_row:end_row],
            segments[:end_row],
            places[begin_row:end_row],
            places[:end_row],
            score_scale,
        )
        highest = jnp.max(scores, axis=2, keepdims=True)
        logsum = highest + jnp.log(jnp.sum(jnp.exp(scores - highest), axis=2, keepdims=True))
        chance_b = jnp.exp(scores - logsum).astype(jnp.bfloat16)
        outputs.append(
            jnp.einsum(
                "hqk,kd->qhd", chance_b, value_b[:end_row], preferred_element_type=jnp.float32
            )
        )
        logsums.append(logsum)
    attn_out = (
        jnp.concatenate(outputs, axis=0)
        .reshape(row_count, head_count * head_width)
        .astype(jnp.bfloat16)
    )
    attn_part = jnp.dot(attn_out, w_output[0], preferred_element_type=jnp.float32)
    resid_full = tokens_f + lax.psum(attn_part.astype(jnp.bfloat16), "kv").astype(jnp.float32)
    resid_mine = lax.dynamic_slice_in_dim(resid_full, own_start, row_share, 0)
    act_two = norm_rows(resid_full, mlp_gain).astype(jnp.bfloat16)
    gate_act = jnp.dot(act_two, w_gate, preferred_element_type=jnp.float32)
    up_act = jnp.dot(act_two, w_up, preferred_element_type=jnp.float32)
    hidden = swiglu(gate_act, up_act).astype(jnp.bfloat16)
    feed_part = jnp.dot(hidden, w_down[0], preferred_element_type=jnp.float32)
    layer_out = (
        resid_mine
        + lax.psum_scatter(
            feed_part.astype(jnp.bfloat16), "kv", scatter_dimension=0, tiled=True
        ).astype(jnp.float32)
    ).astype(jnp.bfloat16)
    live_rows = (places < counts[0]).astype(jnp.float32)
    grad_out = cotangent.astype(jnp.float32) * live_rows[:, None]
    grad_out_b = grad_out.astype(jnp.bfloat16)
    grad_hidden = product_right(grad_out_b, w_down[0])
    grad_down = product_left(hidden, grad_out_b)
    swiglu_out, swiglu_back = jax.vjp(swiglu, gate_act, up_act)
    grad_gate, grad_up = swiglu_back(grad_hidden)
    grad_gate = grad_gate.astype(jnp.bfloat16)
    grad_up = grad_up.astype(jnp.bfloat16)
    grad_wgate = product_left(act_two, grad_gate)
    grad_wup = product_left(act_two, grad_up)
    grad_act_two = product_right(grad_gate, w_gate) + product_right(grad_up, w_up)
    grad_two_full = lax.psum(grad_act_two.astype(jnp.bfloat16), "kv").astype(jnp.float32)
    norm_out, second_back = jax.vjp(norm_rows, resid_full, mlp_gain)
    grad_resid, gain_two = second_back(grad_two_full)
    grad_resid_full = grad_out + grad_resid
    grad_resid_mine = lax.dynamic_slice_in_dim(grad_resid_full, own_start, row_share, 0)
    grad_branch = grad_resid_full.astype(jnp.bfloat16)
    grad_woutput = product_left(attn_out, grad_branch)
    grad_attn = (
        product_right(grad_branch, w_output[0])
        .astype(jnp.bfloat16)
        .reshape(row_count, head_count, head_width)
    )
    grad_query_parts = []
    grad_key_r = jnp.zeros((row_count, head_width), jnp.float32)
    grad_value_r = jnp.zeros((row_count, head_width), jnp.float32)
    for block_index, begin_row in enumerate(range(0, row_count, block_rows)):
        end_row = begin_row + block_rows
        remain = row_count - end_row
        scores = block_scores(
            query_b[begin_row:end_row],
            key_b[:end_row],
            segments[begin_row:end_row],
            segments[:end_row],
            places[begin_row:end_row],
            places[:end_row],
            score_scale,
        )
        chance = jnp.exp(scores - logsums[block_index])
        grad_probs = jnp.einsum(
            "qhd,kd->hqk",
            grad_attn[begin_row:end_row],
            value_b[:end_row],
            preferred_element_type=jnp.float32,
        )
        centre = jnp.sum(chance * grad_probs, axis=2, keepdims=True)
        grad_scores = (chance * (grad_probs - centre)).astype(jnp.bfloat16)
        grad_query_parts.append(
            jnp.einsum(
                "hqk,kd->qhd", grad_scores, key_b[:end_row], preferred_element_type=jnp.float32
            )
            * score_scale
        )
        key_term = (
            jnp.einsum(
                "hqk,qhd->kd",
                grad_scores,
                query_b[begin_row:end_row],
                preferred_element_type=jnp.float32,
            )
            * score_scale
        )
        grad_key_r = grad_key_r + jnp.pad(key_term, ((0, remain), (0, 0)))
        value_term = jnp.einsum(
            "hqk,qhd->kd",
            chance.astype(jnp.bfloat16),
            grad_attn[begin_row:end_row],
            preferred_element_type=jnp.float32,
        )
        grad_value_r = grad_value_r + jnp.pad(value_term, ((0, remain), (0, 0)))
    query_rot, query_back = jax.vjp(lambda vectors: rotate(vectors, cosine, sinus), query_raw)
    grad_query = (
        query_back(jnp.concatenate(grad_query_parts, axis=0))[0]
        .reshape(row_count, head_count * head_width)
        .astype(jnp.bfloat16)
    )
    key_rot, key_back = jax.vjp(lambda vectors: rotate(vectors, cosine, sinus), key_raw)
    grad_key = (
        key_back(grad_key_r[:, None, :])[0].reshape(row_count, head_width).astype(jnp.bfloat16)
    )
    grad_value = grad_value_r.astype(jnp.bfloat16)
    grad_wquery = product_left(act_one, grad_query)
    grad_wkey = product_left(act_one, grad_key)
    grad_wvalue = product_left(act_one, grad_value)
    grad_act_one = (
        product_right(grad_query, w_query)
        + product_right(grad_key, w_key)
        + product_right(grad_value, w_value)
    )
    grad_one_full = lax.psum(grad_act_one.astype(jnp.bfloat16), "kv").astype(jnp.float32)
    first_out, first_back = jax.vjp(norm_rows, tokens_f, attn_gain)
    grad_first, gain_one = first_back(grad_one_full)
    grad_tokens = grad_resid_mine + lax.dynamic_slice_in_dim(grad_first, own_start, row_share, 0)
    (
        sent_query,
        sent_key,
        sent_value,
        sent_output,
        sent_one,
        sent_gate,
        sent_up,
        sent_down,
        sent_two,
    ) = (
        lax.psum_scatter(
            grad_wquery.astype(jnp.bfloat16), "dp", scatter_dimension=0, tiled=True
        ).astype(jnp.float32),
        lax.psum_scatter(
            grad_wkey.astype(jnp.bfloat16), "dp", scatter_dimension=0, tiled=True
        ).astype(jnp.float32),
        lax.psum_scatter(
            grad_wvalue.astype(jnp.bfloat16), "dp", scatter_dimension=0, tiled=True
        ).astype(jnp.float32),
        lax.psum_scatter(
            grad_woutput[None].astype(jnp.bfloat16), "dp", scatter_dimension=1, tiled=True
        ).astype(jnp.float32),
        lax.psum_scatter(
            gain_one.astype(jnp.bfloat16), "dp", scatter_dimension=0, tiled=True
        ).astype(jnp.float32),
        lax.psum_scatter(
            grad_wgate.astype(jnp.bfloat16), "dp", scatter_dimension=0, tiled=True
        ).astype(jnp.float32),
        lax.psum_scatter(
            grad_wup.astype(jnp.bfloat16), "dp", scatter_dimension=0, tiled=True
        ).astype(jnp.float32),
        lax.psum_scatter(
            grad_down[None].astype(jnp.bfloat16), "dp", scatter_dimension=1, tiled=True
        ).astype(jnp.float32),
        lax.psum_scatter(
            gain_two.astype(jnp.bfloat16), "dp", scatter_dimension=0, tiled=True
        ).astype(jnp.float32),
    )
    return (
        layer_out,
        grad_tokens,
        sent_one,
        sent_query,
        sent_key,
        sent_value,
        sent_output,
        sent_two,
        sent_gate,
        sent_up,
        sent_down,
    )


def solution(mesh):
    return jax.shard_map(
        per_device,
        mesh=mesh,
        in_specs=(
            P("dp", None),
            P(),
            P(None, "kv"),
            P(None, "kv"),
            P(None, "kv"),
            P("kv", None, None),
            P(),
            P(None, "kv"),
            P(None, "kv"),
            P("kv", None, None),
            P("dp"),
            P("dp"),
            P("dp", None),
        ),
        out_specs=(
            P(("dp", "kv"), None),
            P(("dp", "kv"), None),
            P("dp"),
            P("dp", "kv"),
            P("dp", "kv"),
            P("dp", "kv"),
            P("kv", "dp", None),
            P("dp"),
            P("dp", "kv"),
            P("dp", "kv"),
            P("kv", "dp", None),
        ),
        check_vma=False,
    )
```

profile of v0, /device:TPU:8, one launch (start us, length us, event | category | flops | bytes accessed | tf_op | source)
XLA Modules:
  0.0 1078.8 jit_solution(14738162998375039660)
XLA Ops:
  27.6 7.5 fusion.98
  35.1 8.0 exponential_reduce_fusion
  43.2 5.5 convolution_convert_fusion.8
  48.7 8.4 fusion.52
  62.9 152.8 %all-reduce.13.cloned.1.call-done = bf16[1024,2048]{1,0:T(8,128)(2,1)} async-done(((bf16[1024,2048]{1,0:T(8,128)(2,1)}), bf16[1024,2048]{1,0:T(8,128)(2,1)}) %all-reduce.13.cloned.1.call-update) | async-done | bytes 4194320 | tf_op jit(solution)/shard_map/psum | solution.py:126
  224.8 11.9 %fusion.102 = f32[1024,1408]{1,0:T(8,128)} fusion(bf16[1024,2048]{1,0:T(8,128)(2,1)S(1)} %multiply_convert_fusion, bf16[2048,1408]{1,0:T(8,128)(2,1)} %param.21), kind=kOutput, calls=%fused_computation.165 | convolution fusion | flops 5905580032 | bytes 15728640 | tf_op jit(solution)/shard_map/dot_general | solution.py:130
  236.7 8.4 fusion.101
  245.2 15.4 %multiply_convert_fusion.2 = (bf16[1024,1408]{1,0:T(8,128)(2,1)}, bf16[1024,1408]{1,0:T(8,128)(2,1)}, bf16[1024,1408]{1,0:T(8,128)(2,1)}) fusion(f32[1024,1408]{1,0:T(8,128)} %fusion.101, f32[1024,1408]{1,0:T(8,128)} %fusion.102, bf16[1,1408,2048]{2,1,0:T(8,128)(2,1)} %param.22, bf16[1024,2048]{1,0:T(8,128)(2,1)S(1)} %copy-done.16, f32[1024]{0:T(1024)S(1)} %copy-done.48), kind=kOutput, calls=%fused_computation.52 | convolution fusion | flops 5934940160 | bytes 30150656 | tf_op jit(solution)/shard_map/dot_general | solution.py:43
  260.6 9.7 fusion.103
  270.3 11.2 %add_convert_fusion.1 = bf16[1024,2048]{1,0:T(8,128)(2,1)} fusion(f32[1024,2048]{1,0:T(8,128)S(1)} %fusion.103, bf16[1024,1408]{1,0:T(8,128)(2,1)S(1)} %copy-done.53, bf16[2048,1408]{1,0:T(8,128)(2,1)} %param.21), kind=kOutput, calls=%fused_computation.29 | convolution fusion | flops 5909774336 | bytes 21233664 | tf_op jit(solution)/shard_map/dot_general | solution.py:43
  282.7 153.0 %all-reduce.15.cloned.1.call-done = bf16[1024,2048]{1,0:T(8,128)(2,1)} async-done(((bf16[1024,2048]{1,0:T(8,128)(2,1)}), bf16[1024,2048]{1,0:T(8,128)(2,1)}) %all-reduce.15.cloned.1.call-update) | async-done | bytes 4194320 | tf_op jit(solution)/shard_map/psum | solution.py:151
  435.7 8.5 fusion.7
  444.2 10.3 fusion.9
  454.5 5.8 fusion.45
  462.7 7.9 fusion.10
  471.9 7.4 fusion
  484.0 7.1 fusion.12
  493.2 11.9 %fusion.2 = bf16[8,512,1024]{1,2,0:T(8,128)(2,1)S(1)} fusion(f32[1024,512,8]{1,0,2:T(8,128)} %get-tuple-element.45, f32[8,512,1024]{1,2,0:T(8,128)} %get-tuple-element.41, f32[8,512]{1,0:T(8,128)S(1)} %get-tuple-element.44, f32[8,512]{1,0:T(8,128)S(1)} %log_add_fusion), kind=kLoop, calls=%fused_computation.4 | loop fusion | flops 16777216 | bytes 41975808 | tf_op jit(solution)/shard_map/convert_element_type | solution.py:186
  512.1 7.1 fusion.28
  541.5 11.0 %fusion.25 = bf16[1024,2048]{1,0:T(8,128)(2,1)} fusion(bf16[1024,1408]{1,0:T(8,128)(2,1)} %get-tuple-element.19, bf16[1,1408,2048]{2,1,0:T(8,128)(2,1)} %param.22), kind=kOutput, calls=%fused_computation.57 | convolution fusion | flops 5907677184 | bytes 12845056 | tf_op jit(solution)/shard_map/dot_general | solution.py:132
  552.7 10.8 %fusion.14 = bf16[1,1408,2048]{2,1,0:T(8,128)(2,1)} fusion(bf16[1024,1408]{1,0:T(8,128)(2,1)} %get-tuple-element.19, bf16[1024,2048]{1,0:T(8,128)(2,1)} %param.25, f32[1024]{0:T(1024)S(1)} %copy-done.49), kind=kOutput, calls=%fused_computation.43 | convolution fusion | flops 5914755072 | bytes 12849152 | tf_op jit(solution)/shard_map/dot_general | solution.py:37
  563.5 11.1 %convolution_convert_fusion.1 = bf16[2048,1408]{1,0:T(8,128)(2,1)} fusion(bf16[1024,2048]{1,0:T(8,128)(2,1)} %copy-done.15, bf16[1024,1408]{1,0:T(8,128)(2,1)} %get-tuple-element.17), kind=kOutput, calls=%fused_computation.41 | convolution fusion | flops 5908463616 | bytes 12845056 | tf_op jit(solution)/shard_map/dot_general | solution.py:37
  575.0 11.0 %convolution_convert_fusion.2 = bf16[2048,1408]{1,0:T(8,128)(2,1)} fusion(bf16[1024,2048]{1,0:T(8,128)(2,1)} %copy-done.15, bf16[1024,1408]{1,0:T(8,128)(2,1)} %get-tuple-element.18), kind=kOutput, calls=%fused_computation.42 | convolution fusion | flops 5908463616 | bytes 12845056 | tf_op jit(solution)/shard_map/dot_general | solution.py:37
  586.0 6.6 convert_element_type.178
  602.4 43.5 %reduce-scatter.11.cloned.1.call-done = bf16[256,512]{1,0:T(8,128)(2,1)} async-done(((bf16[2048,512]{1,0:T(8,128)(2,1)}), bf16[256,512]{1,0:T(8,128)(2,1)}) %reduce-scatter.11.cloned.1.call-update) | async-done | bytes 262160 | tf_op jit(solution)/shard_map/reduce_scatter | solution.py:244
  647.7 153.4 %all-reduce.17.cloned.1.call-done = bf16[1024,2048]{1,0:T(8,128)(2,1)} async-done(((bf16[1024,2048]{1,0:T(8,128)(2,1)}), bf16[1024,2048]{1,0:T(8,128)(2,1)}) %all-reduce.17.cloned.1.call-update) | async-done | bytes 4194320 | tf_op jit(solution)/shard_map/psum | solution.py:229
  801.2 7.8 fusion.8
  809.1 14.3 %all-reduce.8 = (bf16[2048]{0:T(1024)(128)(2,1)S(1)}, bf16[2048]{0:T(1024)(128)(2,1)S(1)}) all-reduce(bf16[2048]{0:T(1024)(128)(2,1)S(1)} %get-tuple-element.13, bf16[2048]{0:T(1024)(128)(2,1)S(1)} %copy-done.47), channel_id=3, replica_groups=mesh['dp'=8,'kv'=4] {'dp'}, use_global_device_ids=true, to_apply=%region_17.18.clone | all-reduce | flops 4096 | bytes 16384
  824.0 57.5 %reduce-scatter.9.cloned.1.call-done = bf16[256,2048]{1,0:T(8,128)(2,1)} async-done(((bf16[1024,2048]{1,0:T(8,128)(2,1)}), bf16[256,2048]{1,0:T(8,128)(2,1)}) %reduce-scatter.9.cloned.1.call-update) | async-done | bytes 1048592 | tf_op jit(solution)/shard_map/reduce_scatter | solution.py:135
  889.4 55.1 %reduce-scatter.23.cloned.1.call-done = bf16[1,176,2048]{2,1,0:T(8,128)(2,1)} async-done(((bf16[1,1408,2048]{2,1,0:T(8,128)(2,1)}), bf16[1,176,2048]{2,1,0:T(8,128)(2,1)}) %reduce-scatter.23.cloned.1.call-update) | async-done | bytes 720912 | tf_op jit(solution)/shard_map/reduce_scatter | solution.py:265
  946.9 60.4 %reduce-scatter.21.cloned.1.call-done = bf16[256,1408]{1,0:T(8,128)(2,1)} async-done(((bf16[2048,1408]{1,0:T(8,128)(2,1)}), bf16[256,1408]{1,0:T(8,128)(2,1)}) %reduce-scatter.21.cloned.1.call-update) | async-done | bytes 720912 | tf_op jit(solution)/shard_map/reduce_scatter | solution.py:262
  1009.6 60.2 %reduce-scatter.19.cloned.1.call-done = bf16[256,1408]{1,0:T(8,128)(2,1)} async-done(((bf16[2048,1408]{1,0:T(8,128)(2,1)}), bf16[256,1408]{1,0:T(8,128)(2,1)}) %reduce-scatter.19.cloned.1.call-update) | async-done | bytes 720912 | tf_op jit(solution)/shard_map/reduce_scatter | solution.py:259
  (223 shorter events, 102.0 us)
Async XLA Ops:
  7.2 50.0 %copy-start = (bf16[1,512,2048]{2,1,0:T(8,128)(2,1)S(1)}, bf16[1,512,2048]{2,1,0:T(8,128)(2,1)}, u32[]{:S(2)}) copy-start(bf16[1,512,2048]{2,1,0:T(8,128)(2,1)} %param.18) | copy-start | bytes 6291460
  7.2 208.5 %all-reduce.13.cloned.1.call-start = ((), (), s32[]{:S(2)}) async-start(), calls=%async_computation.8 | async-start | bytes 8388608 | tf_op jit(solution)/shard_map/psum | solution.py:126
  25.3 9.8 copy-start.4
  27.1 16.1 %copy-start.32 = (f32[8,512]{1,0:T(8,128)}, f32[8,512]{1,0:T(8,128)S(1)}, u32[]{:S(2)}) copy-start(f32[8,512]{1,0:T(8,128)S(1)} %log_add_fusion.1) | copy-start | bytes 49156
  61.6 374.1 %all-reduce.15.cloned.1.call-start = ((), (), s32[]{:S(2)}) async-start(), calls=%async_computation.10 | async-start | bytes 8388608 | tf_op jit(solution)/shard_map/psum | solution.py:151
  221.6 15.1 %slice-start.7 = ((s8[5767168]{0:T(1024)(128)(4,1)}), s8[4194304]{0:T(1024)(128)(4,1)S(1)}, s32[]{:S(2)}) async-start(s8[5767168]{0:T(1024)(128)(4,1)} %bitcast.200), calls=%async_computation.26 | async-start | bytes 8388608
  224.7 12.0 %copy-start.15 = (bf16[1024,2048]{1,0:T(8,128)(2,1)}, bf16[1024,2048]{1,0:T(8,128)(2,1)S(1)}, u32[]{:S(2)}) copy-start(bf16[1024,2048]{1,0:T(8,128)(2,1)S(1)} %multiply_convert_fusion) | copy-start | bytes 12582916
  224.7 11.9 %slice-start.8 = ((s8[5767168]{0:T(1024)(128)(4,1)}), s8[1572864]{0:T(1024)(128)(4,1)S(1)}, s32[]{:S(2)}) async-start(s8[5767168]{0:T(1024)(128)(4,1)} %bitcast.200), calls=%async_computation.27 | async-start | bytes 3145728
  260.6 9.8 copy-start.53
  281.5 312.4 %reduce-scatter.15.cloned.1.call-start = ((), (), s32[]{:S(2)}) async-start(), calls=%async_computation.14 | async-start | bytes 294912 | tf_op jit(solution)/shard_map/reduce_scatter | solution.py:250
  282.7 161.5 %copy-start.44 = (f32[1024]{0:T(1024)S(1)}, f32[1024]{0:T(1024)}, u32[]{:S(2)}) copy-start(f32[1024]{0:T(1024)} %copy-done.43) | copy-start | bytes 12292
  282.7 161.5 %copy-start.35 = (f32[2048]{0:T(1024)S(1)}, f32[2048]{0:T(1024)}, u32[]{:S(2)}) copy-start(f32[2048]{0:T(1024)} %param.19) | copy-start | bytes 24580
  282.7 161.5 %copy-start.37 = (f32[1024]{0:T(1024)S(1)}, f32[1024]{0:T(1024)}, u32[]{:S(2)}) copy-start(f32[1024]{0:T(1024)} %copy-done.36) | copy-start | bytes 12292
  282.7 161.5 %copy-start.49 = (f32[1024]{0:T(1024)S(1)}, f32[1024]{0:T(1024)}, u32[]{:S(2)}) copy-start(f32[1024]{0:T(1024)} %fusion.88) | copy-start | bytes 12292
  435.7 8.5 copy-start.11
  435.7 24.7 %slice-start.4 = ((s8[8388608]{0:T(1024)(128)(4,1)}), s8[4194304]{0:T(1024)(128)(4,1)S(1)}, s32[]{:S(2)}) async-start(s8[8388608]{0:T(1024)(128)(4,1)} %bitcast.184), calls=%async_computation.23 | async-start | bytes 8388608
  444.2 16.2 %slice-start.5 = ((s8[8388608]{0:T(1024)(128)(4,1)}), s8[4194304]{0:T(1024)(128)(4,1)S(1)}, s32[]{:S(2)}) async-start(s8[8388608]{0:T(1024)(128)(4,1)} %bitcast.184), calls=%async_computation.24 | async-start | bytes 8388608
  460.4 10.2 slice-start
  460.4 10.2 slice-start.1
  462.7 9.1 slice-start.3
  484.0 111.4 %reduce-scatter.13.cloned.1.call-start = ((), (), s32[]{:S(2)}) async-start(), calls=%async_computation.13 | async-start | bytes 294912 | tf_op jit(solution)/shard_map/reduce_scatter | solution.py:247
  512.0 88.6 %reduce-scatter.17.cloned.1.call-start = ((), (), s32[]{:S(2)}) async-start(), calls=%async_computation.15 | async-start | bytes 2359296 | tf_op jit(solution)/shard_map/reduce_scatter | solution.py:253
  519.2 126.7 %reduce-scatter.11.cloned.1.call-start = ((), (), s32[]{:S(2)}) async-start(), calls=%async_computation.12 | async-start | bytes 2359296 | tf_op jit(solution)/shard_map/reduce_scatter | solution.py:244
  533.9 267.2 %all-reduce.17.cloned.1.call-start = ((), (), s32[]{:S(2)}) async-start(), calls=%async_computation.11 | async-start | bytes 8388608 | tf_op jit(solution)/shard_map/psum | solution.py:229
  541.4 340.1 %reduce-scatter.9.cloned.1.call-start = ((), (), s32[]{:S(2)}) async-start(), calls=%async_computation.9 | async-start | bytes 5242880 | tf_op jit(solution)/shard_map/reduce_scatter | solution.py:135
  552.5 392.1 %reduce-scatter.23.cloned.1.call-start = ((), (), s32[]{:S(2)}) async-start(), calls=%async_computation.18 | async-start | bytes 6488064 | tf_op jit(solution)/shard_map/reduce_scatter | solution.py:265
  563.5 443.8 %reduce-scatter.21.cloned.1.call-start = ((), (), s32[]{:S(2)}) async-start(), calls=%async_computation.17 | async-start | bytes 6488064 | tf_op jit(solution)/shard_map/reduce_scatter | solution.py:262
  574.7 495.1 %reduce-scatter.19.cloned.1.call-start = ((), (), s32[]{:S(2)}) async-start(), calls=%async_computation.16 | async-start | bytes 6488064 | tf_op jit(solution)/shard_map/reduce_scatter | solution.py:259
  586.0 215.2 %copy-start.45 = (f32[2048]{0:T(1024)S(1)}, f32[2048]{0:T(1024)}, u32[]{:S(2)}) copy-start(f32[2048]{0:T(1024)} %param.14) | copy-start | bytes 24580
  647.7 161.3 %copy-start.42 = (f32[1024]{0:T(1024)S(1)}, f32[1024]{0:T(1024)}, u32[]{:S(2)}) copy-start(f32[1024]{0:T(1024)} %copy-done.41) | copy-start | bytes 12292
  647.7 161.4 %copy-start.47 = (bf16[2048]{0:T(1024)(128)(2,1)S(1)}, bf16[2048]{0:T(1024)(128)(2,1)}, u32[]{:S(2)}) copy-start(bf16[2048]{0:T(1024)(128)(2,1)} %get-tuple-element.11) | copy-start | bytes 12292
  884.7 187.4 %copy-start.1 = (bf16[1,512,2048]{2,1,0:T(8,128)(2,1)S(1)}, bf16[1,512,2048]{2,1,0:T(8,128)(2,1)}, u32[]{:S(2)}) copy-start(bf16[1,512,2048]{2,1,0:T(8,128)(2,1)} %param.18) | copy-start | bytes 6291460
  (42 other events, 182.4 us)
Sparse Core Ops, SparseCore 0:
  61.7 153.9 all-reduce.12
  281.6 153.9 all-reduce.14
  484.1 34.7 reduce-scatter.14
  522.6 33.5 reduce-scatter.12
  559.4 41.1 reduce-scatter.16
  604.7 41.2 reduce-scatter.10
  648.3 152.8 all-reduce.16
  803.5 77.9 reduce-scatter.8
  885.0 59.5 reduce-scatter.22
  948.2 58.9 reduce-scatter.20
  1010.7 59.0 reduce-scatter.18
where the time goes:
time: 1090 us; the launch traced here: 1080 us
  waiting for transfers between devices  740 us (68%)
  matrix products  192 us (18%)
  other arithmetic  105 us (10%)
  between operations  16.3 us (1%)
  blocking collectives  14.3 us (1%)
    psum x1, waiting for transfers between devices, per_device(): lax.psum(grad_act_one.astype(jnp.bfloat16), 'kv').astype(jnp.float32)  153 us
    psum x1, waiting for transfers between devices, per_device(): lax.psum(grad_act_two.astype(jnp.bfloat16), 'kv').astype(jnp.float32)  153 us
    psum x1, waiting for transfers between devices, per_device(): lax.psum(attn_part.astype(jnp.bfloat16), 'kv').astype(jnp.float32)  153 us
    reduce_scatter x1, waiting for transfers between devices, per_device(): lax.psum_scatter(grad_wup.astype(jnp.bfloat16), 'dp', scatter_dimension=0...  60.4 us
    reduce_scatter x1, waiting for transfers between devices, per_device(): lax.psum_scatter(grad_wgate.astype(jnp.bfloat16), 'dp', scatter_dimension...  60.2 us
    reduce_scatter x1, waiting for transfers between devices, per_device(): lax.psum_scatter(feed_part.astype(jnp.bfloat16), 'kv', scatter_dimension=...  57.5 us
    reduce_scatter x1, waiting for transfers between devices, per_device(): lax.psum_scatter(grad_down[None].astype(jnp.bfloat16), 'dp', scatter_dime...  55.1 us
    dot_general x7, matrix products, product_right(): lax.dot_general(first_mat, second_mat, (((1,), (1,)), ((), ())), preferre...  49.1 us
  transfers between devices with their start and end apart: 11, of which 9 were waited for; matrix products, arithmetic and copies ran while one was open for 12% of the time, Pallas kernels for 0%

commit v1 on v0

--- a/solution.py
+++ b/solution.py
@@ -58,6 +58,12 @@
 
 def swiglu(gate_act, up_act):
     return jax.nn.silu(gate_act) * up_act
+
+
+def gather_weight(shard):
+    share = shard.shape[0] // lax.axis_size("dp")
+    mine = lax.dynamic_slice_in_dim(shard, lax.axis_index("dp") * share, share, 0)
+    return lax.all_gather(lax.all_gather(mine, "kv"), "dp", axis=1, tiled=True)
 
 
 def per_device(
@@ -83,6 +89,12 @@
     score_scale = head_width ** (-0.5)
     block_rows = min(512, row_count)
     places = jnp.arange(row_count, dtype=jnp.int32)
+
+    def own_rows(array):
+        return lax.dynamic_slice_in_dim(array, own_start, row_share, 0)
+
+    w_out_full = gather_weight(w_output[0]).reshape(-1, w_output.shape[2])
+    w_qkv_full = gather_weight(jnp.concatenate([w_query, w_key, w_value], axis=1))
     tokens_f = tokens_in.astype(jnp.float32)
     cosine, sinus = rope_tables(seg_positions(segments), head_width)
     act_one = norm_rows(tokens_f, attn_gain).astype(jnp.bfloat16)
@@ -122,20 +134,14 @@
         .reshape(row_count, head_count * head_width)
         .astype(jnp.bfloat16)
     )
-    attn_part = jnp.dot(attn_out, w_output[0], preferred_element_type=jnp.float32)
-    resid_full = tokens_f + lax.psum(attn_part.astype(jnp.bfloat16), "kv").astype(jnp.float32)
-    resid_mine = lax.dynamic_slice_in_dim(resid_full, own_start, row_share, 0)
+    attn_full = lax.all_gather(attn_out, "kv", axis=1, tiled=True)
+    resid_full = tokens_f + jnp.dot(attn_full, w_out_full, preferred_element_type=jnp.float32)
+    resid_mine = own_rows(resid_full)
     act_two = norm_rows(resid_full, mlp_gain).astype(jnp.bfloat16)
     gate_act = jnp.dot(act_two, w_gate, preferred_element_type=jnp.float32)
     up_act = jnp.dot(act_two, w_up, preferred_element_type=jnp.float32)
     hidden = swiglu(gate_act, up_act).astype(jnp.bfloat16)
     feed_part = jnp.dot(hidden, w_down[0], preferred_element_type=jnp.float32)
-    layer_out = (
-        resid_mine
-        + lax.psum_scatter(
-            feed_part.astype(jnp.bfloat16), "kv", scatter_dimension=0, tiled=True
-        ).astype(jnp.float32)
-    ).astype(jnp.bfloat16)
     live_rows = (places < counts[0]).astype(jnp.float32)
     grad_out = cotangent.astype(jnp.float32) * live_rows[:, None]
     grad_out_b = grad_out.astype(jnp.bfloat16)
@@ -148,18 +154,24 @@
     grad_wgate = product_left(act_two, grad_gate)
     grad_wup = product_left(act_two, grad_up)
     grad_act_two = product_right(grad_gate, w_gate) + product_right(grad_up, w_up)
-    grad_two_full = lax.psum(grad_act_two.astype(jnp.bfloat16), "kv").astype(jnp.float32)
-    norm_out, second_back = jax.vjp(norm_rows, resid_full, mlp_gain)
-    grad_resid, gain_two = second_back(grad_two_full)
-    grad_resid_full = grad_out + grad_resid
-    grad_resid_mine = lax.dynamic_slice_in_dim(grad_resid_full, own_start, row_share, 0)
-    grad_branch = grad_resid_full.astype(jnp.bfloat16)
-    grad_woutput = product_left(attn_out, grad_branch)
-    grad_attn = (
-        product_right(grad_branch, w_output[0])
-        .astype(jnp.bfloat16)
-        .reshape(row_count, head_count, head_width)
-    )
+    grad_two_mine = lax.psum_scatter(
+        grad_act_two.astype(jnp.bfloat16), "kv", scatter_dimension=0, tiled=True
+    ).astype(jnp.float32)
+    norm_out, second_back = jax.vjp(norm_rows, resid_mine, mlp_gain)
+    grad_resid, gain_two = second_back(grad_two_mine)
+    grad_resid_mine = own_rows(grad_out) + grad_resid
+    grad_branch = grad_resid_mine.astype(jnp.bfloat16)
+    grad_attn_rows = product_right(grad_branch, w_out_full).astype(jnp.bfloat16)
+    grad_attn = lax.all_to_all(grad_attn_rows, "kv", 1, 0, tiled=True).reshape(
+        row_count, head_count, head_width
+    )
+    grad_woutput = product_left(own_rows(attn_full), grad_branch)
+    layer_out = (
+        resid_mine
+        + lax.psum_scatter(
+            feed_part.astype(jnp.bfloat16), "kv", scatter_dimension=0, tiled=True
+        ).astype(jnp.float32)
+    ).astype(jnp.bfloat16)
     grad_query_parts = []
     grad_key_r = jnp.zeros((row_count, head_width), jnp.float32)
     grad_value_r = jnp.zeros((row_count, head_width), jnp.float32)
@@ -221,15 +233,17 @@
     grad_wquery = product_left(act_one, grad_query)
     grad_wkey = product_left(act_one, grad_key)
     grad_wvalue = product_left(act_one, grad_value)
-    grad_act_one = (
-        product_right(grad_query, w_query)
-        + product_right(grad_key, w_key)
-        + product_right(grad_value, w_value)
-    )
-    grad_one_full = lax.psum(grad_act_one.astype(jnp.bfloat16), "kv").astype(jnp.float32)
-    first_out, first_back = jax.vjp(norm_rows, tokens_f, attn_gain)
-    grad_first, gain_one = first_back(grad_one_full)
-    grad_tokens = grad_resid_mine + lax.dynamic_slice_in_dim(grad_first, own_start, row_share, 0)
+    grad_qkv = jnp.concatenate([grad_query, grad_key, grad_value], axis=1)
+    group_count = lax.axis_size("kv")
+    grad_qkv_rows = lax.all_to_all(
+        grad_qkv.reshape(group_count, row_share, -1), "kv", 0, 0, tiled=True
+    )
+    grad_one_mine = jnp.einsum(
+        "grc,gdc->rd", grad_qkv_rows, w_qkv_full, preferred_element_type=jnp.float32
+    )
+    first_out, first_back = jax.vjp(norm_rows, own_rows(tokens_f), attn_gain)
+    grad_first, gain_one = first_back(grad_one_mine)
+    grad_tokens = grad_resid_mine + grad_first
     (
         sent_query,
         sent_key,
@@ -251,11 +265,17 @@
             grad_wvalue.astype(jnp.bfloat16), "dp", scatter_dimension=0, tiled=True
         ).astype(jnp.float32),
         lax.psum_scatter(
-            grad_woutput[None].astype(jnp.bfloat16), "dp", scatter_dimension=1, tiled=True
-        ).astype(jnp.float32),
-        lax.psum_scatter(
-            gain_one.astype(jnp.bfloat16), "dp", scatter_dimension=0, tiled=True
-        ).astype(jnp.float32),
+            lax.psum_scatter(
+                grad_woutput.reshape(group_count, -1, w_output.shape[2]).astype(jnp.bfloat16),
+                "dp",
+                scatter_dimension=1,
+                tiled=True,
+            ),
+            "kv",
+            scatter_dimension=0,
+            tiled=True,
+        ).astype(jnp.float32),
+        lax.psum_scatter(lax.psum(gain_one, "kv"), "dp", scatter_dimension=0, tiled=True),
         lax.psum_scatter(
             grad_wgate.astype(jnp.bfloat16), "dp", scatter_dimension=0, tiled=True
         ).astype(jnp.float32),
@@ -265,9 +285,7 @@
         lax.psum_scatter(
             grad_down[None].astype(jnp.bfloat16), "dp", scatter_dimension=1, tiled=True
         ).astype(jnp.float32),
-        lax.psum_scatter(
-            gain_two.astype(jnp.bfloat16), "dp", scatter_dimension=0, tiled=True
-        ).astype(jnp.float32),
+        lax.psum_scatter(lax.psum(gain_two, "kv"), "dp", scatter_dimension=0, tiled=True),
     )
     return (
         layer_out,

time: 1090 us -> 967 us (0.89)
  waiting for transfers between devices: 740 us -> 563 us
  matrix products: 192 us -> 226 us
  other arithmetic: 105 us -> 78.2 us
  blocking collectives: 14.3 us -> 33.1 us
  local copies, waits for them, and re-layouts: 10.1 us -> 24.2 us
  starting transfers between devices: 1.25 us -> 13.2 us
    psum x3 -> x0, waiting for transfers between devices: 459 us -> none  [the longest x1 153 us: per_device(): lax.psum(grad_act_one.astype(jnp.bfloat16), 'kv').astype(jnp.float32)]
    all_gather x0 -> x5, waiting for transfers between devices: none -> 199 us  [the longest x4 121 us: gather_weight(): return lax.all_gather(lax.all_gather(mine, 'kv'), 'dp', axis=1, tiled=True)]
    reduce_scatter x1 -> x3, waiting for transfers between devices: 3.87 us -> 74.5 us  [the longest x1 54.9 us: per_device(): lax.psum_scatter(grad_act_two.astype(jnp.bfloat16), 'kv', scatter_dimensi...]
    reduce_scatter x1, waiting for transfers between devices: 60.2 us -> 8.16 us  [per_device(): lax.psum_scatter(grad_wgate.astype(jnp.bfloat16), 'dp', scatter_dimension...]
    reduce_scatter x1, waiting for transfers between devices: 43.5 us -> 0.01 us  [per_device(): lax.psum_scatter(grad_wquery.astype(jnp.bfloat16), 'dp', scatter_dimensio...]
    reduce_scatter x1, waiting for transfers between devices: 0.02 us -> 35.4 us  [per_device(): lax.psum_scatter(grad_wvalue.astype(jnp.bfloat16), 'dp', scatter_dimensio...]
    reduce_scatter x1, waiting for transfers between devices: 0.01 us -> 34.9 us  [per_device(): lax.psum_scatter(grad_wkey.astype(jnp.bfloat16), 'dp', scatter_dimension=...]
    dot_general x1 -> x2, matrix products: 4.38 us -> 26.9 us  [the longest x1 14.5 us: per_device(): jnp.dot(attn_full, w_out_full, preferred_element_type=jnp.float32)]
  transfers between devices with their start and end apart: 11 -> 17, of which waited for: 9 -> 12; matrix products, arithmetic and copies ran while one was open for 12% -> 25% of each run, Pallas kernels for 0% -> 0%
where the time goes in v1:
time: 967 us; the launch traced here: 953 us
  waiting for transfers between devices  563 us (58%)
  matrix products  226 us (23%)
  other arithmetic  78.2 us (8%)
  blocking collectives  33.1 us (3%)
  local copies, waits for them, and re-layouts  24.2 us (3%)
  between operations  16.6 us (2%)
  starting transfers between devices  13.2 us (1%)
    all_gather x4, waiting for transfers between devices, gather_weight(): return lax.all_gather(lax.all_gather(mine, 'kv'), 'dp', axis=1, tiled=True)  121 us
    all_gather x1, waiting for transfers between devices, per_device(): attn_full = lax.all_gather(attn_out, 'kv', axis=1, tiled=True)  78 us
    reduce_scatter x1, waiting for transfers between devices, per_device(): lax.psum_scatter(feed_part.astype(jnp.bfloat16), 'kv', scatter_dimension=...  77 us
    reduce_scatter x1, waiting for transfers between devices, per_device(): lax.psum_scatter(grad_down[None].astype(jnp.bfloat16), 'dp', scatter_dime...  60.4 us
    reduce_scatter x1, waiting for transfers between devices, per_device(): lax.psum_scatter(grad_wup.astype(jnp.bfloat16), 'dp', scatter_dimension=0...  60.3 us
    reduce_scatter x1, waiting for transfers between devices, per_device(): lax.psum_scatter(grad_act_two.astype(jnp.bfloat16), 'kv', scatter_dimensi...  54.9 us
    dot_general x7, matrix products, product_left(): lax.dot_general(first_mat, second_mat, (((0,), (0,)), ((), ())), preferre...  48.1 us
    dot_general x4, matrix products, product_right(): lax.dot_general(first_mat, second_mat, (((1,), (1,)), ((), ())), preferre...  42.1 us
  transfers between devices with their start and end apart: 17, of which 12 were waited for; matrix products, arithmetic and copies ran while one was open for 25% of the time, Pallas kernels for 0%

profile of v1, /device:TPU:8, one launch (start us, length us, event | category | flops | bytes accessed | tf_op | source)
XLA Modules:
  0.0 953.5 jit_solution(17060574637035184759)
XLA Ops:
  35.6 7.7 fusion.91
  43.3 8.0 exponential_reduce_fusion
  56.9 8.4 fusion.43
  67.9 78.0 %all-gather.7.cloned.1.call-done = bf16[1024,2048]{0,1:T(8,128)(2,1)} async-done(((bf16[1024,512]{0,1:T(8,128)(2,1)}), bf16[1024,2048]{0,1:T(8,128)(2,1)}) %all-gather.7.cloned.1.call-update) | async-done | bytes 4194320 | tf_op jit(solution)/shard_map/all_gather | solution.py:137
  145.9 57.5 %all-gather.11.cloned.1.call-done = bf16[4,512,2048]{2,1,0:T(8,128)(2,1)} async-done(((bf16[4,64,2048]{2,1,0:T(8,128)(2,1)}), bf16[4,512,2048]{2,1,0:T(8,128)(2,1)}) %all-gather.11.cloned.1.call-update) | async-done | bytes 8388624 | tf_op jit(solution)/shard_map/all_gather | solution.py:66
  203.5 14.5 %multiply_reduce_fusion = (f32[1024]{0:T(1024)S(1)}, f32[1024,2048]{1,0:T(8,128)S(1)}) fusion(bf16[1024,2048]{0,1:T(8,128)(2,1)} %all-gather.7.cloned.1.call-done, bf16[2048,2048]{1,0:T(8,128)(2,1)} %bitcast.194, bf16[1024,2048]{1,0:T(8,128)(2,1)} %param.13), kind=kOutput, calls=%fused_computation.19 | convolution fusion | flops 8598322176 | bytes 25169920 | tf_op jit(solution)/shard_map/dot_general | solution.py:138
  221.2 11.8 %fusion.94 = f32[1024,1408]{1,0:T(8,128)} fusion(bf16[1024,2048]{1,0:T(8,128)(2,1)S(1)} %multiply_convert_fusion, bf16[2048,1408]{1,0:T(8,128)(2,1)} %param.20), kind=kOutput, calls=%fused_computation.165 | convolution fusion | flops 5905580032 | bytes 15728640 | tf_op jit(solution)/shard_map/dot_general | solution.py:141
  233.0 10.5 %fusion.95 = f32[1024,1408]{1,0:T(8,128)} fusion(bf16[1024,2048]{1,0:T(8,128)(2,1)S(1)} %multiply_convert_fusion, bf16[2048,1408]{1,0:T(8,128)(2,1)} %param.21), kind=kOutput, calls=%fused_computation.166 | convolution fusion | flops 5905580032 | bytes 15728640 | tf_op jit(solution)/shard_map/dot_general | solution.py:142
  243.5 15.6 %multiply_convert_fusion.2 = (bf16[1024,1408]{1,0:T(8,128)(2,1)}, bf16[1024,1408]{1,0:T(8,128)(2,1)}, bf16[1024,1408]{1,0:T(8,128)(2,1)}) fusion(f32[1024,1408]{1,0:T(8,128)} %fusion.94, f32[1024,1408]{1,0:T(8,128)} %fusion.95, bf16[1,1408,2048]{2,1,0:T(8,128)(2,1)} %param.22, f32[1024]{0:T(1024)S(1)} %fusion.81, bf16[1024,2048]{1,0:T(8,128)(2,1)S(1)} %copy-done.18), kind=kOutput, calls=%fused_computation.38 | convolution fusion | flops 5934940160 | bytes 30150656 | tf_op jit(solution)/shard_map/dot_general | solution.py:43
  259.1 9.7 %fusion.96 = f32[1024,2048]{1,0:T(8,128)S(1)} fusion(bf16[1024,1408]{1,0:T(8,128)(2,1)} %get-tuple-element.20, bf16[2048,1408]{1,0:T(8,128)(2,1)} %param.20), kind=kOutput, calls=%fused_computation.167 | convolution fusion | flops 5905580032 | bytes 17039360 | tf_op jit(solution)/shard_map/dot_general | solution.py:43
  268.8 11.0 %add_convert_fusion = bf16[1024,2048]{1,0:T(8,128)(2,1)} fusion(f32[1024,2048]{1,0:T(8,128)S(1)} %fusion.96, bf16[1024,1408]{1,0:T(8,128)(2,1)S(1)} %copy-done.43, bf16[2048,1408]{1,0:T(8,128)(2,1)} %param.21), kind=kOutput, calls=%fused_computation.16 | convolution fusion | flops 5909774336 | bytes 21233664 | tf_op jit(solution)/shard_map/dot_general | solution.py:43
  279.9 10.9 %fusion.18 = bf16[1024,2048]{1,0:T(8,128)(2,1)} fusion(bf16[1024,1408]{1,0:T(8,128)(2,1)} %get-tuple-element.21, bf16[1,1408,2048]{2,1,0:T(8,128)(2,1)} %param.22), kind=kOutput, calls=%fused_computation.43 | convolution fusion | flops 5907677184 | bytes 12845056 | tf_op jit(solution)/shard_map/dot_general | solution.py:144
  301.9 54.9 %reduce-scatter.13.cloned.1.call-done = bf16[256,2048]{1,0:T(8,128)(2,1)} async-done(((bf16[1024,2048]{1,0:T(8,128)(2,1)}), bf16[256,2048]{1,0:T(8,128)(2,1)}) %reduce-scatter.13.cloned.1.call-update) | async-done | bytes 1048592 | tf_op jit(solution)/shard_map/reduce_scatter | solution.py:157
  359.4 77.0 %reduce-scatter.11.cloned.1.call-done = bf16[256,2048]{1,0:T(8,128)(2,1)} async-done(((bf16[1024,2048]{1,0:T(8,128)(2,1)}), bf16[256,2048]{1,0:T(8,128)(2,1)}) %reduce-scatter.11.cloned.1.call-update) | async-done | bytes 1048592 | tf_op jit(solution)/shard_map/reduce_scatter | solution.py:171
  448.4 11.1 %convolution_convert_fusion.2 = bf16[2048,1408]{1,0:T(8,128)(2,1)} fusion(bf16[1024,2048]{1,0:T(8,128)(2,1)} %copy-done.17, bf16[1024,1408]{1,0:T(8,128)(2,1)} %get-tuple-element.20), kind=kOutput, calls=%fused_computation.26 | convolution fusion | flops 5908463616 | bytes 12845056 | tf_op jit(solution)/shard_map/dot_general | solution.py:37
  459.7 11.0 %convolution_convert_fusion.1 = bf16[2048,1408]{1,0:T(8,128)(2,1)} fusion(bf16[1024,2048]{1,0:T(8,128)(2,1)} %copy-done.17, bf16[1024,1408]{1,0:T(8,128)(2,1)} %get-tuple-element.19), kind=kOutput, calls=%fused_computation.25 | convolution fusion | flops 5908463616 | bytes 12845056 | tf_op jit(solution)/shard_map/dot_general | solution.py:37
  482.3 11.7 %fusion.7 = bf16[1,1408,2048]{2,1,0:T(8,128)(2,1)} fusion(bf16[1024,1408]{1,0:T(8,128)(2,1)} %get-tuple-element.21, bf16[1024,2048]{1,0:T(8,128)(2,1)} %param.25, f32[1024]{0:T(1024)S(1)} %fusion.81), kind=kOutput, calls=%fused_computation.28 | convolution fusion | flops 5914755072 | bytes 12849152 | tf_op jit(solution)/shard_map/dot_general | solution.py:37
  494.3 10.5 %all-to-all-done = bf16[256,4,512]{2,0,1:T(8,128)(2,1)S(1)} async-done(((bf16[256,4,512]{2,0,1:T(8,128)(2,1)}), bf16[256,4,512]{2,0,1:T(8,128)(2,1)S(1)}, u32[]{:S(2)}, u32[]{:S(2)}) %all-to-all-start) | async-done | bytes 1048608 | tf_op jit(solution)/shard_map/all_to_all | solution.py:165
  506.5 8.0 fusion.4
  525.4 7.8 fusion
  533.2 7.8 fusion.2
  553.7 10.6 %fusion.54 = bf16[1024,64]{0,1:T(8,128)(2,1)S(1)} fusion(bf16[512,8,64]{0,2,1:T(8,128)(2,1)S(1)} %slice.97, f32[8,512,1024]{1,2,0:T(8,128)} %get-tuple-element.42, f32[8,512]{1,0:T(8,128)S(1)} %copy-done.35, f32[512,64]{0,1:T(8,128)S(1)} %convolution_bitcast_fusion.2), kind=kOutput, calls=%fused_computation.94 | convolution fusion | flops 545390592 | bytes 17580032 | tf_op jit(solution)/shard_map/hqk,qhd->kd/dot_general | solution.py:215
  600.1 8.2 reduce-scatter.25.cloned.1.call-done
  610.5 60.3 %reduce-scatter.27.cloned.1.call-done = bf16[256,1408]{1,0:T(8,128)(2,1)} async-done(((bf16[2048,1408]{1,0:T(8,128)(2,1)}), bf16[256,1408]{1,0:T(8,128)(2,1)}) %reduce-scatter.27.cloned.1.call-update) | async-done | bytes 720912 | tf_op jit(solution)/shard_map/reduce_scatter | solution.py:282
  673.1 60.4 %reduce-scatter.29.cloned.1.call-done = bf16[1,176,2048]{2,1,0:T(8,128)(2,1)} async-done(((bf16[1,1408,2048]{2,1,0:T(8,128)(2,1)}), bf16[1,176,2048]{2,1,0:T(8,128)(2,1)}) %reduce-scatter.29.cloned.1.call-update) | async-done | bytes 720912 | tf_op jit(solution)/shard_map/reduce_scatter | solution.py:285
  735.9 34.9 %reduce-scatter.17.cloned.1.call-done = bf16[256,64]{0,1:T(8,128)(2,1)} async-done(((bf16[2048,64]{0,1:T(8,128)(2,1)}), bf16[256,64]{0,1:T(8,128)(2,1)}) %reduce-scatter.17.cloned.1.call-update) | async-done | bytes 32784 | tf_op jit(solution)/shard_map/reduce_scatter | solution.py:261
  772.2 35.4 %reduce-scatter.19.cloned.1.call-done = bf16[256,64]{0,1:T(8,128)(2,1)} async-done(((bf16[2048,64]{0,1:T(8,128)(2,1)}), bf16[256,64]{0,1:T(8,128)(2,1)}) %reduce-scatter.19.cloned.1.call-update) | async-done | bytes 32784 | tf_op jit(solution)/shard_map/reduce_scatter | solution.py:264
  809.1 63.8 %all-gather.13.cloned.1.call-done = bf16[4,2048,640]{2,1,0:T(8,128)(2,1)} async-done(((bf16[4,256,640]{2,1,0:T(8,128)(2,1)}), bf16[4,2048,640]{2,1,0:T(8,128)(2,1)}) %all-gather.13.cloned.1.call-update) | async-done | bytes 10485776 | tf_op jit(solution)/shard_map/all_gather | solution.py:66
  872.9 12.4 %multiply_reduce_fusion.2 = (f32[2048]{0:T(1024)S(1)}, f32[256]{0:T(256)S(1)}, f32[256,2048]{1,0:T(8,128)}) fusion(f32[1024,2048]{1,0:T(8,128)} %convert_element_type.152, s32[]{:T(128)S(6)} %select_n.31, f32[256]{0:T(256)S(1)} %fusion.84, f32[2048]{0:T(1024)S(1)} %copy-done.41, bf16[4,256,640]{2,1,0:T(8,128)(2,1)S(1)} %all-to-all-done.1, ...), kind=kOutput, calls=%fused_computation.68 | convolution fusion | flops 2687497984 | bytes 16009220 | tf_op jit(solution)/shard_map/grc,gdc->rd/dot_general | solution.py:241
  885.3 23.7 %all-reduce.8 = (f32[2048]{0:T(1024)S(1)}, f32[2048]{0:T(1024)S(1)}) all-reduce(f32[2048]{0:T(1024)S(1)} %get-tuple-element.11, f32[2048]{0:T(1024)S(1)} %get-tuple-element.13), channel_id=5, replica_groups=mesh['dp'=8,'kv'=4] {'dp'}, use_global_device_ids=true, to_apply=%region_18.19.clone | all-reduce | flops 4096 | bytes 32768
  909.1 9.4 all-reduce.9
  925.2 19.5 %reduce-scatter.23.cloned.1.call-done = bf16[1,64,2048]{2,1,0:T(8,128)(2,1)} async-done(((bf16[4,64,2048]{2,1,0:T(8,128)(2,1)}), bf16[1,64,2048]{2,1,0:T(8,128)(2,1)}) %reduce-scatter.23.cloned.1.call-update) | async-done | bytes 262160 | tf_op jit(solution)/shard_map/reduce_scatter | solution.py:267
  (219 shorter events, 154.8 us)
Async XLA Ops:
  7.2 59.4 %all-gather.9.cloned.1.call-start = ((), (), s32[]{:S(2)}) async-start(), calls=%async_computation.13 | async-start | bytes 1310720 | tf_op jit(solution)/shard_map/all_gather | solution.py:66
  9.5 136.4 %all-gather.7.cloned.1.call-start = ((), (), s32[]{:S(2)}) async-start(), calls=%async_computation.12 | async-start | bytes 5242880 | tf_op jit(solution)/shard_map/all_gather | solution.py:137
  25.9 25.4 %copy-start.15 = (pred[512,512]{0,1:T(8,128)(4,1)}, pred[512,512]{0,1:T(8,128)(4,1)S(1)}, u32[]{:S(2)}) copy-start(pred[512,512]{0,1:T(8,128)(4,1)S(1)} %compare_and_fusion) | copy-start | bytes 786436
  33.6 17.7 %copy-start.36 = (f32[8,512]{1,0:T(8,128)}, f32[8,512]{1,0:T(8,128)S(1)}, u32[]{:S(2)}) copy-start(f32[8,512]{1,0:T(8,128)S(1)} %log_add_fusion.1) | copy-start | bytes 49156
  35.0 21.9 %copy-start.26 = (bf16[1024,64]{0,1:T(8,128)(2,1)}, bf16[1024,64]{0,1:T(8,128)(2,1)S(1)}, u32[]{:S(2)}) copy-start(bf16[1024,64]{0,1:T(8,128)(2,1)S(1)} %convolution_convert_fusion.9) | copy-start | bytes 393220
  66.5 137.0 %all-gather.11.cloned.1.call-start = ((), (), s32[]{:S(2)}) async-start(), calls=%async_computation.14 | async-start | bytes 9437184 | tf_op jit(solution)/shard_map/all_gather | solution.py:66
  67.2 289.6 %reduce-scatter.13.cloned.1.call-start = ((), (), s32[]{:S(2)}) async-start(), calls=%async_computation.16 | async-start | bytes 5242880 | tf_op jit(solution)/shard_map/reduce_scatter | solution.py:157
  203.5 14.5 %copy-start.38 = (f32[2048]{0:T(1024)S(1)}, f32[2048]{0:T(1024)}, u32[]{:S(2)}) copy-start(f32[2048]{0:T(1024)} %param.19) | copy-start | bytes 24580
  221.2 11.8 %copy-start.17 = (bf16[1024,2048]{1,0:T(8,128)(2,1)}, bf16[1024,2048]{1,0:T(8,128)(2,1)S(1)}, u32[]{:S(2)}) copy-start(bf16[1024,2048]{1,0:T(8,128)(2,1)S(1)} %multiply_convert_fusion) | copy-start | bytes 12582916
  279.9 156.5 %reduce-scatter.11.cloned.1.call-start = ((), (), s32[]{:S(2)}) async-start(), calls=%async_computation.15 | async-start | bytes 5242880 | tf_op jit(solution)/shard_map/reduce_scatter | solution.py:171
  290.8 275.2 %all-gather.15.cloned.1.call-start = ((), (), s32[]{:S(2)}) async-start(), calls=%async_computation.26 | async-start | bytes 1638400 | tf_op jit(solution)/shard_map/all_gather | solution.py:66
  293.2 296.5 %reduce-scatter.21.cloned.1.call-start = ((), (), s32[]{:S(2)}) async-start(), calls=%async_computation.21 | async-start | bytes 9437184 | tf_op jit(solution)/shard_map/reduce_scatter | solution.py:268
  440.8 29.9 %copy-start.12 = (f32[256,2048]{1,0:T(8,128)}, f32[256,2048]{1,0:T(8,128)S(1)}, u32[]{:S(2)}) copy-start(f32[256,2048]{1,0:T(8,128)S(1)} %get-tuple-element.22) | copy-start | bytes 6291460
  448.3 159.9 %reduce-scatter.25.cloned.1.call-start = ((), (), s32[]{:S(2)}) async-start(), calls=%async_computation.23 | async-start | bytes 6488064 | tf_op jit(solution)/shard_map/reduce_scatter | solution.py:279
  459.5 211.4 %reduce-scatter.27.cloned.1.call-start = ((), (), s32[]{:S(2)}) async-start(), calls=%async_computation.24 | async-start | bytes 6488064 | tf_op jit(solution)/shard_map/reduce_scatter | solution.py:282
  477.5 27.2 %all-to-all-start = ((bf16[256,4,512]{2,0,1:T(8,128)(2,1)}), bf16[256,4,512]{2,0,1:T(8,128)(2,1)S(1)}, u32[]{:S(2)}, u32[]{:S(2)}) async-start(bf16[256,4,512]{2,0,1:T(8,128)(2,1)} %bitcast.180), calls=%async_computation.2 | async-start | bytes 2097152 | tf_op jit(solution)/shard_map/all_to_all | solution.py:165
  482.3 251.3 %reduce-scatter.29.cloned.1.call-start = ((), (), s32[]{:S(2)}) async-start(), calls=%async_computation.25 | async-start | bytes 6488064 | tf_op jit(solution)/shard_map/reduce_scatter | solution.py:285
  494.0 12.5 %copy-start.16 = (pred[512,512]{0,1:T(8,128)(4,1)S(1)}, pred[512,512]{0,1:T(8,128)(4,1)}, u32[]{:S(2)}) copy-start(pred[512,512]{0,1:T(8,128)(4,1)} %copy-done.15) | copy-start | bytes 786436
  494.0 12.5 %copy-start.27 = (bf16[1024,64]{0,1:T(8,128)(2,1)S(1)}, bf16[1024,64]{0,1:T(8,128)(2,1)}, u32[]{:S(2)}) copy-start(bf16[1024,64]{0,1:T(8,128)(2,1)} %copy-done.26) | copy-start | bytes 393220
  494.0 12.5 %copy-start.37 = (f32[8,512]{1,0:T(8,128)S(1)}, f32[8,512]{1,0:T(8,128)}, u32[]{:S(2)}) copy-start(f32[8,512]{1,0:T(8,128)} %copy-done.36) | copy-start | bytes 49156
  494.0 276.8 %reduce-scatter.17.cloned.1.call-start = ((), (), s32[]{:S(2)}) async-start(), calls=%async_computation.19 | async-start | bytes 294912 | tf_op jit(solution)/shard_map/reduce_scatter | solution.py:261
  506.5 18.9 %slice-start = ((s8[16777216]{0:T(1024)(128)(4,1)}), s8[4194304]{0:T(1024)(128)(4,1)S(1)}, s32[]{:S(2)}) async-start(s8[16777216]{0:T(1024)(128)(4,1)} %bitcast.182), calls=%async_computation.27 | async-start | bytes 8388608
  506.5 18.9 %slice-start.1 = ((s8[16777216]{0:T(1024)(128)(4,1)}), s8[4194304]{0:T(1024)(128)(4,1)S(1)}, s32[]{:S(2)}) async-start(s8[16777216]{0:T(1024)(128)(4,1)} %bitcast.182), calls=%async_computation.28 | async-start | bytes 8388608
  514.5 10.9 %slice-start.2 = ((s8[16777216]{0:T(1024)(128)(4,1)}), s8[4194304]{0:T(1024)(128)(4,1)S(1)}, s32[]{:S(2)}) async-start(s8[16777216]{0:T(1024)(128)(4,1)} %bitcast.182), calls=%async_computation.29 | async-start | bytes 8388608
  514.5 10.9 %slice-start.3 = ((s8[16777216]{0:T(1024)(128)(4,1)}), s8[4194304]{0:T(1024)(128)(4,1)S(1)}, s32[]{:S(2)}) async-start(s8[16777216]{0:T(1024)(128)(4,1)} %bitcast.182), calls=%async_computation.30 | async-start | bytes 8388608
  553.4 254.2 %reduce-scatter.19.cloned.1.call-start = ((), (), s32[]{:S(2)}) async-start(), calls=%async_computation.20 | async-start | bytes 294912 | tf_op jit(solution)/shard_map/reduce_scatter | solution.py:264
  566.0 306.9 %all-gather.13.cloned.1.call-start = ((), (), s32[]{:S(2)}) async-start(), calls=%async_computation.17 | async-start | bytes 11796480 | tf_op jit(solution)/shard_map/all_gather | solution.py:66
  566.7 356.7 %reduce-scatter.15.cloned.1.call-start = ((), (), s32[]{:S(2)}) async-start(), calls=%async_computation.18 | async-start | bytes 2359296 | tf_op jit(solution)/shard_map/reduce_scatter | solution.py:258
  582.8 290.0 %all-to-all-start.1 = ((bf16[4,256,640]{2,1,0:T(8,128)(2,1)}), bf16[4,256,640]{2,1,0:T(8,128)(2,1)S(1)}, u32[]{:S(2)}, u32[]{:S(2)}) async-start(bf16[4,256,640]{2,1,0:T(8,128)(2,1)} %bitcast.31), calls=%async_computation.3 | async-start | bytes 2621440 | tf_op jit(solution)/shard_map/all_to_all | solution.py:238
  589.7 355.0 %reduce-scatter.23.cloned.1.call-start = ((), (), s32[]{:S(2)}) async-start(), calls=%async_computation.22 | async-start | bytes 1310720 | tf_op jit(solution)/shard_map/reduce_scatter | solution.py:267
  598.2 274.6 %copy-start.41 = (f32[2048]{0:T(1024)S(1)}, f32[2048]{0:T(1024)}, u32[]{:S(2)}) copy-start(f32[2048]{0:T(1024)} %param.14) | copy-start | bytes 24580
  918.6 27.9 %copy-start.1 = (bf16[1,512,2048]{2,1,0:T(8,128)(2,1)S(1)}, bf16[1,512,2048]{2,1,0:T(8,128)(2,1)}, u32[]{:S(2)}) copy-start(bf16[1,512,2048]{2,1,0:T(8,128)(2,1)} %param.18) | copy-start | bytes 6291460
  (33 other events, 150.2 us)
Sparse Core Ops, SparseCore 0:
  10.2 29.0 all-gather.8
  66.6 79.2 all-gather.6
  147.9 55.5 all-gather.10
  280.0 76.7 reduce-scatter.12
  359.0 77.2 reduce-scatter.10
  438.4 32.4 all-gather.14
  474.3 70.9 reduce-scatter.20
  549.2 59.0 reduce-scatter.24
  611.7 59.0 reduce-scatter.26
  674.5 59.0 reduce-scatter.28
  737.2 33.6 reduce-scatter.16
  774.0 33.6 reduce-scatter.18
  809.6 63.2 all-gather.12
  876.0 41.3 reduce-scatter.14
  919.6 25.0 reduce-scatter.22

commit v2 on v1

--- a/solution.py
+++ b/solution.py
@@ -1,9 +1,15 @@
+import functools
+
 import jax
 import jax.numpy as jnp
 from jax import lax
+from jax.experimental import pallas as pl
+from jax.experimental.pallas import tpu as pltpu
 from jax.sharding import PartitionSpec as P
 
 EPS = 1e-05
+MESH = pl.DeviceIdType.MESH
+VMEM_LIMIT = 60 * 1024 * 1024
 
 
 def norm_rows(values, norm_gain):
@@ -64,6 +70,175 @@
     share = shard.shape[0] // lax.axis_size("dp")
     mine = lax.dynamic_slice_in_dim(shard, lax.axis_index("dp") * share, share, 0)
     return lax.all_gather(lax.all_gather(mine, "kv"), "dp", axis=1, tiled=True)
+
+
+def row_halves(rows):
+    upper = -(-rows // 32) * 16
+    return ((0, upper), (upper, rows - upper))
+
+
+def product_scatter_kernel(count, dp, *refs):
+    lhs, rhs, outs = refs[:count], refs[count : 2 * count], refs[2 * count : 3 * count]
+    sent, held = refs[3 * count : 4 * count], refs[4 * count : 5 * count]
+    late = (refs[5 * count : 6 * count], refs[6 * count : 7 * count])
+    first_send, first_recv, late_send, late_recv = refs[7 * count :]
+    me = lax.axis_index("dp")
+    upper = me // 2
+    bits = dp.bit_length() - 1
+    slots = dp // 2
+
+    def bit(place):
+        return (me // 2**place) % 2
+
+    def partner(place):
+        return me + 2**place * (1 - 2 * bit(place))
+
+    def first_copy(a, t):
+        return pltpu.make_async_remote_copy(
+            src_ref=sent[a].at[t],
+            dst_ref=held[a].at[t],
+            send_sem=first_send.at[a, t],
+            recv_sem=first_recv.at[a, t],
+            device_id={"dp": partner(0)},
+            device_id_type=MESH,
+        )
+
+    def stage_bit(half, stage):
+        return stage - 1 if half == 0 else bits - 1 - stage
+
+    def slot_of(half, stage, index, value):
+        if half == 0:
+            return index * 2**stage + value * 2 ** (stage - 1) + upper % 2 ** (stage - 1)
+        top = 2 ** (bits - stage)
+        return index + value * (top // 2) + (upper // top) * top
+
+    def late_copy(a, half, stage, index, slot):
+        start, size = row_halves(lhs[a].shape[1])[half]
+        place = stage_bit(half, stage) + 1
+        buffer = slots - 2 ** (bits - stage) + index
+        return pltpu.make_async_remote_copy(
+            src_ref=held[a].at[slot, pl.ds(start, size)],
+            dst_ref=late[half][a].at[buffer],
+            send_sem=late_send.at[a, half, buffer],
+            recv_sem=late_recv.at[a, half, buffer],
+            device_id={"dp": partner(place)},
+            device_id_type=MESH,
+        )
+
+    def product(a, chunk):
+        return jnp.dot(lhs[a][chunk], rhs[a][...], preferred_element_type=jnp.float32)
+
+    def other_chunks(a):
+        def step(t, carry):
+            sent[a][t] = product(a, 2 * t + 1 - bit(0)).astype(jnp.bfloat16)
+            first_copy(a, t).start()
+            return carry
+
+        lax.fori_loop(0, slots, step, 0)
+
+    def own_chunks(a):
+        def step(e, carry):
+            t = 0
+            for place in range(bits - 1):
+                t = t + 2**place * ((e // 2**place + 1 + upper // 2**place) % 2)
+            own = product(a, 2 * t + bit(0))
+            first_copy(a, t).wait_recv()
+            held[a][t] = (held[a][t].astype(jnp.float32) + own).astype(jnp.bfloat16)
+
+            @pl.when(e % 2 == 0)
+            def _():
+                late_copy(a, 0, 1, t // 2, t).start()
+
+            @pl.when(e < slots // 2)
+            def _():
+                late_copy(a, 1, 1, t % (slots // 2), t).start()
+
+            return carry
+
+        lax.fori_loop(0, slots, step, 0)
+
+    def later(a, stage):
+        for half in range(2):
+            start, size = row_halves(lhs[a].shape[1])[half]
+            keep_bit = bit(stage_bit(half, stage) + 1)
+            if stage < bits - 1:
+                follow = stage_bit(half, stage + 1)
+            for index in range(2 ** (bits - 1 - stage)):
+                slot = slot_of(half, stage, index, keep_bit)
+                late_copy(a, half, stage, index, slot).wait_recv()
+                total = held[a][slot, pl.ds(start, size)].astype(jnp.float32) + late[half][a][
+                    slots - 2 ** (bits - stage) + index
+                ].astype(jnp.float32)
+                if stage == bits - 1:
+                    outs[a][pl.ds(start, size)] = total
+                else:
+                    held[a][slot, pl.ds(start, size)] = total.astype(jnp.bfloat16)
+            if stage < bits - 1:
+                for index in range(2 ** (bits - 2 - stage)):
+                    slot = slot_of(half, stage + 1, index, 1 - bit(follow + 1))
+                    late_copy(a, half, stage + 1, index, slot).start()
+
+    barrier = pltpu.get_barrier_semaphore()
+    for place in range(bits):
+        pl.semaphore_signal(
+            barrier, inc=1, device_id={"dp": partner(place)}, device_id_type=MESH
+        )
+    pl.semaphore_wait(barrier, bits)
+    pending = []
+    for a in range(count):
+        other_chunks(a)
+        own_chunks(a)
+        pending.append((a, 1))
+        if a > 0:
+            done, stage = pending.pop(0)
+            later(done, stage)
+            if stage < bits - 1:
+                pending.append((done, stage + 1))
+    while pending:
+        done, stage = pending.pop(0)
+        later(done, stage)
+        if stage < bits - 1:
+            pending.append((done, stage + 1))
+    for a in range(count):
+        for t in range(slots):
+            first_copy(a, t).wait_send()
+        for half in range(2):
+            for stage in range(1, bits):
+                for index in range(2 ** (bits - 1 - stage)):
+                    late_copy(a, half, stage, index, 0).wait_send()
+
+
+def product_scatter(pairs, collective_id):
+    count = len(pairs)
+    dp = pairs[0][0].shape[0]
+    slots = dp // 2
+    dims = [(lhs.shape[1], rhs.shape[1]) for lhs, rhs in pairs]
+    flops = sum(2 * lhs.size * rhs.shape[1] for lhs, rhs in pairs)
+    moved = sum(2 * (lhs.size + rhs.size) for lhs, rhs in pairs)
+    vmem = pl.BlockSpec(memory_space=pltpu.VMEM)
+    return pl.pallas_call(
+        functools.partial(product_scatter_kernel, count, dp),
+        out_shape=[jax.ShapeDtypeStruct(dim, jnp.float32) for dim in dims],
+        in_specs=[vmem] * (2 * count),
+        out_specs=[vmem] * count,
+        scratch_shapes=[pltpu.VMEM((slots,) + dim, jnp.bfloat16) for dim in dims] * 2
+        + [
+            pltpu.VMEM((slots - 1, row_halves(rows)[half][1], columns), jnp.bfloat16)
+            for half in range(2)
+            for rows, columns in dims
+        ]
+        + [pltpu.SemaphoreType.DMA((count, slots))] * 2
+        + [pltpu.SemaphoreType.DMA((count, 2, slots - 1))] * 2,
+        compiler_params=pltpu.CompilerParams(
+            collective_id=collective_id, has_side_effects=True, vmem_limit_bytes=VMEM_LIMIT
+        ),
+        cost_estimate=pl.CostEstimate(flops=flops * 3, bytes_accessed=moved, transcendentals=0),
+    )(*[lhs for lhs, _ in pairs], *[rhs for _, rhs in pairs])
+
+
+def row_chunks(matrix, count):
+    chunks = matrix.T.reshape(count, matrix.shape[1] // count, matrix.shape[0])
+    return jnp.pad(chunks, ((0, 0), (0, -chunks.shape[1] % 16), (0, 0)))
 
 
 def per_device(
@@ -146,13 +321,21 @@
     grad_out = cotangent.astype(jnp.float32) * live_rows[:, None]
     grad_out_b = grad_out.astype(jnp.bfloat16)
     grad_hidden = product_right(grad_out_b, w_down[0])
-    grad_down = product_left(hidden, grad_out_b)
     swiglu_out, swiglu_back = jax.vjp(swiglu, gate_act, up_act)
     grad_gate, grad_up = swiglu_back(grad_hidden)
     grad_gate = grad_gate.astype(jnp.bfloat16)
     grad_up = grad_up.astype(jnp.bfloat16)
-    grad_wgate = product_left(act_two, grad_gate)
-    grad_wup = product_left(act_two, grad_up)
+    pack_count = lax.axis_size("dp")
+    act_chunks = row_chunks(act_two, pack_count)
+    sent_gate, sent_up, sent_down = product_scatter(
+        [
+            (act_chunks, grad_gate),
+            (act_chunks, grad_up),
+            (row_chunks(hidden, pack_count), grad_out_b),
+        ],
+        1,
+    )
+    sent_down = sent_down[: hidden.shape[1] // pack_count][None]
     grad_act_two = product_right(grad_gate, w_gate) + product_right(grad_up, w_up)
     grad_two_mine = lax.psum_scatter(
         grad_act_two.astype(jnp.bfloat16), "kv", scatter_dimension=0, tiled=True
@@ -250,9 +433,6 @@
         sent_value,
         sent_output,
         sent_one,
-        sent_gate,
-        sent_up,
-        sent_down,
         sent_two,
     ) = (
         lax.psum_scatter(
@@ -276,15 +456,6 @@
             tiled=True,
         ).astype(jnp.float32),
         lax.psum_scatter(lax.psum(gain_one, "kv"), "dp", scatter_dimension=0, tiled=True),
-        lax.psum_scatter(
-            grad_wgate.astype(jnp.bfloat16), "dp", scatter_dimension=0, tiled=True
-        ).astype(jnp.float32),
-        lax.psum_scatter(
-            grad_wup.astype(jnp.bfloat16), "dp", scatter_dimension=0, tiled=True
-        ).astype(jnp.float32),
-        lax.psum_scatter(
-            grad_down[None].astype(jnp.bfloat16), "dp", scatter_dimension=1, tiled=True
-        ).astype(jnp.float32),
         lax.psum_scatter(lax.psum(gain_two, "kv"), "dp", scatter_dimension=0, tiled=True),
     )
     return (

time: 967 us -> 834 us (0.86)
  waiting for transfers between devices: 563 us -> 287 us
  Pallas kernels: 0 us -> 127 us
  blocking collectives: 33.1 us -> 70.2 us
  matrix products: 226 us -> 194 us
  local copies, waits for them, and re-layouts: 24.2 us -> 38.1 us
    reduce_scatter x3 -> x0, waiting for transfers between devices: 129 us -> none  [the longest x1 60.4 us: per_device(): lax.psum_scatter(grad_down[None].astype(jnp.bfloat16), 'dp', scatter_dime...]
    pallas_call x0 -> x1, Pallas kernels: none -> 127 us  [product_scatter(): pl.pallas_call(functools.partial(product_scatter_kernel, count, dp), out_...]
    all_gather x4, waiting for transfers between devices: 121 us -> 59 us  [gather_weight(): return lax.all_gather(lax.all_gather(mine, 'kv'), 'dp', axis=1, tiled=True)]
    all_to_all x0 -> x1, blocking collectives: none -> 38 us  [per_device(): lax.all_to_all(grad_attn_rows, 'kv', 1, 0, tiled=True)]
    reduce_scatter x1, waiting for transfers between devices: 35.4 us -> 0.01 us  [per_device(): lax.psum_scatter(grad_wvalue.astype(jnp.bfloat16), 'dp', scatter_dimensio...]
    reduce_scatter x1, waiting for transfers between devices: 34.9 us -> 0.02 us  [per_device(): lax.psum_scatter(grad_wkey.astype(jnp.bfloat16), 'dp', scatter_dimension=...]
    dot_general x7 -> x4, matrix products: 48.1 us -> 14.4 us  [product_left(): lax.dot_general(first_mat, second_mat, (((0,), (0,)), ((), ())), preferre...]
    all_to_all x1 -> x0, waiting for transfers between devices: 10.5 us -> none  [per_device(): lax.all_to_all(grad_attn_rows, 'kv', 1, 0, tiled=True)]
  transfers between devices with their start and end apart: 17 -> 13, of which waited for: 12 -> 6; matrix products, arithmetic and copies ran while one was open for 25% -> 26% of each run, Pallas kernels for 0% -> 16%
where the time goes in v2:
time: 834 us; the launch traced here: 821 us
  waiting for transfers between devices  287 us (34%)
  matrix products  194 us (23%)
  Pallas kernels  127 us (15%)
  other arithmetic  80.5 us (10%)
  blocking collectives  70.2 us (8%)
  local copies, waits for them, and re-layouts  38.1 us (5%)
  between operations  16.8 us (2%)
    pallas_call x1, Pallas kernels, product_scatter(): pl.pallas_call(functools.partial(product_scatter_kernel, count, dp), out_...  127 us
    reduce_scatter x1, waiting for transfers between devices, per_device(): lax.psum_scatter(feed_part.astype(jnp.bfloat16), 'kv', scatter_dimension=...  76.4 us
    all_gather x1, waiting for transfers between devices, per_device(): attn_full = lax.all_gather(attn_out, 'kv', axis=1, tiled=True)  70.2 us
    reduce_scatter x1, waiting for transfers between devices, per_device(): lax.psum_scatter(grad_act_two.astype(jnp.bfloat16), 'kv', scatter_dimensi...  59.5 us
    all_gather x4, waiting for transfers between devices, gather_weight(): return lax.all_gather(lax.all_gather(mine, 'kv'), 'dp', axis=1, tiled=True)  59 us
    dot_general x4, matrix products, product_right(): lax.dot_general(first_mat, second_mat, (((1,), (1,)), ((), ())), preferre...  40.2 us
    all_to_all x1, blocking collectives, per_device(): lax.all_to_all(grad_attn_rows, 'kv', 1, 0, tiled=True)  38 us
    unnamed x1, blocking collectives  22.8 us
  transfers between devices with their start and end apart: 13, of which 6 were waited for; matrix products, arithmetic and copies ran while one was open for 26% of the time, Pallas kernels for 16%

profile of v2, /device:TPU:8, one launch (start us, length us, event | category | flops | bytes accessed | tf_op | source)
XLA Modules:
  0.0 820.5 jit_solution(10058269700080300159)
XLA Ops:
  36.4 7.8 fusion.95
  44.1 8.0 exponential_reduce_fusion
  52.2 5.5 fusion.43
  57.8 8.4 %fusion.44 = bf16[512,8,64]{0,2,1:T(8,128)(2,1)S(1)} fusion(f32[8,512,1024]{1,2,0:T(8,128)} %get-tuple-element.49, f32[8,512]{1,0:T(8,128)S(1)} %log_add_fusion, bf16[1024,64]{0,1:T(8,128)(2,1)S(1)} %convolution_convert_fusion.6), kind=kOutput, calls=%fused_computation.88 | convolution fusion | flops 545521664 | bytes 17448960 | tf_op jit(solution)/shard_map/hqk,kd->qhd/dot_general | solution.py:302
  68.8 7.8 convert_multiply_fusion
  76.6 70.2 %all-gather.7.cloned.1.call-done = bf16[1024,2048]{0,1:T(8,128)(2,1)} async-done(((bf16[1024,512]{0,1:T(8,128)(2,1)}), bf16[1024,2048]{0,1:T(8,128)(2,1)}) %all-gather.7.cloned.1.call-update) | async-done | bytes 4194320 | tf_op jit(solution)/shard_map/all_gather | solution.py:312
  146.8 57.5 %all-gather.11.cloned.1.call-done = bf16[4,512,2048]{2,1,0:T(8,128)(2,1)} async-done(((bf16[4,64,2048]{2,1,0:T(8,128)(2,1)}), bf16[4,512,2048]{2,1,0:T(8,128)(2,1)}) %all-gather.11.cloned.1.call-update) | async-done | bytes 8388624 | tf_op jit(solution)/shard_map/all_gather | solution.py:72
  204.3 14.5 %multiply_reduce_fusion = (f32[1024]{0:T(1024)S(1)}, f32[1024,2048]{1,0:T(8,128)S(1)}) fusion(bf16[1024,2048]{0,1:T(8,128)(2,1)} %all-gather.7.cloned.1.call-done, bf16[2048,2048]{1,0:T(8,128)(2,1)} %bitcast.214, bf16[1024,2048]{1,0:T(8,128)(2,1)} %param.13), kind=kOutput, calls=%fused_computation.19 | convolution fusion | flops 8598322176 | bytes 25169920 | tf_op jit(solution)/shard_map/dot_general | solution.py:313
  218.8 12.9 %fusion.98 = f32[1024,1408]{1,0:T(8,128)} fusion(bf16[2048,1408]{1,0:T(8,128)(2,1)} %param.20, f32[1024,2048]{1,0:T(8,128)S(1)} %get-tuple-element.53, f32[2048]{0:T(1024)S(1)} %copy-done.32, f32[1024]{0:T(1024)S(1)} %add_rsqrt_fusion), kind=kOutput, calls=%fused_computation.168 | convolution fusion | flops 5911871488 | bytes 19935232 | tf_op jit(solution)/shard_map/dot_general | solution.py:316
  231.7 12.6 %fusion.11 = (bf16[1408,1024]{0,1:T(8,128)(2,1)}, f32[1024,1408]{1,0:T(8,128)}) fusion(f32[1024,1408]{1,0:T(8,128)} %fusion.98, bf16[2048,1408]{1,0:T(8,128)(2,1)} %param.21, f32[1024,2048]{1,0:T(8,128)S(1)} %get-tuple-element.53, f32[2048]{0:T(1024)S(1)} %copy-done.32, f32[1024]{0:T(1024)S(1)} %add_rsqrt_fusion), kind=kOutput, calls=%fused_computation.31 | convolution fusion | flops 5920522240 | bytes 28585984 | tf_op jit(solution)/shard_map/dot_general | solution.py:317
  244.4 14.8 %multiply_convert_fusion.2 = (bf16[1024,1408]{1,0:T(8,128)(2,1)}, bf16[1024,1408]{1,0:T(8,128)(2,1)}) fusion(f32[1024,1408]{1,0:T(8,128)} %fusion.98, f32[1024,1408]{1,0:T(8,128)} %get-tuple-element.60, bf16[1024,2048]{1,0:T(8,128)(2,1)S(1)} %copy-done.15, bf16[1,1408,2048]{2,1,0:T(8,128)(2,1)} %param.22), kind=kOutput, calls=%fused_computation.41 | convolution fusion | flops 5925765120 | bytes 27262976 | tf_op jit(solution)/shard_map/dot_general | solution.py:49
  259.2 8.6 %fusion.99 = f32[1024,2048]{1,0:T(8,128)S(1)} fusion(bf16[1024,1408]{1,0:T(8,128)(2,1)} %get-tuple-element.26.refs_3_, bf16[2048,1408]{1,0:T(8,128)(2,1)S(1)} %bitcast.217), kind=kOutput, calls=%fused_computation.169 | convolution fusion | flops 5905580032 | bytes 17039360 | tf_op jit(solution)/shard_map/dot_general | solution.py:49
  267.8 11.0 %add_convert_fusion = bf16[1024,2048]{1,0:T(8,128)(2,1)} fusion(f32[1024,2048]{1,0:T(8,128)S(1)} %fusion.99, bf16[1024,1408]{1,0:T(8,128)(2,1)S(1)} %copy-done.40, bf16[2048,1408]{1,0:T(8,128)(2,1)} %param.21), kind=kOutput, calls=%fused_computation.16 | convolution fusion | flops 5909774336 | bytes 21233664 | tf_op jit(solution)/shard_map/dot_general | solution.py:49
  278.9 12.6 %fusion.21 = bf16[1024,2048]{1,0:T(8,128)(2,1)} fusion(bf16[1,1408,2048]{2,1,0:T(8,128)(2,1)} %param.22, f32[1024,1408]{1,0:T(8,128)} %get-tuple-element.60, f32[1024,1408]{1,0:T(8,128)} %fusion.98), kind=kOutput, calls=%fused_computation.46 | convolution fusion | flops 5916327936 | bytes 21495808 | tf_op jit(solution)/shard_map/dot_general | solution.py:319
  296.2 59.5 %reduce-scatter.10.cloned.1.call-done = bf16[256,2048]{1,0:T(8,128)(2,1)} async-done(((bf16[1024,2048]{1,0:T(8,128)(2,1)}), bf16[256,2048]{1,0:T(8,128)(2,1)}) %reduce-scatter.10.cloned.1.call-update) | async-done | bytes 1048592 | tf_op jit(solution)/shard_map/reduce_scatter | solution.py:340
  358.9 76.4 %reduce-scatter.8.cloned.1.call-done = bf16[256,2048]{1,0:T(8,128)(2,1)} async-done(((bf16[1024,2048]{1,0:T(8,128)(2,1)}), bf16[256,2048]{1,0:T(8,128)(2,1)}) %reduce-scatter.8.cloned.1.call-update) | async-done | bytes 1048592 | tf_op jit(solution)/shard_map/reduce_scatter | solution.py:354
  439.7 7.6 convolution_convert_fusion
  447.4 5.8 convolution_convert_fusion.2
  453.2 38.0 %all_to_all.21 = bf16[256,4,512]{2,0,1:T(8,128)(2,1)S(1)} all-to-all(bf16[256,4,512]{2,0,1:T(8,128)(2,1)S(1)} %bitcast.206), channel_id=1, replica_groups=mesh['dp'=8,'kv'=4] {'kv'}, dimensions={1} | all-to-all | bytes 2097152 | tf_op jit(solution)/shard_map/all_to_all | solution.py:348
  493.0 9.2 %fusion.4 = (f32[8,512]{1,0:T(8,128)S(1)}, f32[512,512,8]{1,0,2:T(8,128)}) fusion(f32[512,512,8]{1,0,2:T(8,128)} %copy-done.2, f32[8,512]{1,0:T(8,128)} %copy-done.30, pred[512,512]{0,1:T(8,128)(4,1)S(1)} %compare_and_fusion, bf16[512,8,64]{0,2,1:T(8,128)(2,1)S(1)} %slice.95, bf16[1024,64]{0,1:T(8,128)(2,1)S(1)} %convolution_convert_fusion.6), kind=kOutput, calls=%fused_computation.12 | convolution fusion | flops 278917120 | bytes 17661952 | tf_op jit(solution)/shard_map/qhd,kd->hqk/dot_general | solution.py:374
  502.2 8.2 %fusion.6 = bf16[8,512,512]{1,2,0:T(8,128)(2,1)S(1)} fusion(f32[512,512,8]{1,0,2:T(8,128)} %get-tuple-element.57, f32[512,512,8]{1,0,2:T(8,128)} %copy-done.2, f32[8,512]{1,0:T(8,128)S(1)} %get-tuple-element.56, f32[8,512]{1,0:T(8,128)S(1)} %copy-done.31, pred[512,512]{0,1:T(8,128)(4,1)S(1)} %compare_and_fusion), kind=kLoop, calls=%fused_computation.14 | loop fusion | flops 12582912 | bytes 21266432 | tf_op jit(solution)/shard_map/convert_element_type | solution.py:381
  513.9 7.6 fusion
  521.6 8.2 fusion.2
  542.5 8.8 %fusion.55 = bf16[1024,64]{0,1:T(8,128)(2,1)S(1)} fusion(bf16[512,8,64]{0,2,1:T(8,128)(2,1)S(1)} %slice.97, f32[8,512,1024]{1,2,0:T(8,128)} %get-tuple-element.49, f32[8,512]{1,0:T(8,128)S(1)} %log_add_fusion, f32[512,64]{0,1:T(8,128)S(1)} %convolution_bitcast_fusion.2), kind=kOutput, calls=%fused_computation.95 | convolution fusion | flops 545390592 | bytes 17580032 | tf_op jit(solution)/shard_map/hqk,qhd->kd/dot_general | solution.py:398
  568.0 6.5 convert_element_type.134
  577.6 6.1 fusion.134
  583.7 6.4 copy.81
  601.8 127.3 %shard_map.212 = (f32[256,1408]{1,0:T(8,128)}, f32[256,1408]{1,0:T(8,128)}, f32[176,2048]{1,0:T(8,128)}) custom-call(bf16[8,256,1024]{2,1,0:T(8,128)(2,1)} %bitcast.202, bf16[8,256,1024]{2,1,0:T(8,128)(2,1)} %bitcast.203, bf16[8,176,1024]{2,1,0:T(8,128)(2,1)} %bitcast.209, bf16[1024,1408]{1,0:T(8,128)(2,1)} %get-tuple-element.26.refs_3_, ...), custom_call_target="tpu_custom_call" | custom-call | flops 53150220288 | bytes 21233664 | tf_op jit(solution)/shard_map/pallas_call | solution.py:219
  733.3 12.5 %multiply_reduce_fusion.2 = (f32[2048]{0:T(1024)S(1)}, f32[256]{0:T(256)S(1)}, f32[256,2048]{1,0:T(8,128)}) fusion(f32[1024,2048]{1,0:T(8,128)} %convert_element_type.134, s32[]{:T(128)S(6)} %select_n.31, f32[256]{0:T(256)S(1)} %fusion.86, f32[2048]{0:T(1024)S(1)} %copy-done.36, bf16[4,256,640]{2,1,0:T(8,128)(2,1)S(1)} %all-to-all-done.1, ...), kind=kOutput, calls=%fused_computation.71 | convolution fusion | flops 2687497984 | bytes 16009220 | tf_op jit(solution)/shard_map/grc,gdc->rd/dot_general | solution.py:424
  745.8 22.8 %all-reduce.8 = (f32[2048]{0:T(1024)S(1)}, f32[2048]{0:T(1024)S(1)}) all-reduce(f32[2048]{0:T(1024)S(1)} %get-tuple-element.17, f32[2048]{0:T(1024)S(1)} %copy-done.35), channel_id=5, replica_groups=mesh['dp'=8,'kv'=4] {'dp'}, use_global_device_ids=true, to_apply=%region_18.19.clone | all-reduce | flops 4096 | bytes 32768
  768.7 9.4 %all-reduce.9 = (f32[256]{0:T(256)}, f32[256]{0:T(256)}) all-reduce(f32[256]{0:T(256)S(1)} %dynamic-slice.2, f32[256]{0:T(256)S(1)} %dynamic-slice.4), channel_id=1, replica_groups=mesh['dp'=8,'kv'=4] {'kv'}, use_global_device_ids=true, to_apply=%region_17.18 | all-reduce | flops 512 | bytes 4096 | tf_op jit(solution)/shard_map/psum | solution.py:458
  784.9 20.3 %reduce-scatter.20.cloned.1.call-done = bf16[1,64,2048]{2,1,0:T(8,128)(2,1)} async-done(((bf16[4,64,2048]{2,1,0:T(8,128)(2,1)}), bf16[1,64,2048]{2,1,0:T(8,128)(2,1)}) %reduce-scatter.20.cloned.1.call-update) | async-done | bytes 262160 | tf_op jit(solution)/shard_map/reduce_scatter | solution.py:447
  (208 shorter events, 110.7 us)
Async XLA Ops:
  7.2 60.2 %all-gather.9.cloned.1.call-start = ((), (), s32[]{:S(2)}) async-start(), calls=%async_computation.10 | async-start | bytes 1310720 | tf_op jit(solution)/shard_map/all_gather | solution.py:72
  9.5 137.3 %all-gather.7.cloned.1.call-start = ((), (), s32[]{:S(2)}) async-start(), calls=%async_computation.9 | async-start | bytes 5242880 | tf_op jit(solution)/shard_map/all_gather | solution.py:312
  26.8 9.5 %copy-start.20 = (bf16[1024,64]{0,1:T(8,128)(2,1)}, bf16[1024,64]{0,1:T(8,128)(2,1)S(1)}, u32[]{:S(2)}) copy-start(bf16[1024,64]{0,1:T(8,128)(2,1)S(1)} %get-tuple-element.41) | copy-start | bytes 393220
  34.4 17.8 %copy-start.30 = (f32[8,512]{1,0:T(8,128)}, f32[8,512]{1,0:T(8,128)S(1)}, u32[]{:S(2)}) copy-start(f32[8,512]{1,0:T(8,128)S(1)} %log_add_fusion.1) | copy-start | bytes 49156
  67.3 137.0 %all-gather.11.cloned.1.call-start = ((), (), s32[]{:S(2)}) async-start(), calls=%async_computation.11 | async-start | bytes 9437184 | tf_op jit(solution)/shard_map/all_gather | solution.py:72
  68.1 287.7 %reduce-scatter.10.cloned.1.call-start = ((), (), s32[]{:S(2)}) async-start(), calls=%async_computation.13 | async-start | bytes 5242880 | tf_op jit(solution)/shard_map/reduce_scatter | solution.py:340
  204.3 14.5 %copy-start.32 = (f32[2048]{0:T(1024)S(1)}, f32[2048]{0:T(1024)}, u32[]{:S(2)}) copy-start(f32[2048]{0:T(1024)} %param.19) | copy-start | bytes 24580
  218.8 12.9 %copy-start.11 = (f32[1024,2048]{1,0:T(8,128)}, f32[1024,2048]{1,0:T(8,128)S(1)}, u32[]{:S(2)}) copy-start(f32[1024,2048]{1,0:T(8,128)S(1)} %get-tuple-element.53) | copy-start | bytes 25165828
  218.8 12.9 %copy-start.37 = (f32[1024]{0:T(1024)}, f32[1024]{0:T(1024)S(1)}, u32[]{:S(2)}) copy-start(f32[1024]{0:T(1024)S(1)} %add_rsqrt_fusion) | copy-start | bytes 12292
  231.7 12.6 %copy-start.15 = (bf16[1024,2048]{1,0:T(8,128)(2,1)S(1)}, bf16[1024,2048]{1,0:T(8,128)(2,1)}, u32[]{:S(2)}) copy-start(bf16[1024,2048]{1,0:T(8,128)(2,1)} %get-tuple-element.30.refs_5_) | copy-start | bytes 12582916
  231.7 27.4 %slice-start.4 = ((s8[5767168]{0:T(1024)(128)(4,1)}), s8[4194304]{0:T(1024)(128)(4,1)S(1)}, s32[]{:S(2)}) async-start(s8[5767168]{0:T(1024)(128)(4,1)} %bitcast.216), calls=%async_computation.25 | async-start | bytes 8388608
  244.4 14.8 %slice-start.5 = ((s8[5767168]{0:T(1024)(128)(4,1)}), s8[1572864]{0:T(1024)(128)(4,1)S(1)}, s32[]{:S(2)}) async-start(s8[5767168]{0:T(1024)(128)(4,1)} %bitcast.216), calls=%async_computation.26 | async-start | bytes 3145728
  278.8 156.5 %reduce-scatter.8.cloned.1.call-start = ((), (), s32[]{:S(2)}) async-start(), calls=%async_computation.12 | async-start | bytes 5242880 | tf_op jit(solution)/shard_map/reduce_scatter | solution.py:354
  291.5 261.5 %all-gather.15.cloned.1.call-start = ((), (), s32[]{:S(2)}) async-start(), calls=%async_computation.20 | async-start | bytes 1638400 | tf_op jit(solution)/shard_map/all_gather | solution.py:72
  294.4 307.1 %reduce-scatter.18.cloned.1.call-start = ((), (), s32[]{:S(2)}) async-start(), calls=%async_computation.18 | async-start | bytes 9437184 | tf_op jit(solution)/shard_map/reduce_scatter | solution.py:448
  447.3 281.8 %reduce-scatter.14.cloned.1.call-start = ((), (), s32[]{:S(2)}) async-start(), calls=%async_computation.16 | async-start | bytes 294912 | tf_op jit(solution)/shard_map/reduce_scatter | solution.py:441
  493.0 20.9 %slice-start = ((s8[16777216]{0:T(1024)(128)(4,1)}), s8[4194304]{0:T(1024)(128)(4,1)S(1)}, s32[]{:S(2)}) async-start(s8[16777216]{0:T(1024)(128)(4,1)} %bitcast.197), calls=%async_computation.21 | async-start | bytes 8388608
  493.0 20.9 %slice-start.1 = ((s8[16777216]{0:T(1024)(128)(4,1)}), s8[4194304]{0:T(1024)(128)(4,1)S(1)}, s32[]{:S(2)}) async-start(s8[16777216]{0:T(1024)(128)(4,1)} %bitcast.197), calls=%async_computation.22 | async-start | bytes 8388608
  502.2 10.3 %copy-start.14 = (bf16[1024,8,64]{0,2,1:T(8,128)(2,1)S(1)}, bf16[1024,8,64]{0,2,1:T(8,128)(2,1)}, u32[]{:S(2)}) copy-start(bf16[1024,8,64]{0,2,1:T(8,128)(2,1)} %copy-done.13) | copy-start | bytes 3145732
  502.2 11.7 %slice-start.2 = ((s8[16777216]{0:T(1024)(128)(4,1)}), s8[4194304]{0:T(1024)(128)(4,1)S(1)}, s32[]{:S(2)}) async-start(s8[16777216]{0:T(1024)(128)(4,1)} %bitcast.197), calls=%async_computation.23 | async-start | bytes 8388608
  502.2 11.7 %slice-start.3 = ((s8[16777216]{0:T(1024)(128)(4,1)}), s8[4194304]{0:T(1024)(128)(4,1)S(1)}, s32[]{:S(2)}) async-start(s8[16777216]{0:T(1024)(128)(4,1)} %bitcast.197), calls=%async_computation.24 | async-start | bytes 8388608
  542.2 188.3 %reduce-scatter.16.cloned.1.call-start = ((), (), s32[]{:S(2)}) async-start(), calls=%async_computation.17 | async-start | bytes 294912 | tf_op jit(solution)/shard_map/reduce_scatter | solution.py:444
  552.9 180.4 %all-gather.13.cloned.1.call-start = ((), (), s32[]{:S(2)}) async-start(), calls=%async_computation.14 | async-start | bytes 11796480 | tf_op jit(solution)/shard_map/all_gather | solution.py:72
  553.5 229.5 %reduce-scatter.12.cloned.1.call-start = ((), (), s32[]{:S(2)}) async-start(), calls=%async_computation.15 | async-start | bytes 2359296 | tf_op jit(solution)/shard_map/reduce_scatter | solution.py:438
  567.9 9.6 %copy-start.33 = (f32[2048]{0:T(1024)S(1)}, f32[2048]{0:T(1024)}, u32[]{:S(2)}) copy-start(f32[2048]{0:T(1024)} %param.19) | copy-start | bytes 24580
  568.0 9.6 %copy-start.38 = (f32[1024]{0:T(1024)S(1)}, f32[1024]{0:T(1024)}, u32[]{:S(2)}) copy-start(f32[1024]{0:T(1024)} %copy-done.37) | copy-start | bytes 12292
  596.3 137.0 %all-to-all-start.1 = ((bf16[4,256,640]{2,1,0:T(8,128)(2,1)}), bf16[4,256,640]{2,1,0:T(8,128)(2,1)S(1)}, u32[]{:S(2)}, u32[]{:S(2)}) async-start(bf16[4,256,640]{2,1,0:T(8,128)(2,1)} %bitcast.31), calls=%async_computation.3 | async-start | bytes 2621440 | tf_op jit(solution)/shard_map/all_to_all | solution.py:421
  601.2 204.0 %reduce-scatter.20.cloned.1.call-start = ((), (), s32[]{:S(2)}) async-start(), calls=%async_computation.19 | async-start | bytes 1310720 | tf_op jit(solution)/shard_map/reduce_scatter | solution.py:447
  601.8 131.5 %copy-start.36 = (f32[2048]{0:T(1024)S(1)}, f32[2048]{0:T(1024)}, u32[]{:S(2)}) copy-start(f32[2048]{0:T(1024)} %param.14) | copy-start | bytes 24580
  731.9 13.9 %copy-start.35 = (f32[2048]{0:T(1024)S(1)}, f32[2048]{0:T(1024)}, u32[]{:S(2)}) copy-start(f32[2048]{0:T(1024)} %get-tuple-element.19) | copy-start | bytes 24580
  778.2 35.1 %copy-start.1 = (bf16[1,512,2048]{2,1,0:T(8,128)(2,1)S(1)}, bf16[1,512,2048]{2,1,0:T(8,128)(2,1)}, u32[]{:S(2)}) copy-start(bf16[1,512,2048]{2,1,0:T(8,128)(2,1)} %param.18) | copy-start | bytes 6291460
  783.0 29.1 %copy-start.23 = (f32[176,2048]{1,0:T(8,128)S(1)}, f32[176,2048]{1,0:T(8,128)}, u32[]{:S(2)}) copy-start(f32[176,2048]{1,0:T(8,128)} %get-tuple-element.16) | copy-start | bytes 4325380
  (28 other events, 126.0 us)
Sparse Core Ops, SparseCore 0:
  10.2 29.0 all-gather.8
  67.5 79.2 all-gather.6
  148.7 55.5 all-gather.10
  279.0 76.7 reduce-scatter.9
  358.0 77.2 reduce-scatter.7
  437.3 42.5 all-gather.14
  483.4 73.8 reduce-scatter.17
  561.2 33.5 reduce-scatter.13
  597.8 33.8 reduce-scatter.15
  633.6 99.6 all-gather.12
  736.9 40.9 reduce-scatter.11
  780.1 25.0 reduce-scatter.19

commit v3 on v2

--- a/solution.py
+++ b/solution.py
@@ -66,10 +66,16 @@
     return jax.nn.silu(gate_act) * up_act
 
 
-def gather_weight(shard):
+def gather_share(shard):
     share = shard.shape[0] // lax.axis_size("dp")
     mine = lax.dynamic_slice_in_dim(shard, lax.axis_index("dp") * share, share, 0)
-    return lax.all_gather(lax.all_gather(mine, "kv"), "dp", axis=1, tiled=True)
+    return lax.all_gather(mine, "kv")
+
+
+def other_groups(array):
+    count = lax.axis_size("kv")
+    doubled = jnp.concatenate([array, array], axis=0)
+    return lax.dynamic_slice_in_dim(doubled, lax.axis_index("kv") + 1, count - 1, 0)
 
 
 def row_halves(rows):
@@ -236,8 +242,270 @@
     )(*[lhs for lhs, _ in pairs], *[rhs for _, rhs in pairs])
 
 
+def times(first, second):
+    return jnp.dot(first, second, preferred_element_type=jnp.float32)
+
+
+def times_t(first, second):
+    return lax.dot_general(
+        first, second, (((1,), (1,)), ((), ())), preferred_element_type=jnp.float32
+    )
+
+
+class Spread:
+    def __init__(self, buffer, send_sem, recv_sem, dp, split):
+        self.buffer, self.send_sem, self.recv_sem = buffer, send_sem, recv_sem
+        self.me = lax.axis_index("dp")
+        self.bits = dp.bit_length() - 1
+        columns = buffer.shape[3]
+        self.columns = ((0, split), (split, columns - split))
+
+    def flipped(self, places):
+        device = self.me
+        for place in places:
+            device = device + 2**place * (1 - 2 * ((self.me // 2**place) % 2))
+        return device
+
+    def copies(self, stage, arriving):
+        result = []
+        for half in range(2):
+            order = list(range(1, self.bits))
+            order = (order if half == 0 else order[::-1]) + [0]
+            for subset in range(2**stage):
+                places = [order[b] for b in range(stage) if subset >> b & 1]
+                if arriving:
+                    places = places + [order[stage]]
+                part = self.buffer.at[:, self.flipped(places), :, pl.ds(*self.columns[half])]
+                number = 2**stage - 1 + subset
+                result.append(
+                    pltpu.make_async_remote_copy(
+                        src_ref=part,
+                        dst_ref=part,
+                        send_sem=self.send_sem.at[half, number],
+                        recv_sem=self.recv_sem.at[half, number],
+                        device_id={"dp": self.flipped([order[stage]])},
+                        device_id_type=MESH,
+                    )
+                )
+        return result
+
+    def start(self, stage):
+        for copy in self.copies(stage, False):
+            copy.start()
+
+    def wait_recv(self, stage):
+        for copy in self.copies(stage, True):
+            copy.wait_recv()
+
+    def wait_send(self):
+        for stage in range(self.bits):
+            for copy in self.copies(stage, False):
+                copy.wait_send()
+
+
+def greet(dp, groups):
+    pack, group = lax.axis_index("dp"), lax.axis_index("kv")
+    bits = dp.bit_length() - 1
+    barrier = pltpu.get_barrier_semaphore()
+    for place in range(bits):
+        other = pack + 2**place * (1 - 2 * ((pack // 2**place) % 2))
+        pl.semaphore_signal(barrier, inc=1, device_id={"dp": other}, device_id_type=MESH)
+    for step in range(1, groups):
+        other = (group + step) % groups
+        pl.semaphore_signal(barrier, inc=1, device_id={"kv": other}, device_id_type=MESH)
+    pl.semaphore_wait(barrier, bits + groups - 1)
+
+
+def feed_forward_kernel(dp, groups, *refs):
+    (
+        attn_hbm, attn_ref, part_ref, own_hbm, gate_hbm, up_hbm, down_hbm, cot_hbm, live_hbm,
+        tokens_ref, gain_ref, live_ref,
+        act_out, hidden_out, gate_out, up_out, back_out, feed_out, resid_out, rows_out, all_out,
+        attn_in, all_ref, own_ref, w_gate, w_up, w_down, cot_ref, live_all, grad_hidden, resid_ref,
+        load_sem, send_sem, recv_sem, spread_send, spread_recv, out_sem,
+    ) = refs
+    block = pl.program_id(0)
+    blocks = groups
+    group = lax.axis_index("kv")
+    pack = lax.axis_index("dp")
+    rows = tokens_ref.shape[0]
+    others = groups - 1
+    spread = Spread(all_ref, spread_send, spread_recv, dp, all_ref.shape[3] // 2)
+    loads = [
+        pltpu.make_async_copy(source, target, load_sem.at[index])
+        for index, (source, target) in enumerate(
+            (
+                (down_hbm, w_down),
+                (cot_hbm, cot_ref),
+                (live_hbm, live_all),
+                (own_hbm, own_ref),
+                (gate_hbm, w_gate),
+                (up_hbm, w_up),
+            )
+        )
+    ]
+
+    def attn_copy(part, step, slot):
+        span = pl.ds(part * rows, rows)
+        return pltpu.make_async_remote_copy(
+            src_ref=attn_hbm.at[span],
+            dst_ref=attn_in.at[slot, span],
+            send_sem=send_sem.at[part, slot],
+            recv_sem=recv_sem.at[part, slot],
+            device_id={"kv": (group + 1 + step) % groups},
+            device_id_type=MESH,
+        )
+
+    def hidden_gradient(part):
+        span = pl.ds(part * rows, rows)
+        masked = (cot_ref[span].astype(jnp.float32) * live_all[span]).astype(jnp.bfloat16)
+        grad_hidden[span] = times_t(masked, w_down[...]).astype(jnp.bfloat16)
+
+    @pl.when(block == 0)
+    def _():
+        for load in loads:
+            load.start()
+        all_ref[:, pack] = part_ref[...]
+        greet(dp, groups)
+        for step in range(others):
+            attn_copy(0, step, others - 1 - step).start()
+        spread.start(0)
+        for part in range(1, blocks):
+            for step in range(others):
+                attn_copy(part, step, others - 1 - step).start()
+        for load in loads[:3]:
+            load.wait()
+        stages = dp.bit_length() - 1
+        for stage in range(stages):
+            if stage < blocks:
+                hidden_gradient(stage)
+            spread.wait_recv(stage)
+            if stage + 1 < stages:
+                spread.start(stage + 1)
+        for part in range(stages, blocks):
+            hidden_gradient(part)
+        for load in loads[3:]:
+            load.wait()
+
+    for slot in range(others):
+        attn_copy(block, 0, slot).wait_recv()
+    span = pl.ds(pl.multiple_of(block * rows, rows), rows)
+    width = own_ref.shape[0]
+    total = tokens_ref[...].astype(jnp.float32) + times(attn_ref[...], own_ref[...])
+    for slot in range(others):
+        total = total + times(attn_in[slot, span], all_ref[slot].reshape(width, -1))
+    resid_ref[...] = total
+    inverse = lax.rsqrt(jnp.mean(total * total, axis=1, keepdims=True) + EPS)
+    act = (total * inverse * gain_ref[...]).astype(jnp.bfloat16)
+    act_out[...] = act.T
+    gate = times(act, w_gate[...])
+    up = times(act, w_up[...])
+    chance = jax.nn.sigmoid(gate)
+    swish = gate * chance
+    hidden = swish * up
+    feed_out[...] = times(hidden.astype(jnp.bfloat16), w_down[...]).astype(jnp.bfloat16)
+    hidden_out[...] = (hidden * live_ref[...]).astype(jnp.bfloat16).T
+    grad = grad_hidden[span].astype(jnp.float32)
+    gate_b = (grad * up * chance * (1.0 + gate * (1.0 - chance))).astype(jnp.bfloat16)
+    up_b = (grad * swish).astype(jnp.bfloat16)
+    gate_out[...] = gate_b
+    up_out[...] = up_b
+    back_out[...] = (times_t(gate_b, w_gate[...]) + times_t(up_b, w_up[...])).astype(jnp.bfloat16)
+
+    @pl.when(block == group)
+    def _():
+        copy = pltpu.make_async_copy(resid_ref, resid_out, out_sem.at[0])
+        copy.start()
+        copy.wait()
+
+    @pl.when(block == blocks - 1)
+    def _():
+        mine = pl.ds(pl.multiple_of(group * rows, rows), rows)
+        copies = [
+            pltpu.make_async_copy(attn_in.at[:, mine], rows_out, out_sem.at[1]),
+            pltpu.make_async_copy(all_ref, all_out, out_sem.at[2]),
+        ]
+        for copy in copies:
+            copy.start()
+        for part in range(blocks):
+            for slot in range(others):
+                attn_copy(part, others - 1 - slot, slot).wait_send()
+        spread.wait_send()
+        for copy in copies:
+            copy.wait()
+
+
+def feed_forward(attn, part, w_own, w_gate, w_up, w_down, cotangent, live, tokens, gain, sizes, collective_id):
+    dp, groups = sizes
+    count, features = tokens.shape
+    rows = count // groups
+    width, hidden = w_own.shape[0], w_gate.shape[1]
+    share = part.shape[1]
+    others = groups - 1
+    any_spec = pl.BlockSpec(memory_space=pl.ANY)
+    by_row = lambda columns: pl.BlockSpec((rows, columns), lambda i: (i, 0))
+    by_column = lambda height: pl.BlockSpec((height, rows), lambda i: (0, i))
+    flops = 2 * count * features * (groups * width + 6 * hidden)
+    return pl.pallas_call(
+        functools.partial(feed_forward_kernel, dp, groups),
+        grid=(groups,),
+        out_shape=[
+            jax.ShapeDtypeStruct((features, count), jnp.bfloat16),
+            jax.ShapeDtypeStruct((hidden, count), jnp.bfloat16),
+            jax.ShapeDtypeStruct((count, hidden), jnp.bfloat16),
+            jax.ShapeDtypeStruct((count, hidden), jnp.bfloat16),
+            jax.ShapeDtypeStruct((count, features), jnp.bfloat16),
+            jax.ShapeDtypeStruct((count, features), jnp.bfloat16),
+            jax.ShapeDtypeStruct((rows, features), jnp.float32),
+            jax.ShapeDtypeStruct((others, rows, width), jnp.bfloat16),
+            jax.ShapeDtypeStruct((others, dp, share, features), jnp.bfloat16),
+        ],
+        in_specs=[
+            any_spec,
+            by_row(width),
+            pl.BlockSpec(memory_space=pltpu.VMEM),
+            any_spec, any_spec, any_spec, any_spec, any_spec, any_spec,
+            by_row(features),
+            pl.BlockSpec(memory_space=pltpu.VMEM),
+            by_row(1),
+        ],
+        out_specs=[
+            by_column(features), by_column(hidden), by_row(hidden), by_row(hidden),
+            by_row(features), by_row(features), any_spec, any_spec, any_spec,
+        ],
+        scratch_shapes=[
+            pltpu.VMEM((others, count, width), jnp.bfloat16),
+            pltpu.VMEM((others, dp, share, features), jnp.bfloat16),
+            pltpu.VMEM((width, features), jnp.bfloat16),
+            pltpu.VMEM((features, hidden), jnp.bfloat16),
+            pltpu.VMEM((features, hidden), jnp.bfloat16),
+            pltpu.VMEM((hidden, features), jnp.bfloat16),
+            pltpu.VMEM((count, features), jnp.bfloat16),
+            pltpu.VMEM((count, 1), jnp.float32),
+            pltpu.VMEM((count, hidden), jnp.bfloat16),
+            pltpu.VMEM((rows, features), jnp.float32),
+            pltpu.SemaphoreType.DMA((6,)),
+            pltpu.SemaphoreType.DMA((groups, others)),
+            pltpu.SemaphoreType.DMA((groups, others)),
+            pltpu.SemaphoreType.DMA((2, dp - 1)),
+            pltpu.SemaphoreType.DMA((2, dp - 1)),
+            pltpu.SemaphoreType.DMA((3,)),
+        ],
+        compiler_params=pltpu.CompilerParams(
+            collective_id=collective_id, has_side_effects=True, vmem_limit_bytes=VMEM_LIMIT
+        ),
+        cost_estimate=pl.CostEstimate(flops=flops, bytes_accessed=40 * count * features, transcendentals=0),
+    )(attn, attn, part, w_own, w_gate, w_up, w_down, cotangent, live, tokens, gain, live)
+
+
+def by_group(ring):
+    count = lax.axis_size("kv")
+    doubled = jnp.concatenate([ring, ring], axis=0)
+    return lax.dynamic_slice_in_dim(doubled, count - lax.axis_index("kv"), count, 0)
+
+
 def row_chunks(matrix, count):
-    chunks = matrix.T.reshape(count, matrix.shape[1] // count, matrix.shape[0])
+    chunks = matrix.reshape(count, matrix.shape[0] // count, matrix.shape[1])
     return jnp.pad(chunks, ((0, 0), (0, -chunks.shape[1] % 16), (0, 0)))
 
 
@@ -268,8 +536,12 @@
     def own_rows(array):
         return lax.dynamic_slice_in_dim(array, own_start, row_share, 0)
 
-    w_out_full = gather_weight(w_output[0]).reshape(-1, w_output.shape[2])
-    w_qkv_full = gather_weight(jnp.concatenate([w_query, w_key, w_value], axis=1))
+    pack_count, group_count = lax.axis_size("dp"), lax.axis_size("kv")
+    w_out_part = other_groups(gather_share(w_output[0]))
+    w_qkv_part, w_out_part = lax.optimization_barrier(
+        (jnp.concatenate([w_query, w_key, w_value], axis=1), w_out_part)
+    )
+    w_qkv_full = lax.all_gather(gather_share(w_qkv_part), "dp", axis=1, tiled=True)
     tokens_f = tokens_in.astype(jnp.float32)
     cosine, sinus = rope_tables(seg_positions(segments), head_width)
     act_one = norm_rows(tokens_f, attn_gain).astype(jnp.bfloat16)
@@ -309,51 +581,68 @@
         .reshape(row_count, head_count * head_width)
         .astype(jnp.bfloat16)
     )
-    attn_full = lax.all_gather(attn_out, "kv", axis=1, tiled=True)
-    resid_full = tokens_f + jnp.dot(attn_full, w_out_full, preferred_element_type=jnp.float32)
-    resid_mine = own_rows(resid_full)
-    act_two = norm_rows(resid_full, mlp_gain).astype(jnp.bfloat16)
-    gate_act = jnp.dot(act_two, w_gate, preferred_element_type=jnp.float32)
-    up_act = jnp.dot(act_two, w_up, preferred_element_type=jnp.float32)
-    hidden = swiglu(gate_act, up_act).astype(jnp.bfloat16)
-    feed_part = jnp.dot(hidden, w_down[0], preferred_element_type=jnp.float32)
-    live_rows = (places < counts[0]).astype(jnp.float32)
-    grad_out = cotangent.astype(jnp.float32) * live_rows[:, None]
-    grad_out_b = grad_out.astype(jnp.bfloat16)
-    grad_hidden = product_right(grad_out_b, w_down[0])
-    swiglu_out, swiglu_back = jax.vjp(swiglu, gate_act, up_act)
-    grad_gate, grad_up = swiglu_back(grad_hidden)
-    grad_gate = grad_gate.astype(jnp.bfloat16)
-    grad_up = grad_up.astype(jnp.bfloat16)
-    pack_count = lax.axis_size("dp")
-    act_chunks = row_chunks(act_two, pack_count)
+    live_rows = (places < counts[0]).astype(jnp.float32)[:, None]
+    (
+        act_flipped,
+        hidden_flipped,
+        grad_gate,
+        grad_up,
+        grad_act_two,
+        feed_part,
+        resid_mine,
+        attn_others,
+        w_out_others,
+    ) = feed_forward(
+        attn_out,
+        w_out_part,
+        w_output[0],
+        w_gate,
+        w_up,
+        w_down[0],
+        cotangent,
+        live_rows,
+        tokens_in,
+        mlp_gain[None],
+        (pack_count, group_count),
+        1,
+    )
+    act_chunks = row_chunks(act_flipped, pack_count)
     sent_gate, sent_up, sent_down = product_scatter(
         [
             (act_chunks, grad_gate),
             (act_chunks, grad_up),
-            (row_chunks(hidden, pack_count), grad_out_b),
+            (row_chunks(hidden_flipped, pack_count), cotangent),
         ],
-        1,
-    )
-    sent_down = sent_down[: hidden.shape[1] // pack_count][None]
-    grad_act_two = product_right(grad_gate, w_gate) + product_right(grad_up, w_up)
-    grad_two_mine = lax.psum_scatter(
-        grad_act_two.astype(jnp.bfloat16), "kv", scatter_dimension=0, tiled=True
-    ).astype(jnp.float32)
+        2,
+    )
+    sent_down = sent_down[: w_down.shape[1] // pack_count][None]
+    grad_two_mine = lax.psum_scatter(grad_act_two, "kv", scatter_dimension=0, tiled=True)
+    grad_two_mine, feed_part, sent_down = lax.optimization_barrier(
+        (grad_two_mine, feed_part, sent_down)
+    )
+    grad_out_mine = own_rows(cotangent).astype(jnp.float32) * own_rows(live_rows)
     norm_out, second_back = jax.vjp(norm_rows, resid_mine, mlp_gain)
-    grad_resid, gain_two = second_back(grad_two_mine)
-    grad_resid_mine = own_rows(grad_out) + grad_resid
+    grad_resid, gain_two = second_back(grad_two_mine.astype(jnp.float32))
+    grad_resid_mine = grad_out_mine + grad_resid
     grad_branch = grad_resid_mine.astype(jnp.bfloat16)
-    grad_attn_rows = product_right(grad_branch, w_out_full).astype(jnp.bfloat16)
-    grad_attn = lax.all_to_all(grad_attn_rows, "kv", 1, 0, tiled=True).reshape(
+    attn_ring = jnp.concatenate([own_rows(attn_out)[None], attn_others], axis=0)
+    w_out_ring = jnp.concatenate(
+        [w_output, w_out_others.reshape(group_count - 1, w_output.shape[1], -1)], axis=0
+    )
+    grad_attn_ring = jnp.einsum(
+        "rd,gcd->grc", grad_branch, w_out_ring, preferred_element_type=jnp.float32
+    ).astype(jnp.bfloat16)
+    grad_attn = lax.all_to_all(by_group(grad_attn_ring), "kv", 0, 0, tiled=True).reshape(
         row_count, head_count, head_width
     )
-    grad_woutput = product_left(own_rows(attn_full), grad_branch)
+    grad_woutput = by_group(
+        jnp.einsum("grc,rd->gcd", attn_ring, grad_branch, preferred_element_type=jnp.float32).astype(
+            jnp.bfloat16
+        )
+    )
     layer_out = (
         resid_mine
-        + lax.psum_scatter(
-            feed_part.astype(jnp.bfloat16), "kv", scatter_dimension=0, tiled=True
-        ).astype(jnp.float32)
+        + lax.psum_scatter(feed_part, "kv", scatter_dimension=0, tiled=True).astype(jnp.float32)
     ).astype(jnp.bfloat16)
     grad_query_parts = []
     grad_key_r = jnp.zeros((row_count, head_width), jnp.float32)
@@ -417,7 +706,6 @@
     grad_wkey = product_left(act_one, grad_key)
     grad_wvalue = product_left(act_one, grad_value)
     grad_qkv = jnp.concatenate([grad_query, grad_key, grad_value], axis=1)
-    group_count = lax.axis_size("kv")
     grad_qkv_rows = lax.all_to_all(
         grad_qkv.reshape(group_count, row_share, -1), "kv", 0, 0, tiled=True
     )
@@ -446,7 +734,7 @@
         ).astype(jnp.float32),
         lax.psum_scatter(
             lax.psum_scatter(
-                grad_woutput.reshape(group_count, -1, w_output.shape[2]).astype(jnp.bfloat16),
+                grad_woutput,
                 "dp",
                 scatter_dimension=1,
                 tiled=True,

time: 834 us -> 720 us (0.86)
  matrix products: 194 us -> 98.4 us
  waiting for transfers between devices: 287 us -> 192 us
  Pallas kernels: 127 us -> 214 us
    pallas_call x0 -> x1, Pallas kernels: none -> 125 us  [feed_forward(): pl.pallas_call(functools.partial(feed_forward_kernel, dp, groups), grid=(...]
    dot_general x8 -> x2, matrix products: 92.8 us -> 8.19 us  [the longest x1 5.81 us: per_device(): jnp.einsum('rd,gcd->grc', grad_branch, w_out_ring, preferred_element_type...]
    reduce_scatter x4, waiting for transfers between devices: 156 us -> 87.5 us  [the longest x1 66.9 us: per_device(): lax.psum_scatter(feed_part, 'kv', scatter_dimension=0, tiled=True)]
    all_gather x5 -> x3, waiting for transfers between devices: 129 us -> 64 us  [the longest x1 64 us: per_device(): lax.all_gather(gather_share(w_qkv_part), 'dp', axis=1, tiled=True)]
    pallas_call x1, Pallas kernels: 127 us -> 89 us  [product_scatter(): pl.pallas_call(functools.partial(product_scatter_kernel, count, dp), out_...]
    reduce_scatter x1, waiting for transfers between devices: 0.01 us -> 35.8 us  [per_device(): lax.psum_scatter(grad_wvalue.astype(jnp.bfloat16), 'dp', scatter_dimensio...]
    unnamed x102 -> x94, local copies, waits for them, and re-layouts: 22.1 us -> 14.9 us
  transfers between devices with their start and end apart: 13 -> 11, of which waited for: 6 -> 5; matrix products, arithmetic and copies ran while one was open for 26% -> 27% of each run, Pallas kernels for 16% -> 13%
where the time goes in v3:
time: 720 us; the launch traced here: 706 us
  Pallas kernels  214 us (30%)
  waiting for transfers between devices  192 us (27%)
  matrix products  98.4 us (14%)
  other arithmetic  77.5 us (11%)
  blocking collectives  71.3 us (10%)
  local copies, waits for them, and re-layouts  30.9 us (4%)
  between operations  16.6 us (2%)
    pallas_call x1, Pallas kernels, feed_forward(): pl.pallas_call(functools.partial(feed_forward_kernel, dp, groups), grid=(...  125 us
    pallas_call x1, Pallas kernels, product_scatter(): pl.pallas_call(functools.partial(product_scatter_kernel, count, dp), out_...  89 us
    reduce_scatter x1, waiting for transfers between devices, per_device(): lax.psum_scatter(feed_part, 'kv', scatter_dimension=0, tiled=True)  66.9 us
    all_gather x1, waiting for transfers between devices, per_device(): lax.all_gather(gather_share(w_qkv_part), 'dp', axis=1, tiled=True)  64 us
    all_to_all x1, blocking collectives, per_device(): lax.all_to_all(by_group(grad_attn_ring), 'kv', 0, 0, tiled=True)  38.2 us
    reduce_scatter x1, waiting for transfers between devices, per_device(): lax.psum_scatter(grad_wvalue.astype(jnp.bfloat16), 'dp', scatter_dimensio...  35.8 us
    unnamed x1, blocking collectives  23.7 us
    reduce_scatter x1, waiting for transfers between devices, per_device(): lax.psum_scatter(lax.psum_scatter(grad_woutput, 'dp', scatter_dimension=1...  20.6 us
  transfers between devices with their start and end apart: 11, of which 5 were waited for; matrix products, arithmetic and copies ran while one was open for 27% of the time, Pallas kernels for 13%

profile of v3, /device:TPU:8, one launch (start us, length us, event | category | flops | bytes accessed | tf_op | source)
XLA Modules:
  0.0 706.4 jit_solution(3779567400290924533)
XLA Ops:
  10.6 3.1 multiply_reduce_fusion
  14.7 3.2 multiply_convert_fusion
  23.0 4.6 fusion.96
  33.3 7.3 %fusion.94 = (f32[8,512]{1,0:T(8,128)S(1)}, f32[8,512,1024]{1,2,0:T(8,128)}) fusion(bf16[1024,8,64]{0,2,1:T(8,128)(2,1)S(1)} %fusion.25, bf16[1024,64]{0,1:T(8,128)(2,1)S(1)} %get-tuple-element.65, pred[512,1024]{0,1:T(8,128)(4,1)S(1)} %fusion.26), kind=kOutput, calls=%fused_computation.155 | convolution fusion | flops 549449728 | bytes 17973248 | tf_op jit(solution)/shard_map/qhd,kd->hqk/dot_general | solution.py:56
  43.0 8.0 %exponential_reduce_fusion = f32[8,512]{1,0:T(8,128)S(1)} fusion(f32[8,512,1024]{1,2,0:T(8,128)} %get-tuple-element.73, f32[8,512]{1,0:T(8,128)S(1)} %get-tuple-element.72), kind=kLoop, calls=%fused_computation.9 | loop fusion | flops 8384512 | bytes 16809984 | tf_op jit(solution)/shard_map/reduce_sum | solution.py:571
  51.0 8.4 %fusion.40 = bf16[512,8,64]{0,2,1:T(8,128)(2,1)S(1)} fusion(f32[8,512,1024]{1,2,0:T(8,128)} %get-tuple-element.73, f32[8,512]{1,0:T(8,128)S(1)} %log_add_fusion, bf16[1024,64]{0,1:T(8,128)(2,1)S(1)} %convolution_convert_fusion.5), kind=kOutput, calls=%fused_computation.73 | convolution fusion | flops 545521664 | bytes 17448960 | tf_op jit(solution)/shard_map/hqk,kd->qhd/dot_general | solution.py:574
  62.4 3.1 pad_maximum_fusion
  67.8 124.8 %shard_map.212 = (bf16[2048,1024]{1,0:T(8,128)(2,1)}, bf16[1408,1024]{1,0:T(8,128)(2,1)}, bf16[1024,1408]{1,0:T(8,128)(2,1)}, bf16[1024,1408]{1,0:T(8,128)(2,1)}...) custom-call(bf16[1024,512]{1,0:T(8,128)(2,1)} %copy.58.refs_0_.refs_, ...), custom_call_target="tpu_custom_call" | custom-call | flops 44023414784 | bytes 83886080 | tf_op jit(solution)/shard_map/pallas_call | solution.py:449
  192.6 89.0 %shard_map.213 = (f32[256,1408]{1,0:T(8,128)}, f32[256,1408]{1,0:T(8,128)}, f32[176,2048]{1,0:T(8,128)}) custom-call(bf16[8,256,1024]{2,1,0:T(8,128)(2,1)} %bitcast.179, bf16[8,256,1024]{2,1,0:T(8,128)(2,1)} %bitcast.180, bf16[8,176,1024]{2,1,0:T(8,128)(2,1)} %bitcast.181, bf16[1024,1408]{1,0:T(8,128)(2,1)} %get-tuple-element.34.refs_3_, ...), custom_call_target="tpu_custom_call" | custom-call | flops 53150220288 | bytes 21233664 | tf_op jit(solution)/shard_map/pallas_call | solution.py:225
  291.4 66.9 %reduce-scatter.10.cloned.1.call-done = bf16[256,2048]{1,0:T(8,128)(2,1)} async-done(((bf16[1024,2048]{1,0:T(8,128)(2,1)}), bf16[256,2048]{1,0:T(8,128)(2,1)}) %reduce-scatter.10.cloned.1.call-update) | async-done | bytes 1048592 | tf_op jit(solution)/shard_map/reduce_scatter | solution.py:645
  358.3 4.1 fusion.22
  364.8 4.9 fusion.4
  369.8 5.8 fusion.31
  376.0 38.2 %all_to_all.10 = bf16[4,256,512]{1,2,0:T(8,128)(2,1)S(1)} all-to-all(bf16[4,256,512]{1,2,0:T(8,128)(2,1)S(1)} %fusion.55), channel_id=1, replica_groups=mesh['dp'=8,'kv'=4] {'kv'}, dimensions={0} | all-to-all | bytes 2097152 | tf_op jit(solution)/shard_map/all_to_all | solution.py:635
  419.9 8.8 %fusion.9 = (f32[8,512]{1,0:T(8,128)S(1)}, f32[512,512,8]{1,0,2:T(8,128)}) fusion(f32[512,512,8]{1,0,2:T(8,128)} %copy-done, f32[8,512]{1,0:T(8,128)} %copy-done.31, pred[512,512]{0,1:T(8,128)(4,1)S(1)} %compare_and_fusion, bf16[512,8,64]{0,2,1:T(8,128)(2,1)S(1)} %slice.95, bf16[1024,64]{0,1:T(8,128)(2,1)S(1)} %convolution_convert_fusion.5), kind=kOutput, calls=%fused_computation.18 | convolution fusion | flops 278917120 | bytes 17661952 | tf_op jit(solution)/shard_map/qhd,kd->hqk/dot_general | solution.py:663
  428.8 8.7 %fusion.11 = bf16[8,512,512]{1,2,0:T(8,128)(2,1)S(1)} fusion(f32[512,512,8]{1,0,2:T(8,128)} %get-tuple-element.79, f32[512,512,8]{1,0,2:T(8,128)} %copy-done, f32[8,512]{1,0:T(8,128)S(1)} %get-tuple-element.78, f32[8,512]{1,0:T(8,128)S(1)} %copy-done.32, pred[512,512]{0,1:T(8,128)(4,1)S(1)} %compare_and_fusion), kind=kLoop, calls=%fused_computation.20 | loop fusion | flops 12582912 | bytes 21266432 | tf_op jit(solution)/shard_map/convert_element_type | solution.py:670
  440.8 7.7 %fusion = (f32[8,512]{1,0:T(8,128)S(1)}, f32[1024,512,8]{1,0,2:T(8,128)}) fusion(f32[8,512,1024]{1,2,0:T(8,128)S(1)} %bitcast.164, f32[8,512]{1,0:T(8,128)S(1)} %log_add_fusion, bf16[512,8,64]{0,2,1:T(8,128)(2,1)S(1)} %slice.97, bf16[1024,64]{0,1:T(8,128)(2,1)S(1)} %convolution_convert_fusion.5), kind=kOutput, calls=%fused_computation.4 | convolution fusion | flops 549449728 | bytes 34242560 | tf_op jit(solution)/shard_map/qhd,kd->hqk/dot_general | solution.py:663
  448.5 8.0 %fusion.2 = bf16[8,512,1024]{1,2,0:T(8,128)(2,1)S(1)} fusion(f32[1024,512,8]{1,0,2:T(8,128)} %get-tuple-element.77, f32[8,512,1024]{1,2,0:T(8,128)S(1)} %bitcast.164, f32[8,512]{1,0:T(8,128)S(1)} %get-tuple-element.76, f32[8,512]{1,0:T(8,128)S(1)} %log_add_fusion), kind=kLoop, calls=%fused_computation.6 | loop fusion | flops 16777216 | bytes 41975808 | tf_op jit(solution)/shard_map/convert_element_type | solution.py:670
  463.5 6.8 convolution_bitcast_fusion.2
  470.6 8.8 %fusion.51 = bf16[1024,64]{0,1:T(8,128)(2,1)S(1)} fusion(bf16[512,8,64]{0,2,1:T(8,128)(2,1)S(1)} %slice.97, f32[8,512,1024]{1,2,0:T(8,128)} %get-tuple-element.73, f32[8,512]{1,0:T(8,128)S(1)} %log_add_fusion, f32[512,64]{0,1:T(8,128)} %convolution_bitcast_fusion.2), kind=kOutput, calls=%fused_computation.80 | convolution fusion | flops 545390592 | bytes 17580032 | tf_op jit(solution)/shard_map/hqk,qhd->kd/dot_general | solution.py:687
  484.9 5.0 fusion.34
  492.4 3.7 convolution_convert_fusion.1
  499.0 5.0 all-to-all-start.1
  504.5 6.5 convert_element_type.114
  514.1 3.7 reduce-scatter.14.cloned.1.call-done
  519.2 35.8 %reduce-scatter.16.cloned.1.call-done = bf16[256,64]{0,1:T(8,128)(2,1)} async-done(((bf16[2048,64]{0,1:T(8,128)(2,1)}), bf16[256,64]{0,1:T(8,128)(2,1)}) %reduce-scatter.16.cloned.1.call-update) | async-done | bytes 32784 | tf_op jit(solution)/shard_map/reduce_scatter | solution.py:732
  556.4 64.0 %all-gather.7.cloned.1.call-done = bf16[4,2048,640]{2,1,0:T(8,128)(2,1)} async-done(((bf16[4,256,640]{2,1,0:T(8,128)(2,1)}), bf16[4,2048,640]{2,1,0:T(8,128)(2,1)}) %all-gather.7.cloned.1.call-update) | async-done | bytes 10485776 | tf_op jit(solution)/shard_map/all_gather | solution.py:544
  620.4 12.4 %multiply_reduce_fusion.1 = (f32[2048]{0:T(1024)S(1)}, f32[256]{0:T(256)S(1)}, f32[256,2048]{1,0:T(8,128)}) fusion(f32[1024,2048]{1,0:T(8,128)} %convert_element_type.114, s32[]{:T(128)S(6)} %select_n.39, f32[256]{0:T(256)S(1)} %fusion.85, f32[2048]{0:T(1024)S(1)} %copy-done.36, bf16[4,256,640]{2,1,0:T(8,128)(2,1)S(1)} %all-to-all-done.1, ...), kind=kOutput, calls=%fused_computation.54 | convolution fusion | flops 2687497984 | bytes 16009220 | tf_op jit(solution)/shard_map/grc,gdc->rd/dot_general | solution.py:712
  632.8 23.7 %all-reduce.8 = (f32[2048]{0:T(1024)S(1)}, f32[2048]{0:T(1024)S(1)}) all-reduce(f32[2048]{0:T(1024)S(1)} %get-tuple-element.45, f32[2048]{0:T(1024)S(1)} %copy-done.34), channel_id=5, replica_groups=mesh['dp'=8,'kv'=4] {'dp'}, use_global_device_ids=true, to_apply=%region_17.18.clone | all-reduce | flops 4096 | bytes 32768
  656.6 9.4 %all-reduce.9 = (f32[256]{0:T(256)}, f32[256]{0:T(256)}) all-reduce(f32[256]{0:T(256)S(1)} %dynamic-slice.6, f32[256]{0:T(256)S(1)} %dynamic-slice.8), channel_id=1, replica_groups=mesh['dp'=8,'kv'=4] {'kv'}, use_global_device_ids=true, to_apply=%region_16.17 | all-reduce | flops 512 | bytes 4096 | tf_op jit(solution)/shard_map/psum | solution.py:746
  666.1 4.0 fusion.23
  672.1 20.6 %reduce-scatter.20.cloned.1.call-done = bf16[1,64,2048]{2,1,0:T(8,128)(2,1)} async-done(((bf16[4,64,2048]{2,1,0:T(8,128)(2,1)}), bf16[1,64,2048]{2,1,0:T(8,128)(2,1)}) %reduce-scatter.20.cloned.1.call-update) | async-done | bytes 262160 | tf_op jit(solution)/shard_map/reduce_scatter | solution.py:735
  (190 shorter events, 75.8 us)
Async XLA Ops:
  7.2 6.5 copy-start.28
  7.2 7.5 %copy-start.35 = (f32[2048]{0:T(1024)S(1)}, f32[2048]{0:T(1024)}, u32[]{:S(2)}) copy-start(f32[2048]{0:T(1024)} %param.14) | copy-start | bytes 24580
  7.2 58.3 %all-gather.5.cloned.1.call-start = ((), (), s32[]{:S(2)}) async-start(), calls=%async_computation.9 | async-start | bytes 1310720 | tf_op jit(solution)/shard_map/all_gather | solution.py:72
  9.0 272.7 %reduce-scatter.8.cloned.1.call-start = ((), (), s32[]{:S(2)}) async-start(), calls=%async_computation.10 | async-start | bytes 5242880 | tf_op jit(solution)/shard_map/reduce_scatter | solution.py:619
  28.7 4.6 copy-start.16
  30.8 9.9 %copy-start = (f32[512,512,8]{1,0,2:T(8,128)}, f32[512,512,8]{1,0,2:T(8,128)S(1)}, u32[]{:S(2)}) copy-start(f32[512,512,8]{1,0,2:T(8,128)S(1)} %get-tuple-element.75) | copy-start | bytes 25165828
  32.5 8.1 %copy-start.31 = (f32[8,512]{1,0:T(8,128)}, f32[8,512]{1,0:T(8,128)S(1)}, u32[]{:S(2)}) copy-start(f32[8,512]{1,0:T(8,128)S(1)} %log_add_fusion.1) | copy-start | bytes 49156
  192.6 165.7 %reduce-scatter.10.cloned.1.call-start = ((), (), s32[]{:S(2)}) async-start(), calls=%async_computation.11 | async-start | bytes 5242880 | tf_op jit(solution)/shard_map/reduce_scatter | solution.py:645
  281.6 5.1 copy-start.7
  281.7 199.4 %all-gather.9.cloned.1.call-start = ((), (), s32[]{:S(2)}) async-start(), calls=%async_computation.18 | async-start | bytes 1638400 | tf_op jit(solution)/shard_map/all_gather | solution.py:72
  283.1 5.0 copy-start.10
  288.1 215.8 %reduce-scatter.18.cloned.1.call-start = ((), (), s32[]{:S(2)}) async-start(), calls=%async_computation.16 | async-start | bytes 9437184 | tf_op jit(solution)/shard_map/reduce_scatter | solution.py:736
  369.8 148.0 %reduce-scatter.14.cloned.1.call-start = ((), (), s32[]{:S(2)}) async-start(), calls=%async_computation.14 | async-start | bytes 294912 | tf_op jit(solution)/shard_map/reduce_scatter | solution.py:729
  419.9 8.8 %copy-start.32 = (f32[8,512]{1,0:T(8,128)S(1)}, f32[8,512]{1,0:T(8,128)}, u32[]{:S(2)}) copy-start(f32[8,512]{1,0:T(8,128)} %copy-done.31) | copy-start | bytes 49156
  419.9 20.9 %slice-start = ((s8[16777216]{0:T(1024)(128)(4,1)}), s8[4194304]{0:T(1024)(128)(4,1)S(1)}, s32[]{:S(2)}) async-start(s8[16777216]{0:T(1024)(128)(4,1)} %bitcast.163), calls=%async_computation.19 | async-start | bytes 8388608
  419.9 20.9 %slice-start.1 = ((s8[16777216]{0:T(1024)(128)(4,1)}), s8[4194304]{0:T(1024)(128)(4,1)S(1)}, s32[]{:S(2)}) async-start(s8[16777216]{0:T(1024)(128)(4,1)} %bitcast.163), calls=%async_computation.20 | async-start | bytes 8388608
  428.7 10.7 %copy-start.9 = (bf16[1024,8,64]{0,2,1:T(8,128)(2,1)S(1)}, bf16[1024,8,64]{0,2,1:T(8,128)(2,1)}, u32[]{:S(2)}) copy-start(bf16[1024,8,64]{0,2,1:T(8,128)(2,1)} %copy-done.8) | copy-start | bytes 3145732
  428.8 12.1 %slice-start.2 = ((s8[16777216]{0:T(1024)(128)(4,1)}), s8[4194304]{0:T(1024)(128)(4,1)S(1)}, s32[]{:S(2)}) async-start(s8[16777216]{0:T(1024)(128)(4,1)} %bitcast.163), calls=%async_computation.21 | async-start | bytes 8388608
  428.8 12.1 %slice-start.3 = ((s8[16777216]{0:T(1024)(128)(4,1)}), s8[4194304]{0:T(1024)(128)(4,1)S(1)}, s32[]{:S(2)}) async-start(s8[16777216]{0:T(1024)(128)(4,1)} %bitcast.163), calls=%async_computation.22 | async-start | bytes 8388608
  456.6 5.4 copy-start.2
  470.4 84.6 %reduce-scatter.16.cloned.1.call-start = ((), (), s32[]{:S(2)}) async-start(), calls=%async_computation.15 | async-start | bytes 294912 | tf_op jit(solution)/shard_map/reduce_scatter | solution.py:732
  470.6 8.8 %copy-start.3 = (bf16[1024,2048]{1,0:T(8,128)(2,1)S(1)}, bf16[1024,2048]{1,0:T(8,128)(2,1)}, u32[]{:S(2)}) copy-start(bf16[1024,2048]{1,0:T(8,128)(2,1)} %copy-done.1) | copy-start | bytes 12582916
  481.0 139.3 %all-gather.7.cloned.1.call-start = ((), (), s32[]{:S(2)}) async-start(), calls=%async_computation.12 | async-start | bytes 11796480 | tf_op jit(solution)/shard_map/all_gather | solution.py:544
  481.8 188.3 %reduce-scatter.12.cloned.1.call-start = ((), (), s32[]{:S(2)}) async-start(), calls=%async_computation.13 | async-start | bytes 2359296 | tf_op jit(solution)/shard_map/reduce_scatter | solution.py:726
  484.9 5.0 copy-start.13
  499.0 57.5 %all-to-all-start.1 = ((bf16[4,256,640]{2,1,0:T(8,128)(2,1)}), bf16[4,256,640]{2,1,0:T(8,128)(2,1)S(1)}, u32[]{:S(2)}, u32[]{:S(2)}) async-start(bf16[4,256,640]{2,1,0:T(8,128)(2,1)} %bitcast.37), calls=%async_computation.3 | async-start | bytes 2621440 | tf_op jit(solution)/shard_map/all_to_all | solution.py:709
  503.9 188.8 %reduce-scatter.20.cloned.1.call-start = ((), (), s32[]{:S(2)}) async-start(), calls=%async_computation.17 | async-start | bytes 1310720 | tf_op jit(solution)/shard_map/reduce_scatter | solution.py:735
  504.5 6.5 copy-start.38
  504.5 115.9 %copy-start.36 = (f32[2048]{0:T(1024)S(1)}, f32[2048]{0:T(1024)}, u32[]{:S(2)}) copy-start(f32[2048]{0:T(1024)} %param.14) | copy-start | bytes 24580
  556.4 76.4 %copy-start.34 = (f32[2048]{0:T(1024)S(1)}, f32[2048]{0:T(1024)}, u32[]{:S(2)}) copy-start(f32[2048]{0:T(1024)} %get-tuple-element.47) | copy-start | bytes 24580
  670.1 26.9 %copy-start.21 = (f32[256,1408]{1,0:T(8,128)S(1)}, f32[256,1408]{1,0:T(8,128)}, u32[]{:S(2)}) copy-start(f32[256,1408]{1,0:T(8,128)} %get-tuple-element.101) | copy-start | bytes 4325380
  670.1 28.0 %copy-start.20 = (f32[176,2048]{1,0:T(8,128)S(1)}, f32[176,2048]{1,0:T(8,128)}, u32[]{:S(2)}) copy-start(f32[176,2048]{1,0:T(8,128)} %get-tuple-element.36) | copy-start | bytes 4325380
  (22 other events, 55.7 us)
Sparse Core Ops, SparseCore 0:
  10.2 29.0 all-gather.4
  192.7 77.7 reduce-scatter.7
  281.8 76.4 reduce-scatter.9
  360.3 42.6 all-gather.8
  406.3 74.0 reduce-scatter.17
  484.2 33.5 reduce-scatter.13
  521.4 33.5 reduce-scatter.15
  557.1 63.2 all-gather.6
  624.0 41.3 reduce-scatter.11
  667.5 25.0 reduce-scatter.19

commit v4 on v3

v4 whole, which is shorter than its diff:
```python
import functools

import jax
import jax.numpy as jnp
from jax import lax
from jax.experimental import pallas as pl
from jax.experimental.pallas import tpu as pltpu
from jax.sharding import PartitionSpec as P

EPS = 1e-05
LOG2E = 1.4426950408889634
MESH = pl.DeviceIdType.MESH
VMEM_LIMIT = 60 * 1024 * 1024


def row_halves(rows):
    upper = -(-rows // 32) * 16
    return ((0, upper), (upper, rows - upper))


def times(first, second):
    return jnp.dot(first, second, preferred_element_type=jnp.float32)


def times_t(first, second):
    return lax.dot_general(
        first, second, (((1,), (1,)), ((), ())), preferred_element_type=jnp.float32
    )


def to_group(step, groups, source, target, sems):
    return pltpu.make_async_remote_copy(
        src_ref=source,
        dst_ref=target,
        send_sem=sems.at[0, step - 1],
        recv_sem=sems.at[1, step - 1],
        device_id={"kv": (lax.axis_index("kv") + step) % groups},
        device_id_type=MESH,
    )


class Spread:
    def __init__(self, buffer, send_sem, recv_sem, dp):
        self.buffer, self.send_sem, self.recv_sem = buffer, send_sem, recv_sem
        self.me = lax.axis_index("dp")
        self.bits = dp.bit_length() - 1
        columns = buffer.shape[3]
        split = -(-columns // 256) * 128
        self.columns = ((0, split), (split, columns - split))

    def flipped(self, places):
        device = self.me
        for place in places:
            device = device + 2**place * (1 - 2 * ((self.me // 2**place) % 2))
        return device

    def copies(self, stage, arriving):
        result = []
        for half in range(2):
            order = list(range(1, self.bits))
            order = (order if half == 0 else order[::-1]) + [0]
            for subset in range(2**stage):
                places = [order[b] for b in range(stage) if subset >> b & 1]
                if arriving:
                    places = places + [order[stage]]
                part = self.buffer.at[:, self.flipped(places), :, pl.ds(*self.columns[half])]
                number = 2**stage - 1 + subset
                result.append(
                    pltpu.make_async_remote_copy(
                        src_ref=part,
                        dst_ref=part,
                        send_sem=self.send_sem.at[half, number],
                        recv_sem=self.recv_sem.at[half, number],
                        device_id={"dp": self.flipped([order[stage]])},
                        device_id_type=MESH,
                    )
                )
        return result

    def start(self, stage):
        for copy in self.copies(stage, False):
            copy.start()

    def wait_recv(self, stage):
        for copy in self.copies(stage, True):
            copy.wait_recv()

    def wait_send(self):
        for stage in range(self.bits):
            for copy in self.copies(stage, False):
                copy.wait_send()


def greet(dp, groups):
    pack, group = lax.axis_index("dp"), lax.axis_index("kv")
    bits = dp.bit_length() - 1
    barrier = pltpu.get_barrier_semaphore()
    for place in range(bits):
        other = pack + 2**place * (1 - 2 * ((pack // 2**place) % 2))
        pl.semaphore_signal(barrier, inc=1, device_id={"dp": other}, device_id_type=MESH)
    for step in range(1, groups):
        other = (group + step) % groups
        pl.semaphore_signal(barrier, inc=1, device_id={"kv": other}, device_id_type=MESH)
    pl.semaphore_wait(barrier, bits + groups - 1)


def attention_kernel(groups, head_width, *refs):
    (
        tokens_ref, gain_ref, query_w, pair_w, seg_column, seg_row, frequency, part_hbm,
        attn_out, act_out, query_out, key_out, value_out, logsum_out,
        cosine_out, sine_a_out, sine_b_out, cosine_t_out, sine_t_out, parts_out,
        query_m, value_t, part_sems,
    ) = refs
    rows = tokens_ref.shape[0] // groups
    width, span_w = query_w.shape[1], key_out.shape[1]
    heads, pair, half = span_w // head_width, 2 * head_width, head_width // 2
    scale = head_width**-0.5 * LOG2E

    def part_copy(step):
        return to_group(step, groups, part_hbm, parts_out.at[groups - 1 - step], part_sems)

    greet(1, groups)
    for step in range(1, groups):
        part_copy(step).start()
    lanes = lax.broadcasted_iota(jnp.int32, (rows, pair), 1)
    low_half = lanes % head_width < half
    head_lanes = lax.broadcasted_iota(jnp.int32, (rows, span_w), 1) // head_width

    for block in range(groups):
        part = pl.ds(block * rows, rows)
        values = tokens_ref[part].astype(jnp.float32)
        inverse = lax.rsqrt(jnp.mean(values * values, axis=1, keepdims=True) + EPS)
        act = (values * inverse * gain_ref[...]).astype(jnp.bfloat16)
        act_out[:, part] = act.T
        query_raw = times(act, query_w[...])
        pair_raw = times(act, pair_w[...])
        before = (seg_row[...] < seg_column[part]).astype(jnp.float32)
        places = (
            lax.broadcasted_iota(jnp.int32, (rows, 1), 0) + block * rows
        ).astype(jnp.float32) - jnp.sum(before, axis=1, keepdims=True)
        angles = places * frequency[...]
        cosine, sine = jnp.cos(angles), jnp.sin(angles)
        sine_a, sine_b = jnp.where(low_half, -sine, 0.0), jnp.where(low_half, 0.0, sine)
        cosine_out[part], sine_a_out[part], sine_b_out[part] = cosine, sine_a, sine_b
        cosine_t_out[:, part] = cosine.T[:half]
        sine_t_out[:, part] = sine.T[:half]

        def rotated(vectors):
            return (
                vectors * cosine
                + pltpu.roll(vectors, pair - half, 1) * sine_a
                + pltpu.roll(vectors, half, 1) * sine_b
            ).astype(jnp.bfloat16)

        for start in range(0, width, pair):
            query_out[part, pl.ds(start, pair)] = rotated(query_raw[:, start : start + pair])
        other = pltpu.roll(pair_raw, head_width, 1)
        keys_two = rotated(jnp.where(lanes < head_width, pair_raw, other))
        values_two = jnp.where(lanes < head_width, other, pair_raw)
        key_out[part] = jnp.concatenate([keys_two] * (span_w // pair), axis=1)
        value_out[part] = jnp.concatenate(
            [values_two.astype(jnp.bfloat16)] * (span_w // pair), axis=1
        )
        value_t[:, part] = values_two.T[:head_width].astype(jnp.bfloat16)
        query_seg = seg_row[:, part]
        query_place = lax.broadcasted_iota(jnp.int32, (rows, rows), 1) + block * rows

        def span(number, carry):
            columns = pl.ds(pl.multiple_of(number * span_w, span_w), span_w)
            query = query_out[part, columns]
            for head in range(heads):
                query_m[pl.ds(head * rows, rows)] = jnp.where(head_lanes == head, query, 0)

            def keys(step, carry):
                highest, total, output = carry
                piece = block - step
                key_part = pl.ds(pl.multiple_of(piece * rows, rows), rows)
                key_place = lax.broadcasted_iota(jnp.int32, (rows, rows), 0) + piece * rows
                allowed = (seg_column[key_part] == query_seg) & (key_place <= query_place)
                bias = jnp.where(allowed, 0.0, -jnp.inf)
                scores = times_t(key_out[key_part], query_m[...]) * scale
                scores = scores + jnp.concatenate([bias] * heads, axis=1)
                top = jnp.maximum(highest, jnp.max(scores, axis=0, keepdims=True))
                shrink = jnp.exp2(highest - top)
                chance = jnp.exp2(scores - top)
                total = total * shrink + jnp.sum(chance, axis=0, keepdims=True)
                output = output * shrink + times(value_t[:, key_part], chance.astype(jnp.bfloat16))
                return top, total, output

            first = (
                jnp.full((1, heads * rows), -jnp.inf, jnp.float32),
                jnp.zeros((1, heads * rows), jnp.float32),
                jnp.zeros((head_width, heads * rows), jnp.float32),
            )
            highest, total, output = lax.fori_loop(0, block + 1, keys, first)
            output = output / total
            stacked = jnp.concatenate(
                [output[:, head * rows : (head + 1) * rows] for head in range(heads)], axis=0
            )
            attn_out[part, columns] = stacked.T.astype(jnp.bfloat16)
            logsum_out[number * groups + block] = highest + jnp.log(total) * LOG2E
            return carry

        lax.fori_loop(0, width // span_w, span, 0)
    for step in range(1, groups):
        part_copy(step).wait()


def attention(tokens, gain, query_w, pair_w, segments, part, groups, collective_id):
    count, features = tokens.shape
    width, head_width = query_w.shape[1], pair_w.shape[1] // 2
    span_w = 256
    rows, heads, half = count // groups, span_w // head_width, head_width // 2
    frequency = 10000.0 ** (-(jnp.arange(half, dtype=jnp.float32) * 2.0 / head_width))
    vmem = pl.BlockSpec(memory_space=pltpu.VMEM)
    any_spec = pl.BlockSpec(memory_space=pl.ANY)
    bf16, f32 = jnp.bfloat16, jnp.float32
    return pl.pallas_call(
        functools.partial(attention_kernel, groups, head_width),
        out_shape=[
            jax.ShapeDtypeStruct((count, width), bf16),
            jax.ShapeDtypeStruct((features, count), bf16),
            jax.ShapeDtypeStruct((count, width), bf16),
            jax.ShapeDtypeStruct((count, span_w), bf16),
            jax.ShapeDtypeStruct((count, span_w), bf16),
            jax.ShapeDtypeStruct((width // span_w * groups, 1, heads * rows), f32),
            jax.ShapeDtypeStruct((count, 2 * head_width), f32),
            jax.ShapeDtypeStruct((count, 2 * head_width), f32),
            jax.ShapeDtypeStruct((count, 2 * head_width), f32),
            jax.ShapeDtypeStruct((half, count), f32),
            jax.ShapeDtypeStruct((half, count), f32),
            jax.ShapeDtypeStruct((groups - 1,) + part.shape, bf16),
        ],
        in_specs=[vmem] * 7 + [any_spec],
        out_specs=[vmem] * 11 + [any_spec],
        scratch_shapes=[
            pltpu.VMEM((heads * rows, span_w), bf16),
            pltpu.VMEM((head_width, count), bf16),
            pltpu.SemaphoreType.DMA((2, groups - 1)),
        ],
        compiler_params=pltpu.CompilerParams(
            collective_id=collective_id, has_side_effects=True, vmem_limit_bytes=VMEM_LIMIT
        ),
        cost_estimate=pl.CostEstimate(
            flops=4 * count * features * width, bytes_accessed=8 * tokens.size, transcendentals=0
        ),
    )(
        tokens,
        gain,
        query_w,
        pair_w,
        segments[:, None],
        segments[None],
        jnp.tile(frequency, 4)[None],
        part,
    )


def feed_forward_kernel(dp, groups, *refs):
    (
        attn_hbm, attn_ref, part_ref, own_hbm, gate_hbm, up_hbm, down_hbm, cot_hbm, live_hbm,
        tokens_ref, gain_ref, live_ref,
        act_out, hidden_out, gate_out, up_out, back_out, feed_out, resid_out, rows_out, all_out,
        attn_in, all_ref, own_ref, w_gate, w_up, w_down, cot_ref, live_all, grad_hidden, resid_ref,
        load_sem, send_sem, recv_sem, spread_send, spread_recv, out_sem,
    ) = refs
    block = pl.program_id(0)
    blocks = groups
    group = lax.axis_index("kv")
    pack = lax.axis_index("dp")
    rows = tokens_ref.shape[0]
    others = groups - 1
    spread = Spread(all_ref, spread_send, spread_recv, dp)
    loads = [
        pltpu.make_async_copy(source, target, load_sem.at[index])
        for index, (source, target) in enumerate(
            (
                (down_hbm, w_down),
                (cot_hbm, cot_ref),
                (live_hbm, live_all),
                (own_hbm, own_ref),
                (gate_hbm, w_gate),
                (up_hbm, w_up),
            )
        )
    ]

    def attn_copy(part, step, slot, source, place):
        span = pl.ds(part * rows, rows)
        return pltpu.make_async_remote_copy(
            src_ref=source.at[span],
            dst_ref=attn_in.at[slot, span],
            send_sem=send_sem.at[part, place],
            recv_sem=recv_sem.at[part, slot],
            device_id={"kv": (group + step) % groups},
            device_id_type=MESH,
        )

    def send_rows(part):
        for step in range(1, groups):
            copy = attn_copy(part, step, others - step, attn_hbm, step - 1)
            if step in relayed:
                pl.when((group == 0) | (group == 3))(copy.start)
            else:
                copy.start()

    relayed = (2,) if groups == 4 else ()
    relays = ((1, 0, 3), (2, 2, 1)) if groups == 4 else ()

    def wait_rows(part, slot):
        attn_copy(part, 1, slot, attn_hbm, 0).wait_recv()

    def pass_on(part):
        for holder, slot, step in relays:

            @pl.when(group == holder)
            def _():
                wait_rows(part, slot)
                attn_copy(part, step, 1, attn_in.at[slot], 1).start()

    def wait_block(part):
        for slot in range(others):
            holders = [holder for holder, place, _ in relays if place == slot]
            if holders:

                @pl.when(group != holders[0])
                def _():
                    wait_rows(part, slot)
            else:
                wait_rows(part, slot)

    def hidden_gradient(part):
        span = pl.ds(part * rows, rows)
        masked = (cot_ref[span].astype(jnp.float32) * live_all[span]).astype(jnp.bfloat16)
        grad_hidden[span] = times_t(masked, w_down[...]).astype(jnp.bfloat16)

    @pl.when(block == 0)
    def _():
        for load in loads:
            load.start()
        all_ref[:, pack] = part_ref[...]
        greet(dp, groups)
        send_rows(0)
        spread.start(0)
        for part in range(1, blocks):
            send_rows(part)
        for load in loads[:3]:
            load.wait()
        stages = dp.bit_length() - 1
        for stage in range(stages):
            if stage < blocks:
                hidden_gradient(stage)
            spread.wait_recv(stage)
            if stage + 1 < stages:
                spread.start(stage + 1)
            if stage < 2:
                pass_on(stage)
        for part in range(stages, blocks):
            hidden_gradient(part)
        for load in loads[3:]:
            load.wait()

    wait_block(block)
    span = pl.ds(pl.multiple_of(block * rows, rows), rows)
    width = own_ref.shape[0]
    total = tokens_ref[...].astype(jnp.float32) + times(attn_ref[...], own_ref[...])
    for slot in range(others):
        total = total + times_t(attn_in[slot, span], all_ref[slot].reshape(-1, width))
    resid_ref[...] = total
    inverse = lax.rsqrt(jnp.mean(total * total, axis=1, keepdims=True) + EPS)
    act = (total * inverse * gain_ref[...]).astype(jnp.bfloat16)
    act_out[...] = act.T
    gate = times(act, w_gate[...])
    up = times(act, w_up[...])
    chance = jax.nn.sigmoid(gate)
    swish = gate * chance
    hidden = swish * up
    feed_out[...] = times(hidden.astype(jnp.bfloat16), w_down[...]).astype(jnp.bfloat16)
    hidden_out[...] = (hidden * live_ref[...]).astype(jnp.bfloat16).T
    grad = grad_hidden[span].astype(jnp.float32)
    gate_b = (grad * up * chance * (1.0 + gate * (1.0 - chance))).astype(jnp.bfloat16)
    up_b = (grad * swish).astype(jnp.bfloat16)
    gate_out[...] = gate_b
    up_out[...] = up_b
    back_out[...] = (times_t(gate_b, w_gate[...]) + times_t(up_b, w_up[...])).astype(jnp.bfloat16)

    @pl.when(block == group)
    def _():
        copy = pltpu.make_async_copy(resid_ref, resid_out, out_sem.at[0])
        copy.start()
        copy.wait()

    @pl.when(block < blocks - 2)
    def _():
        pass_on(block + 2)

    @pl.when(block == blocks - 1)
    def _():
        mine = pl.ds(pl.multiple_of(group * rows, rows), rows)
        copies = [
            pltpu.make_async_copy(attn_in.at[:, mine], rows_out, out_sem.at[1]),
            pltpu.make_async_copy(all_ref, all_out, out_sem.at[2]),
        ]
        for copy in copies:
            copy.start()
        for part in range(blocks):
            for place in range(others):
                attn_copy(part, 1, 0, attn_hbm, place).wait_send()
        spread.wait_send()
        for copy in copies:
            copy.wait()


def feed_forward(attn, part, w_own, w_gate, w_up, w_down, cotangent, live, tokens, gain, sizes, collective_id):
    dp, groups = sizes
    count, features = tokens.shape
    rows = count // groups
    width, hidden = w_own.shape[0], w_gate.shape[1]
    share = part.shape[1]
    others = groups - 1
    any_spec = pl.BlockSpec(memory_space=pl.ANY)
    by_row = lambda columns: pl.BlockSpec((rows, columns), lambda i: (i, 0))
    by_column = lambda height: pl.BlockSpec((height, rows), lambda i: (0, i))
    flops = 2 * count * features * (groups * width + 6 * hidden)
    return pl.pallas_call(
        functools.partial(feed_forward_kernel, dp, groups),
        grid=(groups,),
        out_shape=[
            jax.ShapeDtypeStruct((features, count), jnp.bfloat16),
            jax.ShapeDtypeStruct((hidden, count), jnp.bfloat16),
            jax.ShapeDtypeStruct((count, hidden), jnp.bfloat16),
            jax.ShapeDtypeStruct((count, hidden), jnp.bfloat16),
            jax.ShapeDtypeStruct((count, features), jnp.bfloat16),
            jax.ShapeDtypeStruct((count, features), jnp.bfloat16),
            jax.ShapeDtypeStruct((rows, features), jnp.float32),
            jax.ShapeDtypeStruct((others, rows, width), jnp.bfloat16),
            jax.ShapeDtypeStruct((others, dp, share, width), jnp.bfloat16),
        ],
        in_specs=[
            any_spec,
            by_row(width),
            pl.BlockSpec(memory_space=pltpu.VMEM),
            any_spec, any_spec, any_spec, any_spec, any_spec, any_spec,
            by_row(features),
            pl.BlockSpec(memory_space=pltpu.VMEM),
            by_row(1),
        ],
        out_specs=[
            by_column(features), by_column(hidden), by_row(hidden), by_row(hidden),
            by_row(features), by_row(features), any_spec, any_spec, any_spec,
        ],
        scratch_shapes=[
            pltpu.VMEM((others, count, width), jnp.bfloat16),
            pltpu.VMEM((others, dp, share, width), jnp.bfloat16),
            pltpu.VMEM((width, features), jnp.bfloat16),
            pltpu.VMEM((features, hidden), jnp.bfloat16),
            pltpu.VMEM((features, hidden), jnp.bfloat16),
            pltpu.VMEM((hidden, features), jnp.bfloat16),
            pltpu.VMEM((count, features), jnp.bfloat16),
            pltpu.VMEM((count, 1), jnp.float32),
            pltpu.VMEM((count, hidden), jnp.bfloat16),
            pltpu.VMEM((rows, features), jnp.float32),
            pltpu.SemaphoreType.DMA((6,)),
            pltpu.SemaphoreType.DMA((groups, others)),
            pltpu.SemaphoreType.DMA((groups, others)),
            pltpu.SemaphoreType.DMA((2, dp - 1)),
            pltpu.SemaphoreType.DMA((2, dp - 1)),
            pltpu.SemaphoreType.DMA((3,)),
        ],
        compiler_params=pltpu.CompilerParams(
            collective_id=collective_id, has_side_effects=True, vmem_limit_bytes=VMEM_LIMIT
        ),
        cost_estimate=pl.CostEstimate(flops=flops, bytes_accessed=40 * count * features, transcendentals=0),
    )(attn, attn, part, w_own, w_gate, w_up, w_down, cotangent, live, tokens, gain, live)


class Scatter:
    def __init__(self, dp, product, store, sent, held, late, sems):
        self.product, self.store, self.sent, self.held, self.late = product, store, sent, held, late
        self.first_send, self.first_recv, self.late_send, self.late_recv = sems
        self.me = lax.axis_index("dp")
        self.upper = self.me // 2
        self.bits = dp.bit_length() - 1
        self.slots = dp // 2
        self.halves = row_halves(held.shape[1])

    def bit(self, place):
        return (self.me // 2**place) % 2

    def partner(self, place):
        return self.me + 2**place * (1 - 2 * self.bit(place))

    def first_copy(self, t):
        return pltpu.make_async_remote_copy(
            src_ref=self.sent.at[t],
            dst_ref=self.held.at[t],
            send_sem=self.first_send.at[t],
            recv_sem=self.first_recv.at[t],
            device_id={"dp": self.partner(0)},
            device_id_type=MESH,
        )

    def stage_bit(self, half, stage):
        return stage - 1 if half == 0 else self.bits - 1 - stage

    def slot_of(self, half, stage, index, value):
        if half == 0:
            low = 2 ** (stage - 1)
            return index * 2**stage + value * low + self.upper % low
        top = 2 ** (self.bits - stage)
        return index + value * (top // 2) + (self.upper // top) * top

    def late_copy(self, half, stage, index, slot):
        start, size = self.halves[half]
        buffer = self.slots - 2 ** (self.bits - stage) + index
        return pltpu.make_async_remote_copy(
            src_ref=self.held.at[slot, pl.ds(start, size)],
            dst_ref=self.late[half].at[buffer],
            send_sem=self.late_send.at[half, buffer],
            recv_sem=self.late_recv.at[half, buffer],
            device_id={"dp": self.partner(self.stage_bit(half, stage) + 1)},
            device_id_type=MESH,
        )

    def other_chunks(self):
        def step(t, carry):
            self.sent[t] = self.product(2 * t + 1 - self.bit(0)).astype(jnp.bfloat16)
            self.first_copy(t).start()
            return carry

        lax.fori_loop(0, self.slots, step, 0)

    def own_chunks(self):
        def step(e, carry):
            t = 0
            for place in range(self.bits - 1):
                t = t + 2**place * ((e // 2**place + 1 + self.upper // 2**place) % 2)
            own = self.product(2 * t + self.bit(0))
            self.first_copy(t).wait_recv()
            self.held[t] = (self.held[t].astype(jnp.float32) + own).astype(jnp.bfloat16)

            @pl.when(e % 2 == 0)
            def _():
                self.late_copy(0, 1, t // 2, t).start()

            @pl.when(e < self.slots // 2)
            def _():
                self.late_copy(1, 1, t % (self.slots // 2), t).start()

            return carry

        lax.fori_loop(0, self.slots, step, 0)

    def later(self, stage):
        for half in range(2):
            start, size = self.halves[half]
            keep_bit = self.bit(self.stage_bit(half, stage) + 1)
            for index in range(2 ** (self.bits - 1 - stage)):
                slot = self.slot_of(half, stage, index, keep_bit)
                self.late_copy(half, stage, index, slot).wait_recv()
                buffer = self.slots - 2 ** (self.bits - stage) + index
                total = self.held[slot, pl.ds(start, size)].astype(jnp.float32) + self.late[half][
                    buffer
                ].astype(jnp.float32)
                if stage == self.bits - 1:
                    self.store(start, size, total)
                else:
                    self.held[slot, pl.ds(start, size)] = total.astype(jnp.bfloat16)
            if stage < self.bits - 1:
                follow = self.stage_bit(half, stage + 1) + 1
                for index in range(2 ** (self.bits - 2 - stage)):
                    slot = self.slot_of(half, stage + 1, index, 1 - self.bit(follow))
                    self.late_copy(half, stage + 1, index, slot).start()

    def finish(self):
        for t in range(self.slots):
            self.first_copy(t).wait_send()
        for half in range(2):
            for stage in range(1, self.bits):
                for index in range(2 ** (self.bits - 1 - stage)):
                    self.late_copy(half, stage, index, 0).wait_send()


def scatter_scratch(dp, rows, columns):
    slots = dp // 2
    return (
        [pltpu.VMEM((slots, rows, columns), jnp.bfloat16)] * 2
        + [pltpu.VMEM((slots - 1, size, columns), jnp.bfloat16) for _, size in row_halves(rows)]
        + [pltpu.SemaphoreType.DMA((slots,))] * 2
        + [pltpu.SemaphoreType.DMA((2, slots - 1))] * 2
    )


def scatter_from(dp, product, store, refs):
    return Scatter(dp, product, store, refs[0], refs[1], refs[2:4], refs[4:8])


def product_scatter_kernel(count, dp, groups, *refs):
    lhs, rhs, pass_ref = refs[:count], refs[count : 2 * count], refs[2 * count]
    outs, pass_out = refs[2 * count + 1 : 3 * count + 1], refs[3 * count + 1]
    pass_sems, scratch = refs[3 * count + 2], refs[3 * count + 3 :]

    def pass_copy(step):
        return to_group(step, groups, pass_ref, pass_out.at[groups - 1 - step], pass_sems)

    def member(a):
        def product(chunk):
            return times(lhs[a][chunk], rhs[a][...])

        def store(start, size, total):
            outs[a][pl.ds(start, size)] = total

        return scatter_from(dp, product, store, scratch[8 * a : 8 * a + 8])

    members = [member(a) for a in range(count)]
    stages = dp.bit_length() - 1
    greet(dp, groups)
    for step in range(1, groups):
        pass_copy(step).start()
    pending = []
    for a in range(count):
        members[a].other_chunks()
        members[a].own_chunks()
        pending.append((a, 1))
        if a > 0:
            done, stage = pending.pop(0)
            members[done].later(stage)
            if stage < stages - 1:
                pending.append((done, stage + 1))
    while pending:
        done, stage = pending.pop(0)
        members[done].later(stage)
        if stage < stages - 1:
            pending.append((done, stage + 1))
    for one in members:
        one.finish()
    for step in range(1, groups):
        pass_copy(step).wait()


def product_scatter(pairs, passed, groups, collective_id):
    count = len(pairs)
    dp = pairs[0][0].shape[0]
    dims = [(lhs.shape[1], rhs.shape[1]) for lhs, rhs in pairs]
    flops = sum(2 * lhs.size * rhs.shape[1] for lhs, rhs in pairs)
    moved = sum(2 * (lhs.size + rhs.size) for lhs, rhs in pairs)
    vmem = pl.BlockSpec(memory_space=pltpu.VMEM)
    any_spec = pl.BlockSpec(memory_space=pl.ANY)
    return pl.pallas_call(
        functools.partial(product_scatter_kernel, count, dp, groups),
        out_shape=[jax.ShapeDtypeStruct(dim, jnp.float32) for dim in dims]
        + [jax.ShapeDtypeStruct((groups - 1,) + passed.shape, passed.dtype)],
        in_specs=[vmem] * (2 * count) + [any_spec],
        out_specs=[vmem] * count + [any_spec],
        scratch_shapes=[pltpu.SemaphoreType.DMA((2, groups - 1))]
        + sum([scatter_scratch(dp, *dim) for dim in dims], []),
        compiler_params=pltpu.CompilerParams(
            collective_id=collective_id, has_side_effects=True, vmem_limit_bytes=VMEM_LIMIT
        ),
        cost_estimate=pl.CostEstimate(flops=flops * 3, bytes_accessed=moved, transcendentals=0),
    )(*[lhs for lhs, _ in pairs], *[rhs for _, rhs in pairs], passed)


def norm_back(values, gain, grads):
    inverse = lax.rsqrt(jnp.mean(values * values, axis=1, keepdims=True) + EPS)
    scaled = gain * grads
    mean = jnp.mean(scaled * values, axis=1, keepdims=True)
    by_values = inverse * scaled - values * (inverse * inverse * inverse * mean)
    return by_values, jnp.sum(grads * values * inverse, axis=0, keepdims=True)


def attention_back_kernel(dp, groups, head_width, *refs):
    (
        back_ref, resid_hbm, cot_hbm, live_ref, tokens_hbm, attn_gain, mlp_gain,
        out_own, out_others, rows_ref, query_ref, key_ref, value_ref, logsum_ref, attn_ref,
        seg_column, seg_row, cosine_t, sine_t, cosine, sine_a, sine_b, qkv_own, pair_own, qkv_parts,
        tokens_out, gains_out, output_out, grad_out, qkv_all,
        cot_ref, tokens_ref, chunk_ref, weights, query_m, attn_m, key_t, query_t, key_sum, value_sum,
        attn_send, attn_grad, arrived, out_total, out_send, out_recv, branch_ref,
        load_sem, last_sem, attn_sems, grad_sems, out_sems, spread_send, spread_recv, *scatter_refs,
    ) = refs
    group, pack, others = lax.axis_index("kv"), lax.axis_index("dp"), groups - 1
    rows = branch_ref.shape[0]
    width = query_ref.shape[1]
    span_w = key_ref.shape[1]
    pair, half, heads = 2 * head_width, head_width // 2, span_w // head_width
    scale = head_width**-0.5
    mine = pl.ds(pl.multiple_of(group * rows, rows), rows)
    out_part = pl.ds(0, width)

    def load(index, source, target):
        return pltpu.make_async_copy(source, target, load_sem.at[index])

    first_loads = [
        load(0, resid_hbm, tokens_out),
        load(1, cot_hbm.at[mine], cot_ref),
        load(2, out_others, weights.at[:, :, out_part]),
        load(3, qkv_parts, qkv_all.at[:, pack]),
        load(4, tokens_hbm.at[mine], tokens_ref),
    ]
    for one in first_loads:
        one.start()

    def attn_copy(step):
        return to_group(step, groups, attn_send.at[step - 1], attn_grad.at[group], attn_sems)

    def grad_copy(step, block):
        return to_group(
            step, groups, grad_out.at[pl.ds(block * rows, rows)], arrived.at[step - 1], grad_sems
        )

    share = output_out.shape[0]

    def out_copy(step):
        return to_group(
            step, groups, out_send.at[pl.ds(step * share, share)], out_recv.at[step - 1], out_sems
        )

    greet(dp, groups)
    spread = Spread(qkv_all, spread_send, spread_recv, dp)
    lanes = lax.broadcasted_iota(jnp.int32, (rows, span_w), 1) // head_width
    first_loads[3].wait()
    spread.start(0)
    first_loads[0].wait()
    first_loads[1].wait()
    values = tokens_out[...]
    grad_resid, mlp_rows = norm_back(values, mlp_gain[...], back_ref[...].astype(jnp.float32))
    grad_resid = grad_resid + cot_ref[...].astype(jnp.float32) * live_ref[mine]
    tokens_out[...] = grad_resid
    branch_ref[...] = grad_resid.astype(jnp.bfloat16)
    first_loads[2].wait()
    for step in range(1, groups):
        attn_send[step - 1] = times(branch_ref[...], weights[step - 1, :, out_part]).astype(
            jnp.bfloat16
        )
        attn_copy(step).start()
    attn_grad[group] = times_t(branch_ref[...], out_own[...]).astype(jnp.bfloat16)

    def store(start, size, total):
        if start == 0:
            out_total[...] = total[:share]
        out_send[pl.ds(start, size)] = total.astype(jnp.bfloat16)

    scatter = scatter_from(dp, lambda chunk: times(chunk_ref[chunk], branch_ref[...]), store, scatter_refs)
    for place in range(groups):
        turned = (attn_ref[mine] if place == 0 else rows_ref[place - 1]).T
        chunk_ref[:, pl.ds(place * share, share)] = turned.reshape(dp, share, rows)
    scatter.other_chunks()
    scatter.own_chunks()
    for block in range(groups):
        part = pl.ds(block * rows, rows)
        key_t[:, part] = key_ref[part, pl.ds(0, pair)].T[:head_width]
    key_sum[...] = jnp.zeros_like(key_sum)
    value_sum[...] = jnp.zeros_like(value_sum)

    def attend(block):
        part = pl.ds(block * rows, rows)

        @pl.when(block != group)
        def _():
            step = (group - block + groups) % groups
            to_group(step, groups, attn_grad.at[block], attn_grad.at[block], attn_sems).wait_recv()

        query_seg = seg_row[:, part]
        query_place = lax.broadcasted_iota(jnp.int32, (rows, rows), 1) + block * rows

        def wide(entries):
            return jnp.concatenate([entries] * heads, axis=1)

        def span(number, carry):
            columns = pl.ds(pl.multiple_of(number * span_w, span_w), span_w)
            query = query_ref[part, columns]
            grad = attn_grad[block, :, columns]
            weighed = (grad.astype(jnp.float32) * attn_ref[part, columns].astype(jnp.float32)).T
            centres = jnp.sum(weighed.reshape(heads, head_width, rows), axis=1)
            centre = jnp.concatenate([centres[head : head + 1] for head in range(heads)], axis=1)
            logsum = logsum_ref[number * groups + block]
            for head in range(heads):
                place = pl.ds(head * rows, rows)
                query_m[place] = jnp.where(lanes == head, query, 0)
                attn_m[place] = jnp.where(lanes == head, grad, 0)
            query_t[...] = jnp.zeros_like(query_t)

            def keys(piece, carry):
                key_part = pl.ds(pl.multiple_of(piece * rows, rows), rows)
                key_place = lax.broadcasted_iota(jnp.int32, (rows, rows), 0) + piece * rows
                allowed = (seg_column[key_part] == query_seg) & (key_place <= query_place)
                bias = jnp.where(allowed, 0.0, -jnp.inf)
                scores = times_t(key_ref[key_part], query_m[...]) * (scale * LOG2E)
                chance = jnp.exp2(scores - logsum + wide(bias))
                probs = times_t(value_ref[key_part], attn_m[...])
                slope = (chance * (probs - centre)).astype(jnp.bfloat16)
                value_sum[key_part] += times(chance.astype(jnp.bfloat16), attn_m[...])
                key_sum[key_part] += times(slope, query_m[...])
                query_t[...] += times(key_t[:, key_part], slope)
                return carry

            lax.fori_loop(0, block + 1, keys, 0)
            cos, sin = wide(cosine_t[:, part]), wide(sine_t[:, part])
            low, high = query_t[:half] * scale, query_t[half:] * scale
            turned = jnp.concatenate([low * cos + high * sin, high * cos - low * sin], axis=0)
            stacked = jnp.concatenate(
                [turned[:, head * rows : (head + 1) * rows] for head in range(heads)], axis=0
            )
            grad_out[part, columns] = stacked.T.astype(jnp.bfloat16)
            return carry

        lax.fori_loop(0, width // span_w, span, 0)

        def folded(total):
            sums = total[part, pl.ds(0, pair)]
            for step in range(1, span_w // pair):
                sums = sums + total[part, pl.ds(step * pair, pair)]
            return sums + pltpu.roll(sums, head_width, 1)

        grad_k = folded(key_sum) * scale
        grad_k = (
            grad_k * cosine[part]
            - pltpu.roll(grad_k, pair - half, 1) * sine_a[part]
            - pltpu.roll(grad_k, half, 1) * sine_b[part]
        )
        first = lax.broadcasted_iota(jnp.int32, (rows, pair), 1) < head_width
        grad_out[part, pl.ds(width, pair)] = jnp.where(first, grad_k, folded(value_sum)).astype(
            jnp.bfloat16
        )

        @pl.when(block != group)
        def _():
            grad_copy((block - group + groups) % groups, block).start()

    stages = dp.bit_length() - 1
    for block in reversed(range(groups)):
        attend(block)
        if block == groups - 1:
            for stage in range(1, stages - 1):
                scatter.later(stage)
            for stage in range(stages - 1):
                spread.wait_recv(stage)
                if stage < stages - 2:
                    spread.start(stage + 1)
        if block == groups - 2:
            scatter.later(stages - 1)
            spread.start(stages - 1)
            for step in range(1, groups):
                out_copy(step).start()

    spread.wait_recv(stages - 1)
    part_rows = qkv_all.shape[2]
    last_loads = [
        pltpu.make_async_copy(
            qkv_all.at[:, place], weights.at[:, pl.ds(place * part_rows, part_rows)], last_sem.at[place]
        )
        for place in range(dp)
    ]
    for one in last_loads:
        one.start()
    total = out_total[...]
    for step in range(1, groups):
        out_copy(step).wait_recv()
        total = total + out_recv[step - 1].astype(jnp.float32)
    output_out[...] = total
    grad_act = times_t(grad_out[mine, out_part], qkv_own[...])
    grad_act = grad_act + times_t(grad_out[mine, pl.ds(width, pair)], pair_own[...])
    for one in last_loads:
        one.wait()
    for step in range(1, groups):
        to_group(step, groups, arrived.at[step - 1], arrived.at[step - 1], grad_sems).wait_recv()
        grad_act = grad_act + times_t(arrived[step - 1], weights[others - step])
    first_loads[4].wait()
    by_tokens, attn_rows = norm_back(tokens_ref[...].astype(jnp.float32), attn_gain[...], grad_act)
    tokens_out[...] += by_tokens
    columns = gains_out.shape[2]
    for place in range(dp):
        span = slice(place * columns, (place + 1) * columns)
        gains_out[place, 0:1] = mlp_rows[:, span]
        gains_out[place, 1:2] = attn_rows[:, span]
    for step in range(1, groups):
        attn_copy(step).wait_send()
        grad_copy(step, 0).wait_send()
        out_copy(step).wait_send()
    spread.wait_send()
    scatter.finish()


def attention_back(operands, sizes, head_width, collective_id):
    dp, groups = sizes
    others_w, rows_others, query, key, parts = (operands[index] for index in (8, 9, 10, 11, 24))
    rows, width = rows_others.shape[1:]
    features = others_w.shape[1]
    count, span_w = key.shape
    share = width // dp
    stacked = (span_w // head_width) * rows
    columns = width + 2 * head_width
    vmem = pl.BlockSpec(memory_space=pltpu.VMEM)
    any_spec = pl.BlockSpec(memory_space=pl.ANY)
    bf16, f32 = jnp.bfloat16, jnp.float32
    flops = 2 * count * count * width * 10
    return pl.pallas_call(
        functools.partial(attention_back_kernel, dp, groups, head_width),
        out_shape=[
            jax.ShapeDtypeStruct((rows, features), f32),
            jax.ShapeDtypeStruct((dp, 2, features // dp), f32),
            jax.ShapeDtypeStruct((share, features), f32),
            jax.ShapeDtypeStruct((count, columns), bf16),
            jax.ShapeDtypeStruct((groups - 1, dp) + parts.shape[1:], bf16),
        ],
        in_specs=[any_spec if index in (1, 2, 4, 8, 24) else vmem for index in range(25)],
        out_specs=[vmem] * 4 + [any_spec],
        scratch_shapes=[
            pltpu.VMEM((rows, features), bf16),
            pltpu.VMEM((rows, features), bf16),
            pltpu.VMEM((dp, groups * share, rows), bf16),
            pltpu.VMEM((groups - 1, features, columns), bf16),
            pltpu.VMEM((stacked, span_w), bf16),
            pltpu.VMEM((stacked, span_w), bf16),
            pltpu.VMEM((head_width, count), bf16),
            pltpu.VMEM((head_width, stacked), f32),
            pltpu.VMEM((count, span_w), f32),
            pltpu.VMEM((count, span_w), f32),
            pltpu.VMEM((groups - 1, rows, width), bf16),
            pltpu.VMEM((groups, rows, width), bf16),
            pltpu.VMEM((groups - 1, rows, columns), bf16),
            pltpu.VMEM((share, features), f32),
            pltpu.VMEM((groups * share, features), bf16),
            pltpu.VMEM((groups - 1, share, features), bf16),
            pltpu.VMEM((rows, features), bf16),
            pltpu.SemaphoreType.DMA((5,)),
            pltpu.SemaphoreType.DMA((dp,)),
            pltpu.SemaphoreType.DMA((2, groups - 1)),
            pltpu.SemaphoreType.DMA((2, groups - 1)),
            pltpu.SemaphoreType.DMA((2, groups - 1)),
            pltpu.SemaphoreType.DMA((2, dp - 1)),
            pltpu.SemaphoreType.DMA((2, dp - 1)),
        ]
        + scatter_scratch(dp, groups * share, features),
        compiler_params=pltpu.CompilerParams(
            collective_id=collective_id, has_side_effects=True, vmem_limit_bytes=VMEM_LIMIT
        ),
        cost_estimate=pl.CostEstimate(flops=flops, bytes_accessed=40 * 2**20, transcendentals=0),
    )(*operands)


def last_sums_kernel(dp, groups, lhs_ref, rhs_ref, gains_ref, query_out, key_out, value_out, gains_out, near, far, total, near_sems, far_sems, *scatter_refs):
    pack, group = lax.axis_index("dp"), lax.axis_index("kv")

    def store(start, size, value):
        span, width, head_width = pl.ds(start, size), query_out.shape[1], key_out.shape[1]
        query_out[span] = value[:, :width]
        key_out[span] = value[:, width : width + head_width]
        value_out[span] = value[:, width + head_width :]

    scatter = scatter_from(dp, lambda chunk: times(lhs_ref[chunk], rhs_ref[...]), store, scatter_refs)

    def near_copy(step):
        return pltpu.make_async_remote_copy(
            src_ref=gains_ref,
            dst_ref=near.at[step - 1],
            send_sem=near_sems.at[0, step - 1],
            recv_sem=near_sems.at[1, step - 1],
            device_id={"kv": (group + step) % groups},
            device_id_type=MESH,
        )

    def far_copy(step):
        other = (pack + step) % dp
        return pltpu.make_async_remote_copy(
            src_ref=total.at[other],
            dst_ref=far.at[step - 1],
            send_sem=far_sems.at[0, step - 1],
            recv_sem=far_sems.at[1, step - 1],
            device_id={"dp": other},
            device_id_type=MESH,
        )

    barrier = pltpu.get_barrier_semaphore()
    for step in range(1, dp):
        pl.semaphore_signal(
            barrier, inc=1, device_id={"dp": (pack + step) % dp}, device_id_type=MESH
        )
    for step in range(1, groups):
        pl.semaphore_signal(
            barrier, inc=1, device_id={"kv": (group + step) % groups}, device_id_type=MESH
        )
    pl.semaphore_wait(barrier, dp + groups - 2)
    for step in range(1, groups):
        near_copy(step).start()
    scatter.other_chunks()
    value = gains_ref[...]
    for step in range(1, groups):
        near_copy(step).wait_recv()
        value = value + near[step - 1]
    total[...] = value
    for step in range(1, dp):
        far_copy(step).start()
    scatter.own_chunks()
    for stage in range(1, dp.bit_length() - 1):
        scatter.later(stage)
    value = total[pack]
    for step in range(1, dp):
        far_copy(step).wait_recv()
        value = value + far[step - 1]
    gains_out[...] = value
    for step in range(1, groups):
        near_copy(step).wait_send()
    for step in range(1, dp):
        far_copy(step).wait_send()
    scatter.finish()


def last_sums(lhs, rhs, gains, head_width, groups, collective_id):
    dp, rows = lhs.shape[0], lhs.shape[1]
    columns = rhs.shape[1]
    vmem = pl.BlockSpec(memory_space=pltpu.VMEM)
    return pl.pallas_call(
        functools.partial(last_sums_kernel, dp, groups),
        out_shape=[
            jax.ShapeDtypeStruct((rows, columns - 2 * head_width), jnp.float32),
            jax.ShapeDtypeStruct((rows, head_width), jnp.float32),
            jax.ShapeDtypeStruct((rows, head_width), jnp.float32),
            jax.ShapeDtypeStruct(gains.shape[1:], jnp.float32),
        ],
        in_specs=[vmem] * 3,
        out_specs=[vmem] * 4,
        scratch_shapes=[
            pltpu.VMEM((groups - 1,) + gains.shape, jnp.float32),
            pltpu.VMEM((dp - 1,) + gains.shape[1:], jnp.float32),
            pltpu.VMEM(gains.shape, jnp.float32),
            pltpu.SemaphoreType.DMA((2, groups - 1)),
            pltpu.SemaphoreType.DMA((2, dp - 1)),
        ]
        + scatter_scratch(dp, rows, columns),
        compiler_params=pltpu.CompilerParams(
            collective_id=collective_id, has_side_effects=True, vmem_limit_bytes=VMEM_LIMIT
        ),
        cost_estimate=pl.CostEstimate(
            flops=2 * lhs.size * columns, bytes_accessed=2 * lhs.size, transcendentals=0
        ),
    )(lhs, rhs, gains)


def row_chunks(matrix, count):
    chunks = matrix.reshape(count, matrix.shape[0] // count, matrix.shape[1])
    return jnp.pad(chunks, ((0, 0), (0, -chunks.shape[1] % 16), (0, 0)))


def per_device(
    tokens_in,
    attn_gain,
    w_query,
    w_key,
    w_value,
    w_output,
    mlp_gain,
    w_gate,
    w_up,
    w_down,
    counts,
    segments,
    cotangent,
):
    row_count = tokens_in.shape[0]
    head_width = w_key.shape[1]
    pack_count, group_count = lax.axis_size("dp"), lax.axis_size("kv")
    sizes = (pack_count, group_count)
    pack = lax.axis_index("dp")
    share = w_query.shape[0] // pack_count
    w_pair = jnp.concatenate([w_key, w_value], axis=1)

    def own_share(matrix):
        return lax.dynamic_slice_in_dim(matrix, pack * share, share, 0)

    out_part = lax.dynamic_slice_in_dim(w_output[0], pack * share, share, 1).T
    qkv_part = jnp.concatenate([own_share(w_query), own_share(w_pair)], axis=1)
    live_rows = (jnp.arange(row_count) < counts[0]).astype(jnp.float32)[:, None]
    (
        attn_out,
        act_flipped,
        query,
        key,
        value,
        logsums,
        cosine,
        sine_a,
        sine_b,
        cosine_t,
        sine_t,
        out_parts,
    ) = attention(tokens_in, attn_gain[None], w_query, w_pair, segments, out_part, group_count, 5)
    (
        second_flipped,
        hidden_flipped,
        grad_gate,
        grad_up,
        grad_act_two,
        feed_part,
        resid_mine,
        attn_others,
        out_others,
    ) = feed_forward(
        attn_out,
        out_parts,
        w_output[0],
        w_gate,
        w_up,
        w_down[0],
        cotangent,
        live_rows,
        tokens_in,
        mlp_gain[None],
        sizes,
        1,
    )
    second_chunks = row_chunks(second_flipped, pack_count)
    sent_gate, sent_up, sent_down, qkv_parts = product_scatter(
        [
            (second_chunks, grad_gate),
            (second_chunks, grad_up),
            (row_chunks(hidden_flipped, pack_count), cotangent),
        ],
        qkv_part,
        group_count,
        2,
    )
    grad_two_mine = lax.psum_scatter(grad_act_two, "kv", scatter_dimension=0, tiled=True)
    grad_two_mine, feed_part, qkv_parts = lax.optimization_barrier(
        (grad_two_mine, feed_part, qkv_parts)
    )
    grad_tokens, gain_rows, sent_output, grad_qkv, _ = attention_back(
        (
            grad_two_mine,
            resid_mine,
            cotangent,
            live_rows,
            tokens_in,
            attn_gain[None],
            mlp_gain[None],
            w_output[0],
            out_others.reshape(group_count - 1, -1, w_output.shape[1]),
            attn_others,
            query,
            key,
            value,
            logsums,
            attn_out,
            segments[:, None],
            segments[None],
            cosine_t,
            sine_t,
            cosine,
            sine_a,
            sine_b,
            w_query,
            w_pair,
            qkv_parts,
        ),
        sizes,
        head_width,
        3,
    )
    sent_query, sent_key, sent_value, gains = last_sums(
        row_chunks(act_flipped, pack_count), grad_qkv, gain_rows, head_width, group_count, 4
    )
    sent_two, sent_one = gains[0], gains[1]
    sent_output = sent_output[None]
    sent_down = sent_down[: w_down.shape[1] // pack_count][None]
    layer_out = (
        resid_mine
        + lax.psum_scatter(feed_part, "kv", scatter_dimension=0, tiled=True).astype(jnp.float32)
    ).astype(jnp.bfloat16)
    return (
        layer_out,
        grad_tokens,
        sent_one,
        sent_query,
        sent_key,
        sent_value,
        sent_output,
        sent_two,
        sent_gate,
        sent_up,
        sent_down,
    )


def solution(mesh):
    return jax.shard_map(
        per_device,
        mesh=mesh,
        in_specs=(
            P("dp", None),
            P(),
            P(None, "kv"),
            P(None, "kv"),
            P(None, "kv"),
            P("kv", None, None),
            P(),
            P(None, "kv"),
            P(None, "kv"),
            P("kv", None, None),
            P("dp"),
            P("dp"),
            P("dp", None),
        ),
        out_specs=(
            P(("dp", "kv"), None),
            P(("dp", "kv"), None),
            P("dp"),
            P("dp", "kv"),
            P("dp", "kv"),
            P("dp", "kv"),
            P("kv", "dp", None),
            P("dp"),
            P("dp", "kv"),
            P("dp", "kv"),
            P("kv", "dp", None),
        ),
        check_vma=False,
    )
```

time: 720 us -> 490 us (0.68); the launches traced: 706 us -> 484 us
  Pallas kernels: 214 us -> 434 us
  waiting for transfers between devices: 192 us -> 12.2 us
  matrix products: 98.4 us -> 0 us
  other arithmetic: 77.5 us -> 5.43 us
  blocking collectives: 71.3 us -> 0 us
  local copies, waits for them, and re-layouts: 30.9 us -> 17.5 us
    pallas_call x1 -> x4, Pallas kernels: 89 us -> 322 us  [the longest x1 168 us: attention_back(): pl.pallas_call(functools.partial(attention_back_kernel, dp, groups, head_...]
    dot_general x21 -> x0, matrix products: 98.4 us -> none  [the longest x2 16.5 us: per_device(): jnp.einsum('qhd,kd->hqk', grad_attn[begin_row:end_row], value_b[:end_row]...]
    reduce_scatter x1, waiting for transfers between devices: 66.9 us -> 0.01 us  [per_device(): lax.psum_scatter(feed_part, 'kv', scatter_dimension=0, tiled=True)]
    all_gather x3 -> x0, waiting for transfers between devices: 64 us -> none  [the longest x1 64 us: per_device(): lax.all_gather(gather_share(w_qkv_part), 'dp', axis=1, tiled=True)]
    reduce_scatter x5 -> x0, waiting for transfers between devices: 60.1 us -> none  [the longest x1 35.8 us: per_device(): lax.psum_scatter(grad_wvalue.astype(jnp.bfloat16), 'dp', scatter_dimensio...]
    all_to_all x1 -> x0, blocking collectives: 38.2 us -> none  [per_device(): lax.all_to_all(by_group(grad_attn_ring), 'kv', 0, 0, tiled=True)]
    convert_element_type x15 -> x2, other arithmetic: 35.1 us -> 3.48 us  [the longest x1 2.63 us: per_device(): layer_out = (resid_mine + lax.psum_scatter(feed_part, 'kv', scatter_dimen...]
    unnamed x1 -> x0, blocking collectives: 23.7 us -> none
  transfers between devices with their start and end apart: 11 -> 2, of which waited for: 5 -> 1; matrix products, arithmetic and copies ran while one was open for 27% -> 1% of each run, Pallas kernels for 13% -> 60%
where the time goes in v4:
time: 490 us; the launch traced here: 484 us
  Pallas kernels  434 us (89%)
  local copies, waits for them, and re-layouts  17.5 us (4%)
  between operations  15 us (3%)
  waiting for transfers between devices  12.2 us (2%)
  other arithmetic  5.43 us (1%)
    pallas_call x1, Pallas kernels, attention_back(): pl.pallas_call(functools.partial(attention_back_kernel, dp, groups, head_...  168 us
    pallas_call x1, Pallas kernels, feed_forward(): pl.pallas_call(functools.partial(feed_forward_kernel, dp, groups), grid=(...  112 us
    pallas_call x1, Pallas kernels, product_scatter(): pl.pallas_call(functools.partial(product_scatter_kernel, count, dp, group...  91.2 us
    pallas_call x1, Pallas kernels, attention(): pl.pallas_call(functools.partial(attention_kernel, groups, head_width), o...  33.1 us
    pallas_call x1, Pallas kernels, last_sums(): pl.pallas_call(functools.partial(last_sums_kernel, dp, groups), out_shape...  30.5 us
    reduce_scatter x1, waiting for transfers between devices, per_device(): lax.psum_scatter(grad_act_two, 'kv', scatter_dimension=0, tiled=True)  12.2 us
    unnamed x28, local copies, waits for them, and re-layouts  11.8 us
  transfers between devices with their start and end apart: 2, of which 1 were waited for; matrix products, arithmetic and copies ran while one was open for 1% of the time, Pallas kernels for 60%

profile of v4, /device:TPU:8, one launch (start us, length us, event | category | flops | bytes accessed | tf_op | source)
XLA Modules:
  0.0 484.3 jit_solution(4286378265855814621)
XLA Ops:
  7.2 0.0 reduce-scatter.3.cloned.1.call-start
  7.9 0.6 broadcast_in_dim_tile.3.refs_6_
  8.5 1.0 constant_dynamic-slice_fusion.1
  9.5 0.8 copy.31
  10.3 0.8 fusion.refs_8_.refs_11_.refs_3_
  11.2 1.2 copy.29
  12.4 0.3 copy.30
  12.7 1.0 copy.32.refs_4_.refs_15_
  13.7 1.1 pad_maximum_fusion.refs_3_.refs_23_
  14.8 33.1 %shard_map.212 = (bf16[1024,512]{1,0:T(8,128)(2,1)}, bf16[2048,1024]{1,0:T(8,128)(2,1)}, bf16[1024,512]{1,0:T(8,128)(2,1)}, bf16[1024,256]{1,0:T(8,128)(2,1)}, b...) custom-call(bf16[1024,2048]{1,0:T(8,128)(2,1)} %refs_4_.3, ...), custom_call_target="tpu_custom_call" | custom-call | flops 4294967296 | bytes 16777216 | tf_op jit(solution)/shard_map/pallas_call | solution.py:218
  47.9 111.8 %shard_map.213 = (bf16[2048,1024]{1,0:T(8,128)(2,1)}, bf16[1408,1024]{1,0:T(8,128)(2,1)}, bf16[1024,1408]{1,0:T(8,128)(2,1)}, bf16[1024,1408]{1,0:T(8,128)(2,1)}...) custom-call(bf16[1024,512]{1,0:T(8,128)(2,1)} %get-tuple-element.47., ...), custom_call_target="tpu_custom_call" | custom-call | flops 44023414784 | bytes 83886080 | tf_op jit(solution)/shard_map/pallas_call | solution.py:425
  159.7 0.0 reduce-scatter.3.cloned.1.call-update
  159.7 0.0 reduce-scatter.5.cloned.1.call-start
  159.7 0.1 fusion.1
  159.8 1.0 constant_dynamic-slice_fusion
  160.8 0.8 pad_maximum_fusion.1.refs_6_
  161.6 91.2 %shard_map.214 = (f32[256,1408]{1,0:T(8,128)}, f32[256,1408]{1,0:T(8,128)}, f32[176,2048]{1,0:T(8,128)}, bf16[3,256,640]{2,1,0:T(8,128)(2,1)}) custom-call(bf16[8,256,1024]{2,1,0:T(8,128)(2,1)} %bitcast.36, bf16[8,256,1024]{2,1,0:T(8,128)(2,1)} %bitcast.37, bf16[8,176,1024]{2,1,0:T(8,128)(2,1)} %bitcast.38, bf16[1024,1408]{1,0:T(8,128)(2,1)} %get-tuple-element.54.refs_3_, ...), custom_call_target="tpu_custom_call" | custom-call | flops 53150220288 | bytes 21233664 | tf_op jit(solution)/shard_map/pallas_call | solution.py:649
  252.8 12.2 %reduce-scatter.3.cloned.1.call-done.refs_0_ = bf16[256,2048]{1,0:T(8,128)(2,1)} async-done(((bf16[1024,2048]{1,0:T(8,128)(2,1)}), bf16[256,2048]{1,0:T(8,128)(2,1)}) %reduce-scatter.3.cloned.1.call-update) | async-done | bytes 1048592 | tf_op jit(solution)/shard_map/reduce_scatter | solution.py:1124
  265.0 167.6 %shard_map.215 = (f32[256,2048]{1,0:T(8,128)}, f32[8,2,256]{2,1,0:T(2,128)}, f32[64,2048]{1,0:T(8,128)}, bf16[1024,640]{1,0:T(8,128)(2,1)}, bf16[3,8,256,640]{3,2,1,0:T(8,128)(2,1)}) custom-call(bf16[256,2048]{1,0:T(8,128)(2,1)} %reduce-scatter.3.cloned.1.call-done.refs_0_, f32[256,2048]{1,0:T(8,128)} %get-tuple-element.49.refs_1_, ...), custom_call_target="tpu_custom_call" | custom-call | flops 10737418240 | bytes 41943040 | tf_op jit(solution)/shard_map/pallas_call | solution.py:898
  432.6 30.5 %shard_map.216 = (f32[256,512]{1,0:T(8,128)}, f32[256,64]{1,0:T(8,128)}, f32[256,64]{1,0:T(8,128)}, f32[2,256]{1,0:T(2,128)}) custom-call(bf16[8,256,1024]{2,1,0:T(8,128)(2,1)} %bitcast.35, bf16[1024,640]{1,0:T(8,128)(2,1)} %get-tuple-element.73.rhs_ref, f32[8,2,256]{2,1,0:T(2,128)} %get-tuple-element.74.gains_ref), custom_call_target="tpu_custom_call" | custom-call | flops 2684354560 | bytes 4194304 | tf_op jit(solution)/shard_map/pallas_call | solution.py:1014
  463.1 1.6 copy.34
  464.7 1.6 copy.35
  466.3 1.3 fusion.2
  467.6 2.6 add_convert_fusion
  470.3 1.3 copy.43
  471.6 0.1 copy-done.6
  471.6 0.8 copy.44
  472.4 0.8 copy.45
  473.2 1.1 copy.46
  474.3 1.1 copy.47
  475.4 0.8 copy-done.2
  476.2 1.1 copy.48
  (20 shorter events, 0.1 us)
Async XLA Ops:
  7.2 5.2 %copy-start.7 = (bf16[2048,64]{0,1:T(8,128)(2,1)S(1)}, bf16[2048,64]{0,1:T(8,128)(2,1)}, u32[]{:S(2)}) copy-start(bf16[2048,64]{0,1:T(8,128)(2,1)} %param.17) | copy-start | bytes 786436
  7.2 5.5 %copy-start.8 = (s32[1024]{0:T(1024)S(1)}, s32[1024]{0:T(1024)}, u32[]{:S(2)}) copy-start(s32[1024]{0:T(1024)} %param.24) | copy-start | bytes 12292
  7.2 257.7 %reduce-scatter.3.cloned.1.call-start = ((), (), s32[]{:S(2)}) async-start(), calls=%async_computation.2 | async-start | bytes 5242880 | tf_op jit(solution)/shard_map/reduce_scatter | solution.py:1124
  159.7 307.9 %reduce-scatter.5.cloned.1.call-start = ((), (), s32[]{:S(2)}) async-start(), calls=%async_computation.3 | async-start | bytes 5242880 | tf_op jit(solution)/shard_map/reduce_scatter | solution.py:1168
  432.6 35.1 %copy-start = (f32[256,2048]{1,0:T(8,128)S(1)}, f32[256,2048]{1,0:T(8,128)}, u32[]{:S(2)}) copy-start(f32[256,2048]{1,0:T(8,128)} %get-tuple-element.49.refs_1_) | copy-start | bytes 6291460
  467.6 2.6 copy-start.1
  470.3 1.4 copy-start.6
  470.3 2.2 copy-start.5
  471.6 1.6 copy-start.4
  472.4 1.9 copy-start.3
  474.3 1.9 copy-start.2
Sparse Core Ops, SparseCore 0:
  159.8 105.0 reduce-scatter.2
  267.3 115.8 reduce-scatter.4

commit v5 on v4

--- a/solution.py
+++ b/solution.py
@@ -44,9 +44,8 @@
         self.buffer, self.send_sem, self.recv_sem = buffer, send_sem, recv_sem
         self.me = lax.axis_index("dp")
         self.bits = dp.bit_length() - 1
-        columns = buffer.shape[3]
-        split = -(-columns // 256) * 128
-        self.columns = ((0, split), (split, columns - split))
+        rows = buffer.shape[2]
+        self.halves = row_halves(rows)
 
     def flipped(self, places):
         device = self.me
@@ -63,7 +62,7 @@
                 places = [order[b] for b in range(stage) if subset >> b & 1]
                 if arriving:
                     places = places + [order[stage]]
-                part = self.buffer.at[:, self.flipped(places), :, pl.ds(*self.columns[half])]
+                part = self.buffer.at[:, self.flipped(places), pl.ds(*self.halves[half])]
                 number = 2**stage - 1 + subset
                 result.append(
                     pltpu.make_async_remote_copy(
@@ -260,7 +259,7 @@
     (
         attn_hbm, attn_ref, part_ref, own_hbm, gate_hbm, up_hbm, down_hbm, cot_hbm, live_hbm,
         tokens_ref, gain_ref, live_ref,
-        act_out, hidden_out, gate_out, up_out, back_out, feed_out, resid_out, rows_out, all_out,
+        act_out, hidden_out, gate_out, up_out, back_out, feed_a_out, feed_b_out, resid_out, rows_out, all_out,
         attn_in, all_ref, own_ref, w_gate, w_up, w_down, cot_ref, live_all, grad_hidden, resid_ref,
         load_sem, send_sem, recv_sem, spread_send, spread_recv, out_sem,
     ) = refs
@@ -375,7 +374,9 @@
     chance = jax.nn.sigmoid(gate)
     swish = gate * chance
     hidden = swish * up
-    feed_out[...] = times(hidden.astype(jnp.bfloat16), w_down[...]).astype(jnp.bfloat16)
+    feed = times(hidden.astype(jnp.bfloat16), w_down[...]).astype(jnp.bfloat16)
+    feed_a_out[...] = feed[:, : feed_a_out.shape[1]]
+    feed_b_out[...] = feed[:, feed_a_out.shape[1] :]
     hidden_out[...] = (hidden * live_ref[...]).astype(jnp.bfloat16).T
     grad = grad_hidden[span].astype(jnp.float32)
     gate_b = (grad * up * chance * (1.0 + gate * (1.0 - chance))).astype(jnp.bfloat16)
@@ -418,6 +419,7 @@
     width, hidden = w_own.shape[0], w_gate.shape[1]
     share = part.shape[1]
     others = groups - 1
+    early = features // 2
     any_spec = pl.BlockSpec(memory_space=pl.ANY)
     by_row = lambda columns: pl.BlockSpec((rows, columns), lambda i: (i, 0))
     by_column = lambda height: pl.BlockSpec((height, rows), lambda i: (0, i))
@@ -431,7 +433,8 @@
             jax.ShapeDtypeStruct((count, hidden), jnp.bfloat16),
             jax.ShapeDtypeStruct((count, hidden), jnp.bfloat16),
             jax.ShapeDtypeStruct((count, features), jnp.bfloat16),
-            jax.ShapeDtypeStruct((count, features), jnp.bfloat16),
+            jax.ShapeDtypeStruct((count, early), jnp.bfloat16),
+            jax.ShapeDtypeStruct((count, features - early), jnp.bfloat16),
             jax.ShapeDtypeStruct((rows, features), jnp.float32),
             jax.ShapeDtypeStruct((others, rows, width), jnp.bfloat16),
             jax.ShapeDtypeStruct((others, dp, share, width), jnp.bfloat16),
@@ -447,7 +450,7 @@
         ],
         out_specs=[
             by_column(features), by_column(hidden), by_row(hidden), by_row(hidden),
-            by_row(features), by_row(features), any_spec, any_spec, any_spec,
+            by_row(features), by_row(early), by_row(features - early), any_spec, any_spec, any_spec,
         ],
         scratch_shapes=[
             pltpu.VMEM((others, count, width), jnp.bfloat16),
@@ -674,10 +677,10 @@
         back_ref, resid_hbm, cot_hbm, live_ref, tokens_hbm, attn_gain, mlp_gain,
         out_own, out_others, rows_ref, query_ref, key_ref, value_ref, logsum_ref, attn_ref,
         seg_column, seg_row, cosine_t, sine_t, cosine, sine_a, sine_b, qkv_own, pair_own, qkv_parts,
-        tokens_out, gains_out, output_out, grad_out, qkv_all,
+        tokens_out, gains_out, output_out, out_send, grad_out, qkv_all,
         cot_ref, tokens_ref, chunk_ref, weights, query_m, attn_m, key_t, query_t, key_sum, value_sum,
-        attn_send, attn_grad, arrived, out_total, out_send, out_recv, branch_ref,
-        load_sem, last_sem, attn_sems, grad_sems, out_sems, spread_send, spread_recv, *scatter_refs,
+        attn_send, attn_grad, arrived, branch_ref,
+        load_sem, last_sem, attn_sems, grad_sems, spread_send, spread_recv, *scatter_refs,
     ) = refs
     group, pack, others = lax.axis_index("kv"), lax.axis_index("dp"), groups - 1
     rows = branch_ref.shape[0]
@@ -701,20 +704,28 @@
     for one in first_loads:
         one.start()
 
-    def attn_copy(step):
-        return to_group(step, groups, attn_send.at[step - 1], attn_grad.at[group], attn_sems)
-
-    def grad_copy(step, block):
+    spans = width // span_w
+
+    def attn_copy(number, step):
         return to_group(
-            step, groups, grad_out.at[pl.ds(block * rows, rows)], arrived.at[step - 1], grad_sems
+            step, groups, attn_send.at[number, step - 1], attn_grad.at[number, group], attn_sems.at[number]
         )
 
+    def columns_of(number):
+        start = number * span_w
+        return pl.ds(start, span_w if number < spans - 1 else width + pair - start)
+
+    def grad_copy(number, step, block):
+        columns = columns_of(number)
+        return to_group(
+            step,
+            groups,
+            grad_out.at[pl.ds(block * rows, rows), columns],
+            arrived.at[step - 1, :, columns],
+            grad_sems.at[number],
+        )
+
     share = output_out.shape[0]
-
-    def out_copy(step):
-        return to_group(
-            step, groups, out_send.at[pl.ds(step * share, share)], out_recv.at[step - 1], out_sems
-        )
 
     greet(dp, groups)
     spread = Spread(qkv_all, spread_send, spread_recv, dp)
@@ -728,17 +739,23 @@
     grad_resid = grad_resid + cot_ref[...].astype(jnp.float32) * live_ref[mine]
     tokens_out[...] = grad_resid
     branch_ref[...] = grad_resid.astype(jnp.bfloat16)
+    stages = dp.bit_length() - 1
     first_loads[2].wait()
-    for step in range(1, groups):
-        attn_send[step - 1] = times(branch_ref[...], weights[step - 1, :, out_part]).astype(
-            jnp.bfloat16
-        )
-        attn_copy(step).start()
-    attn_grad[group] = times_t(branch_ref[...], out_own[...]).astype(jnp.bfloat16)
+    for number in range(spans):
+        columns = pl.ds(number * span_w, span_w)
+        for step in range(1, groups):
+            attn_send[number, step - 1] = times(branch_ref[...], weights[step - 1, :, columns]).astype(
+                jnp.bfloat16
+            )
+            attn_copy(number, step).start()
+        attn_grad[number, group] = times_t(branch_ref[...], out_own[columns]).astype(jnp.bfloat16)
+
+    spread.wait_recv(0)
+    spread.start(1)
 
     def store(start, size, total):
         if start == 0:
-            out_total[...] = total[:share]
+            output_out[...] = total[:share]
         out_send[pl.ds(start, size)] = total.astype(jnp.bfloat16)
 
     scatter = scatter_from(dp, lambda chunk: times(chunk_ref[chunk], branch_ref[...]), store, scatter_refs)
@@ -753,13 +770,14 @@
     key_sum[...] = jnp.zeros_like(key_sum)
     value_sum[...] = jnp.zeros_like(value_sum)
 
-    def attend(block):
+    def attend(number, block):
         part = pl.ds(block * rows, rows)
 
         @pl.when(block != group)
         def _():
             step = (group - block + groups) % groups
-            to_group(step, groups, attn_grad.at[block], attn_grad.at[block], attn_sems).wait_recv()
+            landed = attn_grad.at[number, block]
+            to_group(step, groups, landed, landed, attn_sems.at[number]).wait_recv()
 
         query_seg = seg_row[:, part]
         query_place = lax.broadcasted_iota(jnp.int32, (rows, rows), 1) + block * rows
@@ -767,10 +785,10 @@
         def wide(entries):
             return jnp.concatenate([entries] * heads, axis=1)
 
-        def span(number, carry):
-            columns = pl.ds(pl.multiple_of(number * span_w, span_w), span_w)
+        if True:
+            columns = pl.ds(number * span_w, span_w)
             query = query_ref[part, columns]
-            grad = attn_grad[block, :, columns]
+            grad = attn_grad[number, block]
             weighed = (grad.astype(jnp.float32) * attn_ref[part, columns].astype(jnp.float32)).T
             centres = jnp.sum(weighed.reshape(heads, head_width, rows), axis=1)
             centre = jnp.concatenate([centres[head : head + 1] for head in range(heads)], axis=1)
@@ -803,9 +821,6 @@
                 [turned[:, head * rows : (head + 1) * rows] for head in range(heads)], axis=0
             )
             grad_out[part, columns] = stacked.T.astype(jnp.bfloat16)
-            return carry
-
-        lax.fori_loop(0, width // span_w, span, 0)
 
         def folded(total):
             sums = total[part, pl.ds(0, pair)]
@@ -813,37 +828,31 @@
                 sums = sums + total[part, pl.ds(step * pair, pair)]
             return sums + pltpu.roll(sums, head_width, 1)
 
-        grad_k = folded(key_sum) * scale
-        grad_k = (
-            grad_k * cosine[part]
-            - pltpu.roll(grad_k, pair - half, 1) * sine_a[part]
-            - pltpu.roll(grad_k, half, 1) * sine_b[part]
-        )
-        first = lax.broadcasted_iota(jnp.int32, (rows, pair), 1) < head_width
-        grad_out[part, pl.ds(width, pair)] = jnp.where(first, grad_k, folded(value_sum)).astype(
-            jnp.bfloat16
-        )
+        if number == spans - 1:
+            grad_k = folded(key_sum) * scale
+            grad_k = (
+                grad_k * cosine[part]
+                - pltpu.roll(grad_k, pair - half, 1) * sine_a[part]
+                - pltpu.roll(grad_k, half, 1) * sine_b[part]
+            )
+            first = lax.broadcasted_iota(jnp.int32, (rows, pair), 1) < head_width
+            grad_out[part, pl.ds(width, pair)] = jnp.where(
+                first, grad_k, folded(value_sum)
+            ).astype(jnp.bfloat16)
 
         @pl.when(block != group)
         def _():
-            grad_copy((block - group + groups) % groups, block).start()
-
-    stages = dp.bit_length() - 1
-    for block in reversed(range(groups)):
-        attend(block)
-        if block == groups - 1:
+            grad_copy(number, (block - group + groups) % groups, block).start()
+
+    turns = [(number, block) for number in range(spans) for block in reversed(range(groups))]
+    for turn, (number, block) in enumerate(turns):
+        attend(number, block)
+        if turn == 3:
             for stage in range(1, stages - 1):
-                scatter.later(stage)
-            for stage in range(stages - 1):
                 spread.wait_recv(stage)
-                if stage < stages - 2:
-                    spread.start(stage + 1)
-        if block == groups - 2:
-            scatter.later(stages - 1)
-            spread.start(stages - 1)
-            for step in range(1, groups):
-                out_copy(step).start()
-
+                spread.start(stage + 1)
+    for stage in range(1, stages - 1):
+        scatter.later(stage)
     spread.wait_recv(stages - 1)
     part_rows = qkv_all.shape[2]
     last_loads = [
@@ -854,30 +863,31 @@
     ]
     for one in last_loads:
         one.start()
-    total = out_total[...]
-    for step in range(1, groups):
-        out_copy(step).wait_recv()
-        total = total + out_recv[step - 1].astype(jnp.float32)
-    output_out[...] = total
     grad_act = times_t(grad_out[mine, out_part], qkv_own[...])
     grad_act = grad_act + times_t(grad_out[mine, pl.ds(width, pair)], pair_own[...])
     for one in last_loads:
         one.wait()
-    for step in range(1, groups):
-        to_group(step, groups, arrived.at[step - 1], arrived.at[step - 1], grad_sems).wait_recv()
-        grad_act = grad_act + times_t(arrived[step - 1], weights[others - step])
+    for number in range(spans):
+        columns = columns_of(number)
+        for step in range(1, groups):
+            landed = arrived.at[step - 1, :, columns]
+            to_group(step, groups, landed, landed, grad_sems.at[number]).wait_recv()
+            grad_act = grad_act + times_t(
+                arrived[step - 1, :, columns], weights[others - step, :, columns]
+            )
     first_loads[4].wait()
     by_tokens, attn_rows = norm_back(tokens_ref[...].astype(jnp.float32), attn_gain[...], grad_act)
     tokens_out[...] += by_tokens
+    scatter.later(stages - 1)
     columns = gains_out.shape[2]
     for place in range(dp):
         span = slice(place * columns, (place + 1) * columns)
         gains_out[place, 0:1] = mlp_rows[:, span]
         gains_out[place, 1:2] = attn_rows[:, span]
     for step in range(1, groups):
-        attn_copy(step).wait_send()
-        grad_copy(step, 0).wait_send()
-        out_copy(step).wait_send()
+        for number in range(spans):
+            attn_copy(number, step).wait_send()
+            grad_copy(number, step, 0).wait_send()
     spread.wait_send()
     scatter.finish()
 
@@ -901,11 +911,12 @@
             jax.ShapeDtypeStruct((rows, features), f32),
             jax.ShapeDtypeStruct((dp, 2, features // dp), f32),
             jax.ShapeDtypeStruct((share, features), f32),
+            jax.ShapeDtypeStruct((groups * share, features), bf16),
             jax.ShapeDtypeStruct((count, columns), bf16),
             jax.ShapeDtypeStruct((groups - 1, dp) + parts.shape[1:], bf16),
         ],
         in_specs=[any_spec if index in (1, 2, 4, 8, 24) else vmem for index in range(25)],
-        out_specs=[vmem] * 4 + [any_spec],
+        out_specs=[vmem] * 5 + [any_spec],
         scratch_shapes=[
             pltpu.VMEM((rows, features), bf16),
             pltpu.VMEM((rows, features), bf16),
@@ -917,18 +928,14 @@
             pltpu.VMEM((head_width, stacked), f32),
             pltpu.VMEM((count, span_w), f32),
             pltpu.VMEM((count, span_w), f32),
-            pltpu.VMEM((groups - 1, rows, width), bf16),
-            pltpu.VMEM((groups, rows, width), bf16),
+            pltpu.VMEM((width // span_w, groups - 1, rows, span_w), bf16),
+            pltpu.VMEM((width // span_w, groups, rows, span_w), bf16),
             pltpu.VMEM((groups - 1, rows, columns), bf16),
-            pltpu.VMEM((share, features), f32),
-            pltpu.VMEM((groups * share, features), bf16),
-            pltpu.VMEM((groups - 1, share, features), bf16),
             pltpu.VMEM((rows, features), bf16),
             pltpu.SemaphoreType.DMA((5,)),
             pltpu.SemaphoreType.DMA((dp,)),
-            pltpu.SemaphoreType.DMA((2, groups - 1)),
-            pltpu.SemaphoreType.DMA((2, groups - 1)),
-            pltpu.SemaphoreType.DMA((2, groups - 1)),
+            pltpu.SemaphoreType.DMA((width // span_w, 2, groups - 1)),
+            pltpu.SemaphoreType.DMA((width // span_w, 2, groups - 1)),
             pltpu.SemaphoreType.DMA((2, dp - 1)),
             pltpu.SemaphoreType.DMA((2, dp - 1)),
         ]
@@ -940,7 +947,7 @@
     )(*operands)
 
 
-def last_sums_kernel(dp, groups, lhs_ref, rhs_ref, gains_ref, query_out, key_out, value_out, gains_out, near, far, total, near_sems, far_sems, *scatter_refs):
+def last_sums_kernel(dp, groups, lhs_ref, rhs_ref, gains_ref, output_ref, sums_ref, query_out, key_out, value_out, output_out, gains_out, out_recv, out_sems, near, far, total, near_sems, far_sems, *scatter_refs):
     pack, group = lax.axis_index("dp"), lax.axis_index("kv")
 
     def store(start, size, value):
@@ -950,6 +957,12 @@
         value_out[span] = value[:, width + head_width :]
 
     scatter = scatter_from(dp, lambda chunk: times(lhs_ref[chunk], rhs_ref[...]), store, scatter_refs)
+
+    share = output_out.shape[0]
+
+    def out_copy(step):
+        source = sums_ref.at[pl.ds(step * share, share)]
+        return to_group(step, groups, source, out_recv.at[step - 1], out_sems)
 
     def near_copy(step):
         return pltpu.make_async_remote_copy(
@@ -984,6 +997,7 @@
     pl.semaphore_wait(barrier, dp + groups - 2)
     for step in range(1, groups):
         near_copy(step).start()
+        out_copy(step).start()
     scatter.other_chunks()
     value = gains_ref[...]
     for step in range(1, groups):
@@ -1000,14 +1014,20 @@
         far_copy(step).wait_recv()
         value = value + far[step - 1]
     gains_out[...] = value
+    value = output_ref[...]
+    for step in range(1, groups):
+        out_copy(step).wait_recv()
+        value = value + out_recv[step - 1].astype(jnp.float32)
+    output_out[...] = value
     for step in range(1, groups):
         near_copy(step).wait_send()
+        out_copy(step).wait_send()
     for step in range(1, dp):
         far_copy(step).wait_send()
     scatter.finish()
 
 
-def last_sums(lhs, rhs, gains, head_width, groups, collective_id):
+def last_sums(lhs, rhs, gains, output, sums, head_width, groups, collective_id):
     dp, rows = lhs.shape[0], lhs.shape[1]
     columns = rhs.shape[1]
     vmem = pl.BlockSpec(memory_space=pltpu.VMEM)
@@ -1017,11 +1037,14 @@
             jax.ShapeDtypeStruct((rows, columns - 2 * head_width), jnp.float32),
             jax.ShapeDtypeStruct((rows, head_width), jnp.float32),
             jax.ShapeDtypeStruct((rows, head_width), jnp.float32),
+            jax.ShapeDtypeStruct(output.shape, jnp.float32),
             jax.ShapeDtypeStruct(gains.shape[1:], jnp.float32),
         ],
-        in_specs=[vmem] * 3,
-        out_specs=[vmem] * 4,
+        in_specs=[vmem] * 5,
+        out_specs=[vmem] * 5,
         scratch_shapes=[
+            pltpu.VMEM((groups - 1,) + output.shape, jnp.bfloat16),
+            pltpu.SemaphoreType.DMA((2, groups - 1)),
             pltpu.VMEM((groups - 1,) + gains.shape, jnp.float32),
             pltpu.VMEM((dp - 1,) + gains.shape[1:], jnp.float32),
             pltpu.VMEM(gains.shape, jnp.float32),
@@ -1035,7 +1058,7 @@
         cost_estimate=pl.CostEstimate(
             flops=2 * lhs.size * columns, bytes_accessed=2 * lhs.size, transcendentals=0
         ),
-    )(lhs, rhs, gains)
+    )(lhs, rhs, gains, output, sums)
 
 
 def row_chunks(matrix, count):
@@ -1092,7 +1115,8 @@
         grad_gate,
         grad_up,
         grad_act_two,
-        feed_part,
+        feed_early,
+        feed_late,
         resid_mine,
         attn_others,
         out_others,
@@ -1122,10 +1146,10 @@
         2,
     )
     grad_two_mine = lax.psum_scatter(grad_act_two, "kv", scatter_dimension=0, tiled=True)
-    grad_two_mine, feed_part, qkv_parts = lax.optimization_barrier(
-        (grad_two_mine, feed_part, qkv_parts)
+    grad_two_mine, feed_early, qkv_parts = lax.optimization_barrier(
+        (grad_two_mine, feed_early, qkv_parts)
     )
-    grad_tokens, gain_rows, sent_output, grad_qkv, _ = attention_back(
+    grad_tokens, gain_rows, own_output, output_sums, grad_qkv, _ = attention_back(
         (
             grad_two_mine,
             resid_mine,
@@ -1157,16 +1181,24 @@
         head_width,
         3,
     )
-    sent_query, sent_key, sent_value, gains = last_sums(
-        row_chunks(act_flipped, pack_count), grad_qkv, gain_rows, head_width, group_count, 4
+    early_sum = lax.psum_scatter(feed_early, "kv", scatter_dimension=0, tiled=True)
+    early_sum, feed_late, grad_qkv = lax.optimization_barrier((early_sum, feed_late, grad_qkv))
+    sent_query, sent_key, sent_value, sent_output, gains = last_sums(
+        row_chunks(act_flipped, pack_count),
+        grad_qkv,
+        gain_rows,
+        own_output,
+        output_sums,
+        head_width,
+        group_count,
+        4,
     )
     sent_two, sent_one = gains[0], gains[1]
     sent_output = sent_output[None]
     sent_down = sent_down[: w_down.shape[1] // pack_count][None]
-    layer_out = (
-        resid_mine
-        + lax.psum_scatter(feed_part, "kv", scatter_dimension=0, tiled=True).astype(jnp.float32)
-    ).astype(jnp.bfloat16)
+    late_sum = lax.psum_scatter(feed_late, "kv", scatter_dimension=0, tiled=True)
+    feed_sum = jnp.concatenate([early_sum, late_sum], axis=1).astype(jnp.float32)
+    layer_out = (resid_mine + feed_sum).astype(jnp.bfloat16)
     return (
         layer_out,
         grad_tokens,

time: 490 us -> 453 us (0.924)
  the two profiles are of different devices: /device:TPU:8 before, /device:TPU:24 now
where the time goes in v5:
time: 453 us; the launch traced here: 445 us
  Pallas kernels  403 us (89%)
  local copies, waits for them, and re-layouts  17.5 us (4%)
  between operations  15 us (3%)
  other arithmetic  5.25 us (1%)
    pallas_call x1, Pallas kernels, attention_back(): pl.pallas_call(functools.partial(attention_back_kernel, dp, groups, head_...  109 us
    pallas_call x1, Pallas kernels, feed_forward(): pl.pallas_call(functools.partial(feed_forward_kernel, dp, groups), grid=(...  96.3 us
    pallas_call x1, Pallas kernels, product_scatter(): pl.pallas_call(functools.partial(product_scatter_kernel, count, dp, group...  95.9 us
    pallas_call x1, Pallas kernels, last_sums(): pl.pallas_call(functools.partial(last_sums_kernel, dp, groups), out_shape...  68.3 us
    pallas_call x1, Pallas kernels, attention(): pl.pallas_call(functools.partial(attention_kernel, groups, head_width), o...  32.9 us
    unnamed x30, local copies, waits for them, and re-layouts  11.8 us
  transfers between devices with their start and end apart: 3, of which 1 were waited for; matrix products, arithmetic and copies ran while one was open for 1% of the time, Pallas kernels for 61%

profile of v5, /device:TPU:24, one launch (start us, length us, event | category | flops | bytes accessed | tf_op | source)
XLA Modules:
  0.0 445.0 jit_solution(13744872598760362457)
XLA Ops:
  7.2 0.0 reduce-scatter.4.cloned.1.call-start
  7.9 0.6 broadcast_in_dim_tile.3.refs_6_
  8.5 1.0 constant_dynamic-slice_fusion.1
  9.5 0.8 copy.31
  10.3 0.8 fusion.refs_8_.refs_11_.refs_3_
  11.2 1.2 copy.29
  12.4 0.3 copy.30
  12.7 1.0 copy.32.refs_4_.refs_15_
  13.7 1.1 pad_maximum_fusion.refs_3_.refs_23_
  14.8 32.9 %shard_map.212 = (bf16[1024,512]{1,0:T(8,128)(2,1)}, bf16[2048,1024]{1,0:T(8,128)(2,1)}, bf16[1024,512]{1,0:T(8,128)(2,1)}, bf16[1024,256]{1,0:T(8,128)(2,1)}, b...) custom-call(bf16[1024,2048]{1,0:T(8,128)(2,1)} %refs_4_.3, ...), custom_call_target="tpu_custom_call" | custom-call | flops 4294967296 | bytes 16777216 | tf_op jit(solution)/shard_map/pallas_call | solution.py:217
  47.8 96.3 %shard_map.213 = (bf16[2048,1024]{1,0:T(8,128)(2,1)}, bf16[1408,1024]{1,0:T(8,128)(2,1)}, bf16[1024,1408]{1,0:T(8,128)(2,1)}, bf16[1024,1408]{1,0:T(8,128)(2,1)}...) custom-call(bf16[1024,512]{1,0:T(8,128)(2,1)} %get-tuple-element.53., ...), custom_call_target="tpu_custom_call" | custom-call | flops 44023414784 | bytes 83886080 | tf_op jit(solution)/shard_map/pallas_call | solution.py:427
  144.1 0.0 reduce-scatter.6.cloned.1.call-start
  144.1 0.1 fusion.1
  144.2 1.0 constant_dynamic-slice_fusion
  145.2 0.8 pad_maximum_fusion.1.refs_6_
  146.0 95.9 %shard_map.214 = (f32[256,1408]{1,0:T(8,128)}, f32[256,1408]{1,0:T(8,128)}, f32[176,2048]{1,0:T(8,128)}, bf16[3,256,640]{2,1,0:T(8,128)(2,1)}) custom-call(bf16[8,256,1024]{2,1,0:T(8,128)(2,1)} %bitcast.36, bf16[8,256,1024]{2,1,0:T(8,128)(2,1)} %bitcast.37, bf16[8,176,1024]{2,1,0:T(8,128)(2,1)} %bitcast.38, bf16[1024,1408]{1,0:T(8,128)(2,1)} %get-tuple-element.60.refs_3_, ...), custom_call_target="tpu_custom_call" | custom-call | flops 53150220288 | bytes 21233664 | tf_op jit(solution)/shard_map/pallas_call | solution.py:652
  241.9 4.4 reduce-scatter.4.cloned.1.call-done.refs_0_
  246.3 0.0 reduce-scatter.8.cloned.1.call-start
  246.4 109.3 %shard_map.215 = (f32[256,2048]{1,0:T(8,128)}, f32[8,2,256]{2,1,0:T(2,128)}, f32[64,2048]{1,0:T(8,128)}, bf16[256,2048]{1,0:T(8,128)(2,1)}, bf16[1024,640]{1,0:T(8,128)(2,1)}, /*index=5*/bf16[3,8,256,640]{3,2,1,0:T(8,128)(2,1)}) custom-call(bf16[256,2048]{1,0:T(8,128)(2,1)} %reduce-scatter.4.cloned.1.call-done.refs_0_, ...), custom_call_target="tpu_custom_call" | custom-call | flops 10737418240 | bytes 41943040 | tf_op jit(solution)/shard_map/pallas_call | solution.py:908
  355.7 68.3 %shard_map.216 = (f32[256,512]{1,0:T(8,128)}, f32[256,64]{1,0:T(8,128)}, f32[256,64]{1,0:T(8,128)}, f32[64,2048]{1,0:T(8,128)}, f32[2,256]{1,0:T(2,128)}) custom-call(bf16[8,256,1024]{2,1,0:T(8,128)(2,1)} %bitcast.35, bf16[1024,640]{1,0:T(8,128)(2,1)} %get-tuple-element.83.rhs_ref, f32[8,2,256]{2,1,0:T(2,128)} %get-tuple-element.84.gains_ref, ...), custom_call_target="tpu_custom_call" | custom-call | flops 2684354560 | bytes 4194304 | tf_op jit(solution)/shard_map/pallas_call | solution.py:1034
  424.0 1.6 copy.34
  425.6 1.6 copy.35
  427.2 1.3 fusion.2
  428.5 2.4 add_convert_fusion
  430.9 1.3 copy.43
  432.3 0.1 copy-done.6
  432.3 0.8 copy.44
  433.1 0.8 copy.45
  433.9 1.1 copy.46
  435.0 1.1 copy.47
  436.1 0.8 copy-done.2
  436.9 1.1 copy.48
  (25 shorter events, 0.1 us)
Async XLA Ops:
  7.2 5.2 %copy-start.8 = (bf16[2048,64]{0,1:T(8,128)(2,1)S(1)}, bf16[2048,64]{0,1:T(8,128)(2,1)}, u32[]{:S(2)}) copy-start(bf16[2048,64]{0,1:T(8,128)(2,1)} %param.17) | copy-start | bytes 786436
  7.2 5.5 %copy-start.9 = (s32[1024]{0:T(1024)S(1)}, s32[1024]{0:T(1024)}, u32[]{:S(2)}) copy-start(s32[1024]{0:T(1024)} %param.24) | copy-start | bytes 12292
  7.2 239.1 %reduce-scatter.4.cloned.1.call-start = ((), (), s32[]{:S(2)}) async-start(), calls=%async_computation.3 | async-start | bytes 5242880 | tf_op jit(solution)/shard_map/reduce_scatter | solution.py:1148
  144.1 211.6 %reduce-scatter.6.cloned.1.call-start = ((), (), s32[]{:S(2)}) async-start(), calls=%async_computation.4 | async-start | bytes 2621440 | tf_op jit(solution)/shard_map/reduce_scatter | solution.py:1184
  246.3 182.2 %reduce-scatter.8.cloned.1.call-start = ((), (), s32[]{:S(2)}) async-start(), calls=%async_computation.5 | async-start | bytes 2621440 | tf_op jit(solution)/shard_map/reduce_scatter | solution.py:1199
  355.7 72.8 %copy-start = (f32[256,2048]{1,0:T(8,128)S(1)}, f32[256,2048]{1,0:T(8,128)}, u32[]{:S(2)}) copy-start(f32[256,2048]{1,0:T(8,128)} %get-tuple-element.55.refs_1_) | copy-start | bytes 6291460
  355.7 72.8 %copy-start.7 = (bf16[256,1024]{1,0:T(8,128)(2,1)S(1)}, bf16[256,1024]{1,0:T(8,128)(2,1)}, u32[]{:S(2)}) copy-start(bf16[256,1024]{1,0:T(8,128)(2,1)} %reduce-scatter.6.cloned.1.call-done) | copy-start | bytes 1572868
  428.5 2.5 copy-start.1
  430.9 1.4 copy-start.6
  430.9 2.2 copy-start.5
  432.3 1.6 copy-start.4
  433.1 1.9 copy-start.3
  435.0 1.9 copy-start.2
Sparse Core Ops, SparseCore 0:
  144.2 102.0 reduce-scatter.3
  248.7 59.2 reduce-scatter.5
  355.8 68.0 reduce-scatter.7

commit v6 on v5

--- a/solution.py
+++ b/solution.py
@@ -258,10 +258,10 @@
 def feed_forward_kernel(dp, groups, *refs):
     (
         attn_hbm, attn_ref, part_ref, own_hbm, gate_hbm, up_hbm, down_hbm, cot_hbm, live_hbm,
-        tokens_ref, gain_ref, live_ref,
-        act_out, hidden_out, gate_out, up_out, back_out, feed_a_out, feed_b_out, resid_out, rows_out, all_out,
+        tokens_ref, gain_ref, live_ref, pass_hbm,
+        act_out, hidden_out, gate_out, up_out, back_out, feed_a_out, feed_b_out, resid_out, rows_out, all_out, pass_out,
         attn_in, all_ref, own_ref, w_gate, w_up, w_down, cot_ref, live_all, grad_hidden, resid_ref,
-        load_sem, send_sem, recv_sem, spread_send, spread_recv, out_sem,
+        load_sem, send_sem, recv_sem, spread_send, spread_recv, out_sem, pass_sems,
     ) = refs
     block = pl.program_id(0)
     blocks = groups
@@ -270,6 +270,7 @@
     rows = tokens_ref.shape[0]
     others = groups - 1
     spread = Spread(all_ref, spread_send, spread_recv, dp)
+    stages = dp.bit_length() - 1
     loads = [
         pltpu.make_async_copy(source, target, load_sem.at[index])
         for index, (source, target) in enumerate(
@@ -295,34 +296,38 @@
             device_id_type=MESH,
         )
 
+    def pass_copy(step):
+        return to_group(step, groups, pass_hbm, pass_out.at[others - step], pass_sems)
+
+    line = groups == 4
+    inner = (group == 1) | (group == 2)
+    direct = (1, 3) if line else tuple(range(1, groups))
+    relays = ((0, 3, 1), (2, 1, others)) if line else ()
+
+    def own_copy(part, step):
+        return attn_copy(part, step, others - step, attn_hbm, step - 1)
+
     def send_rows(part):
-        for step in range(1, groups):
-            copy = attn_copy(part, step, others - step, attn_hbm, step - 1)
-            if step in relayed:
-                pl.when((group == 0) | (group == 3))(copy.start)
-            else:
-                copy.start()
-
-    relayed = (2,) if groups == 4 else ()
-    relays = ((1, 0, 3), (2, 2, 1)) if groups == 4 else ()
+        for step in direct:
+            own_copy(part, step).start()
 
     def wait_rows(part, slot):
         attn_copy(part, 1, slot, attn_hbm, 0).wait_recv()
 
     def pass_on(part):
-        for holder, slot, step in relays:
-
-            @pl.when(group == holder)
+        if line:
+
+            @pl.when(inner)
             def _():
-                wait_rows(part, slot)
-                attn_copy(part, step, 1, attn_in.at[slot], 1).start()
+                for slot, step, place in relays:
+                    wait_rows(part, slot)
+                    attn_copy(part, step, 1, attn_in.at[slot], place).start()
 
     def wait_block(part):
         for slot in range(others):
-            holders = [holder for holder, place, _ in relays if place == slot]
-            if holders:
-
-                @pl.when(group != holders[0])
+            if line and slot != 1:
+
+                @pl.when(jnp.logical_not(inner))
                 def _():
                     wait_rows(part, slot)
             else:
@@ -345,14 +350,13 @@
             send_rows(part)
         for load in loads[:3]:
             load.wait()
-        stages = dp.bit_length() - 1
         for stage in range(stages):
             if stage < blocks:
                 hidden_gradient(stage)
             spread.wait_recv(stage)
             if stage + 1 < stages:
                 spread.start(stage + 1)
-            if stage < 2:
+            if stage < blocks - 1:
                 pass_on(stage)
         for part in range(stages, blocks):
             hidden_gradient(part)
@@ -391,9 +395,12 @@
         copy.start()
         copy.wait()
 
-    @pl.when(block < blocks - 2)
+    @pl.when(block == 0)
     def _():
-        pass_on(block + 2)
+        for part in range(min(stages, blocks - 1), blocks):
+            pass_on(part)
+        for step in range(1, groups):
+            pass_copy(step).start()
 
     @pl.when(block == blocks - 1)
     def _():
@@ -405,21 +412,31 @@
         for copy in copies:
             copy.start()
         for part in range(blocks):
-            for place in range(others):
-                attn_copy(part, 1, 0, attn_hbm, place).wait_send()
+            for step in direct:
+                own_copy(part, step).wait_send()
+        if line:
+
+            @pl.when(inner)
+            def _():
+                for part in range(blocks):
+                    for slot, step, place in relays:
+                        attn_copy(part, step, 1, attn_in.at[slot], place).wait_send()
+
         spread.wait_send()
+        for step in range(1, groups):
+            pass_copy(step).wait()
         for copy in copies:
             copy.wait()
 
 
-def feed_forward(attn, part, w_own, w_gate, w_up, w_down, cotangent, live, tokens, gain, sizes, collective_id):
+def feed_forward(attn, part, w_own, w_gate, w_up, w_down, cotangent, live, tokens, gain, passed, sizes, collective_id):
     dp, groups = sizes
     count, features = tokens.shape
     rows = count // groups
     width, hidden = w_own.shape[0], w_gate.shape[1]
     share = part.shape[1]
     others = groups - 1
-    early = features // 2
+    early = 5 * features // 8
     any_spec = pl.BlockSpec(memory_space=pl.ANY)
     by_row = lambda columns: pl.BlockSpec((rows, columns), lambda i: (i, 0))
     by_column = lambda height: pl.BlockSpec((height, rows), lambda i: (0, i))
@@ -438,6 +455,7 @@
             jax.ShapeDtypeStruct((rows, features), jnp.float32),
             jax.ShapeDtypeStruct((others, rows, width), jnp.bfloat16),
             jax.ShapeDtypeStruct((others, dp, share, width), jnp.bfloat16),
+            jax.ShapeDtypeStruct((others,) + passed.shape, jnp.bfloat16),
         ],
         in_specs=[
             any_spec,
@@ -447,10 +465,11 @@
             by_row(features),
             pl.BlockSpec(memory_space=pltpu.VMEM),
             by_row(1),
+            any_spec,
         ],
         out_specs=[
             by_column(features), by_column(hidden), by_row(hidden), by_row(hidden),
-            by_row(features), by_row(early), by_row(features - early), any_spec, any_spec, any_spec,
+            by_row(features), by_row(early), by_row(features - early), any_spec, any_spec, any_spec, any_spec,
         ],
         scratch_shapes=[
             pltpu.VMEM((others, count, width), jnp.bfloat16),
@@ -464,17 +483,18 @@
             pltpu.VMEM((count, hidden), jnp.bfloat16),
             pltpu.VMEM((rows, features), jnp.float32),
             pltpu.SemaphoreType.DMA((6,)),
-            pltpu.SemaphoreType.DMA((groups, others)),
+            pltpu.SemaphoreType.DMA((groups, groups)),
             pltpu.SemaphoreType.DMA((groups, others)),
             pltpu.SemaphoreType.DMA((2, dp - 1)),
             pltpu.SemaphoreType.DMA((2, dp - 1)),
             pltpu.SemaphoreType.DMA((3,)),
+            pltpu.SemaphoreType.DMA((2, groups - 1)),
         ],
         compiler_params=pltpu.CompilerParams(
             collective_id=collective_id, has_side_effects=True, vmem_limit_bytes=VMEM_LIMIT
         ),
         cost_estimate=pl.CostEstimate(flops=flops, bytes_accessed=40 * count * features, transcendentals=0),
-    )(attn, attn, part, w_own, w_gate, w_up, w_down, cotangent, live, tokens, gain, live)
+    )(attn, attn, part, w_own, w_gate, w_up, w_down, cotangent, live, tokens, gain, live, passed)
 
 
 class Scatter:
@@ -598,13 +618,9 @@
     return Scatter(dp, product, store, refs[0], refs[1], refs[2:4], refs[4:8])
 
 
-def product_scatter_kernel(count, dp, groups, *refs):
-    lhs, rhs, pass_ref = refs[:count], refs[count : 2 * count], refs[2 * count]
-    outs, pass_out = refs[2 * count + 1 : 3 * count + 1], refs[3 * count + 1]
-    pass_sems, scratch = refs[3 * count + 2], refs[3 * count + 3 :]
-
-    def pass_copy(step):
-        return to_group(step, groups, pass_ref, pass_out.at[groups - 1 - step], pass_sems)
+def product_scatter_kernel(count, dp, *refs):
+    lhs, rhs = refs[:count], refs[count : 2 * count]
+    outs, scratch = refs[2 * count : 3 * count], refs[3 * count :]
 
     def member(a):
         def product(chunk):
@@ -617,9 +633,7 @@
 
     members = [member(a) for a in range(count)]
     stages = dp.bit_length() - 1
-    greet(dp, groups)
-    for step in range(1, groups):
-        pass_copy(step).start()
+    greet(dp, 1)
     pending = []
     for a in range(count):
         members[a].other_chunks()
@@ -637,11 +651,9 @@
             pending.append((done, stage + 1))
     for one in members:
         one.finish()
-    for step in range(1, groups):
-        pass_copy(step).wait()
-
-
-def product_scatter(pairs, passed, groups, collective_id):
+
+
+def product_scatter(pairs, collective_id):
     count = len(pairs)
     dp = pairs[0][0].shape[0]
     dims = [(lhs.shape[1], rhs.shape[1]) for lhs, rhs in pairs]
@@ -650,18 +662,16 @@
     vmem = pl.BlockSpec(memory_space=pltpu.VMEM)
     any_spec = pl.BlockSpec(memory_space=pl.ANY)
     return pl.pallas_call(
-        functools.partial(product_scatter_kernel, count, dp, groups),
-        out_shape=[jax.ShapeDtypeStruct(dim, jnp.float32) for dim in dims]
-        + [jax.ShapeDtypeStruct((groups - 1,) + passed.shape, passed.dtype)],
-        in_specs=[vmem] * (2 * count) + [any_spec],
-        out_specs=[vmem] * count + [any_spec],
-        scratch_shapes=[pltpu.SemaphoreType.DMA((2, groups - 1))]
-        + sum([scatter_scratch(dp, *dim) for dim in dims], []),
+        functools.partial(product_scatter_kernel, count, dp),
+        out_shape=[jax.ShapeDtypeStruct(dim, jnp.float32) for dim in dims],
+        in_specs=[vmem] * (2 * count),
+        out_specs=[vmem] * count,
+        scratch_shapes=sum([scatter_scratch(dp, *dim) for dim in dims], []),
         compiler_params=pltpu.CompilerParams(
             collective_id=collective_id, has_side_effects=True, vmem_limit_bytes=VMEM_LIMIT
         ),
         cost_estimate=pl.CostEstimate(flops=flops * 3, bytes_accessed=moved, transcendentals=0),
-    )(*[lhs for lhs, _ in pairs], *[rhs for _, rhs in pairs], passed)
+    )(*[lhs for lhs, _ in pairs], *[rhs for _, rhs in pairs])
 
 
 def norm_back(values, gain, grads):
@@ -1120,6 +1130,7 @@
         resid_mine,
         attn_others,
         out_others,
+        qkv_parts,
     ) = feed_forward(
         attn_out,
         out_parts,
@@ -1131,23 +1142,22 @@
         live_rows,
         tokens_in,
         mlp_gain[None],
+        qkv_part,
         sizes,
         1,
     )
     second_chunks = row_chunks(second_flipped, pack_count)
-    sent_gate, sent_up, sent_down, qkv_parts = product_scatter(
+    sent_gate, sent_up, sent_down = product_scatter(
         [
             (second_chunks, grad_gate),
             (second_chunks, grad_up),
             (row_chunks(hidden_flipped, pack_count), cotangent),
         ],
-        qkv_part,
-        group_count,
         2,
     )
     grad_two_mine = lax.psum_scatter(grad_act_two, "kv", scatter_dimension=0, tiled=True)
-    grad_two_mine, feed_early, qkv_parts = lax.optimization_barrier(
-        (grad_two_mine, feed_early, qkv_parts)
+    grad_two_mine, feed_early, sent_down = lax.optimization_barrier(
+        (grad_two_mine, feed_early, sent_down)
     )
     grad_tokens, gain_rows, own_output, output_sums, grad_qkv, _ = attention_back(
         (

time: 453 us -> 446 us (0.985)
  the two profiles are of different devices: /device:TPU:24 before, /device:TPU:8 now
where the time goes in v6:
time: 446 us; the launch traced here: 437 us
  Pallas kernels  398 us (89%)
  local copies, waits for them, and re-layouts  19.1 us (4%)
  between operations  15 us (3%)
  other arithmetic  5.17 us (1%)
    pallas_call x1, Pallas kernels, attention_back(): pl.pallas_call(functools.partial(attention_back_kernel, dp, groups, head_...  110 us
    pallas_call x1, Pallas kernels, feed_forward(): pl.pallas_call(functools.partial(feed_forward_kernel, dp, groups), grid=(...  108 us
    pallas_call x1, Pallas kernels, product_scatter(): pl.pallas_call(functools.partial(product_scatter_kernel, count, dp), out_...  89.3 us
    pallas_call x1, Pallas kernels, last_sums(): pl.pallas_call(functools.partial(last_sums_kernel, dp, groups), out_shape...  57.7 us
    pallas_call x1, Pallas kernels, attention(): pl.pallas_call(functools.partial(attention_kernel, groups, head_width), o...  33.1 us
    unnamed x26, local copies, waits for them, and re-layouts  12.7 us
  transfers between devices with their start and end apart: 3, of which 0 were waited for; matrix products, arithmetic and copies ran while one was open for 1% of the time, Pallas kernels for 59%

profile of v6, /device:TPU:8, one launch (start us, length us, event | category | flops | bytes accessed | tf_op | source)
XLA Modules:
  0.0 437.2 jit_solution(9583418715733548330)
XLA Ops:
  7.2 0.0 reduce-scatter.4.cloned.1.call-start
  7.2 1.2 copy.30
  8.5 1.2 copy.29
  9.7 1.7 copy.32.refs_4_.refs_15_
  11.4 0.6 broadcast_in_dim_tile.3.refs_6_
  12.0 1.1 pad_maximum_fusion.refs_3_.refs_23_
  13.1 0.1 fusion.1
  13.2 1.0 constant_dynamic-slice_fusion.1
  14.2 0.8 copy.31
  15.7 0.8 fusion.refs_8_.refs_11_.refs_3_
  16.5 1.0 constant_dynamic-slice_fusion
  17.5 0.8 pad_maximum_fusion.1.refs_12_
  18.2 33.1 %shard_map.212 = (bf16[1024,512]{1,0:T(8,128)(2,1)}, bf16[2048,1024]{1,0:T(8,128)(2,1)}, bf16[1024,512]{1,0:T(8,128)(2,1)}, bf16[1024,256]{1,0:T(8,128)(2,1)}, b...) custom-call(bf16[1024,2048]{1,0:T(8,128)(2,1)} %refs_4_.3, ...), custom_call_target="tpu_custom_call" | custom-call | flops 4294967296 | bytes 16777216 | tf_op jit(solution)/shard_map/pallas_call | solution.py:217
  51.3 107.9 %shard_map.213 = (bf16[2048,1024]{1,0:T(8,128)(2,1)}, bf16[1408,1024]{1,0:T(8,128)(2,1)}, bf16[1024,1408]{1,0:T(8,128)(2,1)}, bf16[1024,1408]{1,0:T(8,128)(2,1)}...) custom-call(bf16[1024,512]{1,0:T(8,128)(2,1)} %get-tuple-element.53., ...), custom_call_target="tpu_custom_call" | custom-call | flops 44023414784 | bytes 83886080 | tf_op jit(solution)/shard_map/pallas_call | solution.py:444
  159.3 0.0 reduce-scatter.6.cloned.1.call-start
  159.4 89.3 %shard_map.214 = (f32[256,1408]{1,0:T(8,128)}, f32[256,1408]{1,0:T(8,128)}, f32[176,2048]{1,0:T(8,128)}) custom-call(bf16[8,256,1024]{2,1,0:T(8,128)(2,1)} %bitcast.36, bf16[8,256,1024]{2,1,0:T(8,128)(2,1)} %bitcast.37, bf16[8,176,1024]{2,1,0:T(8,128)(2,1)} %bitcast.38, bf16[1024,1408]{1,0:T(8,128)(2,1)} %get-tuple-element.60.refs_3_, ...), custom_call_target="tpu_custom_call" | custom-call | flops 53150220288 | bytes 21233664 | tf_op jit(solution)/shard_map/pallas_call | solution.py:664
  248.8 0.0 reduce-scatter.8.cloned.1.call-start
  248.8 109.6 %shard_map.215 = (f32[256,2048]{1,0:T(8,128)}, f32[8,2,256]{2,1,0:T(2,128)}, f32[64,2048]{1,0:T(8,128)}, bf16[256,2048]{1,0:T(8,128)(2,1)}, bf16[1024,640]{1,0:T(8,128)(2,1)}, /*index=5*/bf16[3,8,256,640]{3,2,1,0:T(8,128)(2,1)}) custom-call(bf16[256,2048]{1,0:T(8,128)(2,1)} %reduce-scatter.4.cloned.1.call-done.refs_0_, ...), custom_call_target="tpu_custom_call" | custom-call | flops 10737418240 | bytes 41943040 | tf_op jit(solution)/shard_map/pallas_call | solution.py:918
  358.5 0.0 reduce-scatter.6.cloned.1.call-done
  358.5 57.7 %shard_map.216 = (f32[256,512]{1,0:T(8,128)}, f32[256,64]{1,0:T(8,128)}, f32[256,64]{1,0:T(8,128)}, f32[64,2048]{1,0:T(8,128)}, f32[2,256]{1,0:T(2,128)}) custom-call(bf16[8,256,1024]{2,1,0:T(8,128)(2,1)} %bitcast.35, bf16[1024,640]{1,0:T(8,128)(2,1)} %get-tuple-element.83.rhs_ref, f32[8,2,256]{2,1,0:T(2,128)} %get-tuple-element.84.gains_ref, ...), custom_call_target="tpu_custom_call" | custom-call | flops 2684354560 | bytes 4194304 | tf_op jit(solution)/shard_map/pallas_call | solution.py:1044
  416.3 1.6 copy.34
  417.9 1.6 copy.35
  419.5 1.3 fusion.2
  420.8 2.4 add_convert_fusion
  423.2 1.3 copy.43
  424.5 0.1 copy-done.7
  424.6 0.8 copy.44
  425.4 0.8 copy.45
  426.2 1.1 copy.46
  427.3 1.1 copy.47
  428.4 0.8 copy-done.2
  429.1 1.1 copy.48
  (21 shorter events, 0.1 us)
Async XLA Ops:
  7.2 241.6 %reduce-scatter.4.cloned.1.call-start = ((), (), s32[]{:S(2)}) async-start(), calls=%async_computation.3 | async-start | bytes 5242880 | tf_op jit(solution)/shard_map/reduce_scatter | solution.py:1158
  159.3 199.2 %reduce-scatter.6.cloned.1.call-start = ((), (), s32[]{:S(2)}) async-start(), calls=%async_computation.4 | async-start | bytes 3276800 | tf_op jit(solution)/shard_map/reduce_scatter | solution.py:1194
  248.8 172.0 %reduce-scatter.8.cloned.1.call-start = ((), (), s32[]{:S(2)}) async-start(), calls=%async_computation.5 | async-start | bytes 1966080 | tf_op jit(solution)/shard_map/reduce_scatter | solution.py:1209
  358.5 62.3 %copy-start = (f32[256,2048]{1,0:T(8,128)S(1)}, f32[256,2048]{1,0:T(8,128)}, u32[]{:S(2)}) copy-start(f32[256,2048]{1,0:T(8,128)} %get-tuple-element.55.refs_1_) | copy-start | bytes 6291460
  358.5 62.3 %copy-start.5 = (bf16[256,1280]{1,0:T(8,128)(2,1)S(1)}, bf16[256,1280]{1,0:T(8,128)(2,1)}, u32[]{:S(2)}) copy-start(bf16[256,1280]{1,0:T(8,128)(2,1)} %reduce-scatter.6.cloned.1.call-done) | copy-start | bytes 1966084
  420.8 2.4 copy-start.1
  423.2 1.4 copy-start.7
  423.2 2.2 copy-start.6
  424.6 1.6 copy-start.4
  425.4 1.9 copy-start.3
  427.3 1.9 copy-start.2
Sparse Core Ops, SparseCore 0:
  159.4 77.5 reduce-scatter.3
  248.9 61.8 reduce-scatter.5
  358.6 57.7 reduce-scatter.7

commit v7 on v6

--- a/solution.py
+++ b/solution.py
@@ -399,6 +399,9 @@
     def _():
         for part in range(min(stages, blocks - 1), blocks):
             pass_on(part)
+
+    @pl.when(block == 1)
+    def _():
         for step in range(1, groups):
             pass_copy(step).start()
 
@@ -553,11 +556,24 @@
 
         lax.fori_loop(0, self.slots, step, 0)
 
-    def own_chunks(self):
+    def slot_at(self, e):
+        t = 0
+        for place in range(self.bits - 1):
+            t = t + 2**place * ((e // 2**place + 1 + self.upper // 2**place) % 2)
+        return t
+
+    def own_chunks(self, others_too=False):
+        def other(t):
+            self.sent[t] = self.product(2 * t + 1 - self.bit(0)).astype(jnp.bfloat16)
+            self.first_copy(t).start()
+
+        if others_too:
+            other(self.slot_at(0))
+
         def step(e, carry):
-            t = 0
-            for place in range(self.bits - 1):
-                t = t + 2**place * ((e // 2**place + 1 + self.upper // 2**place) % 2)
+            if others_too:
+                pl.when(e + 1 < self.slots)(lambda: other(self.slot_at(e + 1)))
+            t = self.slot_at(e)
             own = self.product(2 * t + self.bit(0))
             self.first_copy(t).wait_recv()
             self.held[t] = (self.held[t].astype(jnp.float32) + own).astype(jnp.bfloat16)
@@ -636,8 +652,7 @@
     greet(dp, 1)
     pending = []
     for a in range(count):
-        members[a].other_chunks()
-        members[a].own_chunks()
+        members[a].own_chunks(others_too=True)
         pending.append((a, 1))
         if a > 0:
             done, stage = pending.pop(0)

time: 446 us -> 442 us (level)
  transfers between devices with their start and end apart: 3 -> 3, of which waited for: 0 -> 0; matrix products, arithmetic and copies ran while one was open for 1% -> 1% of each run, Pallas kernels for 59% -> 58%
where the time goes in v7:
time: 442 us; the launch traced here: 434 us
  Pallas kernels  394 us (89%)
  local copies, waits for them, and re-layouts  19.1 us (4%)
  between operations  14.8 us (3%)
  other arithmetic  5.17 us (1%)
    pallas_call x1, Pallas kernels, feed_forward(): pl.pallas_call(functools.partial(feed_forward_kernel, dp, groups), grid=(...  110 us
    pallas_call x1, Pallas kernels, attention_back(): pl.pallas_call(functools.partial(attention_back_kernel, dp, groups, head_...  108 us
    pallas_call x1, Pallas kernels, product_scatter(): pl.pallas_call(functools.partial(product_scatter_kernel, count, dp), out_...  87.2 us
    pallas_call x1, Pallas kernels, last_sums(): pl.pallas_call(functools.partial(last_sums_kernel, dp, groups), out_shape...  56.2 us
    pallas_call x1, Pallas kernels, attention(): pl.pallas_call(functools.partial(attention_kernel, groups, head_width), o...  33.1 us
    unnamed x26, local copies, waits for them, and re-layouts  12.7 us
  transfers between devices with their start and end apart: 3, of which 0 were waited for; matrix products, arithmetic and copies ran while one was open for 1% of the time, Pallas kernels for 58%

profile of v7, /device:TPU:8, one launch (start us, length us, event | category | flops | bytes accessed | tf_op | source)
XLA Modules:
  0.0 433.9 jit_solution(17300765132356033313)
XLA Ops:
  7.2 0.0 reduce-scatter.4.cloned.1.call-start
  7.2 1.2 copy.30
  8.5 1.2 copy.29
  9.7 1.7 copy.32.refs_4_.refs_15_
  11.4 0.6 broadcast_in_dim_tile.3.refs_6_
  12.0 1.1 pad_maximum_fusion.refs_3_.refs_23_
  13.1 0.1 fusion.1
  13.2 1.0 constant_dynamic-slice_fusion.1
  14.2 0.8 copy.31
  15.7 0.8 fusion.refs_8_.refs_11_.refs_3_
  16.5 1.0 constant_dynamic-slice_fusion
  17.5 0.8 pad_maximum_fusion.1.refs_12_
  18.2 33.1 %shard_map.212 = (bf16[1024,512]{1,0:T(8,128)(2,1)}, bf16[2048,1024]{1,0:T(8,128)(2,1)}, bf16[1024,512]{1,0:T(8,128)(2,1)}, bf16[1024,256]{1,0:T(8,128)(2,1)}, b...) custom-call(bf16[1024,2048]{1,0:T(8,128)(2,1)} %refs_4_.3, ...), custom_call_target="tpu_custom_call" | custom-call | flops 4294967296 | bytes 16777216 | tf_op jit(solution)/shard_map/pallas_call | solution.py:217
  51.3 110.2 %shard_map.213 = (bf16[2048,1024]{1,0:T(8,128)(2,1)}, bf16[1408,1024]{1,0:T(8,128)(2,1)}, bf16[1024,1408]{1,0:T(8,128)(2,1)}, bf16[1024,1408]{1,0:T(8,128)(2,1)}...) custom-call(bf16[1024,512]{1,0:T(8,128)(2,1)} %get-tuple-element.53., ...), custom_call_target="tpu_custom_call" | custom-call | flops 44023414784 | bytes 83886080 | tf_op jit(solution)/shard_map/pallas_call | solution.py:447
  161.6 0.0 reduce-scatter.6.cloned.1.call-start
  161.6 87.2 %shard_map.214 = (f32[256,1408]{1,0:T(8,128)}, f32[256,1408]{1,0:T(8,128)}, f32[176,2048]{1,0:T(8,128)}) custom-call(bf16[8,256,1024]{2,1,0:T(8,128)(2,1)} %bitcast.36, bf16[8,256,1024]{2,1,0:T(8,128)(2,1)} %bitcast.37, bf16[8,176,1024]{2,1,0:T(8,128)(2,1)} %bitcast.38, bf16[1024,1408]{1,0:T(8,128)(2,1)} %get-tuple-element.60.refs_3_, ...), custom_call_target="tpu_custom_call" | custom-call | flops 53150220288 | bytes 21233664 | tf_op jit(solution)/shard_map/pallas_call | solution.py:679
  248.9 0.2 reduce-scatter.8.cloned.1.call-start
  249.1 107.8 %shard_map.215 = (f32[256,2048]{1,0:T(8,128)}, f32[8,2,256]{2,1,0:T(2,128)}, f32[64,2048]{1,0:T(8,128)}, bf16[256,2048]{1,0:T(8,128)(2,1)}, bf16[1024,640]{1,0:T(8,128)(2,1)}, /*index=5*/bf16[3,8,256,640]{3,2,1,0:T(8,128)(2,1)}) custom-call(bf16[256,2048]{1,0:T(8,128)(2,1)} %reduce-scatter.4.cloned.1.call-done.refs_0_, ...), custom_call_target="tpu_custom_call" | custom-call | flops 10737418240 | bytes 41943040 | tf_op jit(solution)/shard_map/pallas_call | solution.py:933
  356.9 0.0 reduce-scatter.6.cloned.1.call-done
  357.0 56.2 %shard_map.216 = (f32[256,512]{1,0:T(8,128)}, f32[256,64]{1,0:T(8,128)}, f32[256,64]{1,0:T(8,128)}, f32[64,2048]{1,0:T(8,128)}, f32[2,256]{1,0:T(2,128)}) custom-call(bf16[8,256,1024]{2,1,0:T(8,128)(2,1)} %bitcast.35, bf16[1024,640]{1,0:T(8,128)(2,1)} %get-tuple-element.83.rhs_ref, f32[8,2,256]{2,1,0:T(2,128)} %get-tuple-element.84.gains_ref, ...), custom_call_target="tpu_custom_call" | custom-call | flops 2684354560 | bytes 4194304 | tf_op jit(solution)/shard_map/pallas_call | solution.py:1059
  413.2 1.6 copy.34
  414.8 1.6 copy.35
  416.4 1.3 fusion.2
  417.7 2.4 add_convert_fusion
  420.1 1.3 copy.43
  421.4 0.1 copy-done.7
  421.5 0.8 copy.44
  422.3 0.8 copy.45
  423.1 1.1 copy.46
  424.2 1.1 copy.47
  425.3 0.8 copy-done.2
  426.1 1.1 copy.48
  (21 shorter events, 0.1 us)
Async XLA Ops:
  7.2 241.7 %reduce-scatter.4.cloned.1.call-start = ((), (), s32[]{:S(2)}) async-start(), calls=%async_computation.3 | async-start | bytes 5242880 | tf_op jit(solution)/shard_map/reduce_scatter | solution.py:1173
  161.6 195.3 %reduce-scatter.6.cloned.1.call-start = ((), (), s32[]{:S(2)}) async-start(), calls=%async_computation.4 | async-start | bytes 3276800 | tf_op jit(solution)/shard_map/reduce_scatter | solution.py:1209
  248.9 168.8 %reduce-scatter.8.cloned.1.call-start = ((), (), s32[]{:S(2)}) async-start(), calls=%async_computation.5 | async-start | bytes 1966080 | tf_op jit(solution)/shard_map/reduce_scatter | solution.py:1224
  357.0 60.7 %copy-start = (f32[256,2048]{1,0:T(8,128)S(1)}, f32[256,2048]{1,0:T(8,128)}, u32[]{:S(2)}) copy-start(f32[256,2048]{1,0:T(8,128)} %get-tuple-element.55.refs_1_) | copy-start | bytes 6291460
  357.0 60.7 %copy-start.5 = (bf16[256,1280]{1,0:T(8,128)(2,1)S(1)}, bf16[256,1280]{1,0:T(8,128)(2,1)}, u32[]{:S(2)}) copy-start(bf16[256,1280]{1,0:T(8,128)(2,1)} %reduce-scatter.6.cloned.1.call-done) | copy-start | bytes 1966084
  417.7 2.4 copy-start.1
  420.1 1.4 copy-start.7
  420.1 2.2 copy-start.6
  421.5 1.6 copy-start.4
  422.3 1.9 copy-start.3
  424.2 1.9 copy-start.2
Sparse Core Ops, SparseCore 0:
  161.7 77.4 reduce-scatter.3
  249.0 67.7 reduce-scatter.5
  357.1 56.6 reduce-scatter.7

commit v8 on v7

--- a/solution.py
+++ b/solution.py
@@ -439,7 +439,7 @@
     width, hidden = w_own.shape[0], w_gate.shape[1]
     share = part.shape[1]
     others = groups - 1
-    early = 5 * features // 8
+    early = 11 * features // 16
     any_spec = pl.BlockSpec(memory_space=pl.ANY)
     by_row = lambda columns: pl.BlockSpec((rows, columns), lambda i: (i, 0))
     by_column = lambda height: pl.BlockSpec((height, rows), lambda i: (0, i))
@@ -1023,7 +1023,7 @@
     for step in range(1, groups):
         near_copy(step).start()
         out_copy(step).start()
-    scatter.other_chunks()
+    scatter.own_chunks(others_too=True)
     value = gains_ref[...]
     for step in range(1, groups):
         near_copy(step).wait_recv()
@@ -1031,7 +1031,6 @@
     total[...] = value
     for step in range(1, dp):
         far_copy(step).start()
-    scatter.own_chunks()
     for stage in range(1, dp.bit_length() - 1):
         scatter.later(stage)
     value = total[pack]

time: 442 us -> 443 us (level)
  no operation moved by 1% of the time
where the time goes in v8:
time: 443 us; the launch traced here: 435 us
  Pallas kernels  395 us (89%)
  local copies, waits for them, and re-layouts  19.2 us (4%)
  between operations  14.8 us (3%)
  other arithmetic  5.17 us (1%)
    pallas_call x1, Pallas kernels, feed_forward(): pl.pallas_call(functools.partial(feed_forward_kernel, dp, groups), grid=(...  110 us
    pallas_call x1, Pallas kernels, attention_back(): pl.pallas_call(functools.partial(attention_back_kernel, dp, groups, head_...  108 us
    pallas_call x1, Pallas kernels, product_scatter(): pl.pallas_call(functools.partial(product_scatter_kernel, count, dp), out_...  87.1 us
    pallas_call x1, Pallas kernels, last_sums(): pl.pallas_call(functools.partial(last_sums_kernel, dp, groups), out_shape...  57 us
    pallas_call x1, Pallas kernels, attention(): pl.pallas_call(functools.partial(attention_kernel, groups, head_width), o...  33.1 us
    unnamed x26, local copies, waits for them, and re-layouts  12.7 us
  transfers between devices with their start and end apart: 3, of which 0 were waited for; matrix products, arithmetic and copies ran while one was open for 1% of the time, Pallas kernels for 58%

profile of v8, /device:TPU:8, one launch (start us, length us, event | category | flops | bytes accessed | tf_op | source)
XLA Modules:
  0.0 434.7 jit_solution(10662549295825541109)
XLA Ops:
  7.2 0.0 reduce-scatter.4.cloned.1.call-start
  7.2 1.2 copy.30
  8.5 1.2 copy.29
  9.7 1.7 copy.32.refs_4_.refs_15_
  11.4 0.6 broadcast_in_dim_tile.3.refs_6_
  12.0 1.1 pad_maximum_fusion.refs_3_.refs_23_
  13.1 0.1 fusion.1
  13.2 1.0 constant_dynamic-slice_fusion.1
  14.2 0.8 copy.31
  15.7 0.8 fusion.refs_8_.refs_11_.refs_3_
  16.5 1.0 constant_dynamic-slice_fusion
  17.5 0.8 pad_maximum_fusion.1.refs_12_
  18.2 33.1 %shard_map.212 = (bf16[1024,512]{1,0:T(8,128)(2,1)}, bf16[2048,1024]{1,0:T(8,128)(2,1)}, bf16[1024,512]{1,0:T(8,128)(2,1)}, bf16[1024,256]{1,0:T(8,128)(2,1)}, b...) custom-call(bf16[1024,2048]{1,0:T(8,128)(2,1)} %refs_4_.3, ...), custom_call_target="tpu_custom_call" | custom-call | flops 4294967296 | bytes 16777216 | tf_op jit(solution)/shard_map/pallas_call | solution.py:217
  51.3 110.2 %shard_map.213 = (bf16[2048,1024]{1,0:T(8,128)(2,1)}, bf16[1408,1024]{1,0:T(8,128)(2,1)}, bf16[1024,1408]{1,0:T(8,128)(2,1)}, bf16[1024,1408]{1,0:T(8,128)(2,1)}...) custom-call(bf16[1024,512]{1,0:T(8,128)(2,1)} %get-tuple-element.53., ...), custom_call_target="tpu_custom_call" | custom-call | flops 44023414784 | bytes 83886080 | tf_op jit(solution)/shard_map/pallas_call | solution.py:447
  161.6 0.0 reduce-scatter.6.cloned.1.call-start
  161.6 87.1 %shard_map.214 = (f32[256,1408]{1,0:T(8,128)}, f32[256,1408]{1,0:T(8,128)}, f32[176,2048]{1,0:T(8,128)}) custom-call(bf16[8,256,1024]{2,1,0:T(8,128)(2,1)} %bitcast.36, bf16[8,256,1024]{2,1,0:T(8,128)(2,1)} %bitcast.37, bf16[8,176,1024]{2,1,0:T(8,128)(2,1)} %bitcast.38, bf16[1024,1408]{1,0:T(8,128)(2,1)} %get-tuple-element.60.refs_3_, ...), custom_call_target="tpu_custom_call" | custom-call | flops 53150220288 | bytes 21233664 | tf_op jit(solution)/shard_map/pallas_call | solution.py:679
  248.8 0.2 reduce-scatter.8.cloned.1.call-start
  249.0 107.9 %shard_map.215 = (f32[256,2048]{1,0:T(8,128)}, f32[8,2,256]{2,1,0:T(2,128)}, f32[64,2048]{1,0:T(8,128)}, bf16[256,2048]{1,0:T(8,128)(2,1)}, bf16[1024,640]{1,0:T(8,128)(2,1)}, /*index=5*/bf16[3,8,256,640]{3,2,1,0:T(8,128)(2,1)}) custom-call(bf16[256,2048]{1,0:T(8,128)(2,1)} %reduce-scatter.4.cloned.1.call-done.refs_0_, ...), custom_call_target="tpu_custom_call" | custom-call | flops 10737418240 | bytes 41943040 | tf_op jit(solution)/shard_map/pallas_call | solution.py:933
  356.9 0.0 reduce-scatter.6.cloned.1.call-done
  357.0 57.0 %shard_map.216 = (f32[256,512]{1,0:T(8,128)}, f32[256,64]{1,0:T(8,128)}, f32[256,64]{1,0:T(8,128)}, f32[64,2048]{1,0:T(8,128)}, f32[2,256]{1,0:T(2,128)}) custom-call(bf16[8,256,1024]{2,1,0:T(8,128)(2,1)} %bitcast.35, bf16[1024,640]{1,0:T(8,128)(2,1)} %get-tuple-element.83.rhs_ref, f32[8,2,256]{2,1,0:T(2,128)} %get-tuple-element.84.gains_ref, ...), custom_call_target="tpu_custom_call" | custom-call | flops 2684354560 | bytes 4194304 | tf_op jit(solution)/shard_map/pallas_call | solution.py:1058
  413.9 1.6 copy.34
  415.6 1.6 copy.35
  417.2 1.3 fusion.2
  418.5 2.4 add_convert_fusion
  420.9 1.3 copy.43
  422.2 0.0 copy-done.7
  422.3 0.8 copy.44
  423.1 0.8 copy.45
  423.9 1.1 copy.46
  425.0 1.1 copy.47
  426.1 0.8 copy-done.2
  426.9 1.1 copy.48
  (21 shorter events, 0.1 us)
Async XLA Ops:
  7.2 241.6 %reduce-scatter.4.cloned.1.call-start = ((), (), s32[]{:S(2)}) async-start(), calls=%async_computation.3 | async-start | bytes 5242880 | tf_op jit(solution)/shard_map/reduce_scatter | solution.py:1172
  161.6 195.3 %reduce-scatter.6.cloned.1.call-start = ((), (), s32[]{:S(2)}) async-start(), calls=%async_computation.4 | async-start | bytes 3604480 | tf_op jit(solution)/shard_map/reduce_scatter | solution.py:1208
  248.8 169.7 %reduce-scatter.8.cloned.1.call-start = ((), (), s32[]{:S(2)}) async-start(), calls=%async_computation.5 | async-start | bytes 1638400 | tf_op jit(solution)/shard_map/reduce_scatter | solution.py:1223
  356.9 61.6 %copy-start = (f32[256,2048]{1,0:T(8,128)S(1)}, f32[256,2048]{1,0:T(8,128)}, u32[]{:S(2)}) copy-start(f32[256,2048]{1,0:T(8,128)} %get-tuple-element.55.refs_1_) | copy-start | bytes 6291460
  356.9 61.6 %copy-start.5 = (bf16[256,1408]{1,0:T(8,128)(2,1)S(1)}, bf16[256,1408]{1,0:T(8,128)(2,1)}, u32[]{:S(2)}) copy-start(bf16[256,1408]{1,0:T(8,128)(2,1)} %reduce-scatter.6.cloned.1.call-done) | copy-start | bytes 2162692
  418.5 2.4 copy-start.1
  420.9 1.4 copy-start.7
  420.9 2.2 copy-start.6
  420.9 3.0 copy-start.4
  423.1 1.9 copy-start.3
  425.0 1.9 copy-start.2
Sparse Core Ops, SparseCore 0:
  161.7 77.4 reduce-scatter.3
  248.9 76.4 reduce-scatter.5
  357.1 54.8 reduce-scatter.7
